TPU v7x, 32 devices: a whole 2x2x4 slice. The times are simulated.
32 devices in a mesh: dp: 8 (over z, core), ctx: 4 (over y, x).
Axes of the slice: x: 2, y: 2, z: 4, core: 2. Of those that a mesh axis runs over, the one named last changes fastest.
Arguments:
- queries: bfloat16 [8, 512, 2048], P('dp', 'ctx'), may hold values from -46 to 46
- keys_values: bfloat16 [8, 512, 1024], P('dp', 'ctx'), may hold values from -4 to 4
- grad_out: bfloat16 [8, 512, 4096], P('dp', 'ctx'), may hold values from -6 to 6
- out_proj: bfloat16 [2048, 4096], P('dp'), may hold values from -0.125 to 0.125
- doc_lengths: int32 [8, 16], P('dp'), may hold values from 1 to 64, as said below
- tile_mask: int32 [8, 4, 4], P('dp'), may hold values from 0 to 1, as said below
- unit_dest: int32 [8, 4, 2], P('dp'), may hold values from 0 to 3, as said below
Outputs:
- attn_out: bfloat16 [8, 512, 4096], P('dp', 'ctx')
- q_grad: bfloat16 [8, 512, 2048], P('dp', 'ctx')
- kv_grad: bfloat16 [8, 512, 1024], P('dp', 'ctx')
Inputs may be any that keep to these rules, and one draw needn't show every extreme that they name: `doc_lengths`: each row sums to 512; exactly one entry equals 64. `tile_mask`: entry [b, a, c] is 1 exactly when some token of tile c precedes or equals some token of tile a in the same dialogue of doc_lengths[b]. Tokens j * 64 to (j + 1) * 64 - 1 of shard s become rows j * 64 to (j + 1) * 64 - 1 of shard unit_dest[b, s, j]; unit_dest[b, s, j] = (s + o_j) mod 4 with 2 distinct offsets o_j for each batch row.
All inputs are finite; a program needn't handle non-finite values.
Results may differ from a plain program's by a relative error of at most 0.012.
The roundings to bfloat16 on the way count: a program that leaves them out, or rounds other values in their place, can miss the bound.
Values may be sent and summed in bfloat16 or wider, within the bound.
No kernel may reach another device: no remote copies, remote signals or barrier semaphores. Data moves between devices by JAX's collectives and lax.ppermute only.
A program may use at most 128 MiB of HBM per device.

v0:
```python
import math

import jax
import jax.numpy as jnp
from jax import lax
from jax.sharding import PartitionSpec as P

QUERY_HEADS = 16
KEY_VALUE_HEADS = 4
HEAD_WIDTH = 128
TILE = 128


def unit_sources(routes):
    shard_ids = jnp.arange(routes.shape[0], dtype=jnp.int32)
    matches = (routes[:, None, :] == shard_ids[None, :, None]).astype(jnp.int32)
    return jnp.sum(matches * shard_ids[:, None, None], axis=0)


def place_units(owners, per_shard, unit_rows):
    unit_count = owners.shape[1]
    starts = owners * per_shard + jnp.arange(unit_count, dtype=jnp.int32)[None, :] * unit_rows
    offsets = jnp.arange(unit_rows, dtype=jnp.int32)
    return (starts[:, :, None] + offsets[None, None, :]).reshape(-1)


def dialogue_of(positions, lengths):
    bounds = jnp.cumsum(lengths)[:-1]
    return jnp.sum((positions[:, None] >= bounds[None, :]).astype(jnp.int32), axis=1)


def window_mask(query_pos, key_pos, lengths, tiles):
    query_doc = dialogue_of(query_pos.reshape(-1), lengths).reshape(query_pos.shape)
    key_doc = dialogue_of(key_pos.reshape(-1), lengths).reshape(key_pos.shape)
    tile_ids = jnp.arange(tiles.shape[0], dtype=jnp.int32)
    query_tiles = (query_pos[:, :, None] // TILE == tile_ids[None, None, :]).astype(jnp.float32)
    key_tiles = (key_pos[:, :, None] // TILE == tile_ids[None, None, :]).astype(jnp.float32)
    tile_rows = jnp.einsum("ucn,nm->ucm", query_tiles, tiles.astype(jnp.float32))
    tile_open = jnp.einsum("ucm,uwm->ucw", tile_rows, key_tiles) > 0.5
    same_doc = query_doc[:, :, None] == key_doc[:, None, :]
    causal = key_pos[:, None, :] <= query_pos[:, :, None]
    return tile_open & same_doc & causal


def on_device(queries, keys_values, grad_out, out_proj, doc_lengths, tile_mask, unit_dest):
    groups = lax.axis_size("ctx")
    shard_index = lax.axis_index("ctx")
    per_shard = queries.shape[1]
    unit_count = unit_dest.shape[2]
    unit_rows = per_shard // unit_count
    total_rows = per_shard * groups
    longest = total_rows // 8
    width = longest + unit_rows
    group_ratio = QUERY_HEADS // KEY_VALUE_HEADS
    key_head_width = KEY_VALUE_HEADS * HEAD_WIDTH
    scale = 1.0 / math.sqrt(HEAD_WIDTH)
    lengths = doc_lengths[0]
    tiles = tile_mask[0]
    routes = unit_dest[0]
    positions = place_units(unit_sources(routes), per_shard, unit_rows)
    shard_ids = jnp.arange(groups, dtype=jnp.int32)
    my_routes = lax.dynamic_index_in_dim(routes, shard_index, 0, keepdims=False)
    outgoing = (shard_ids[:, None] == my_routes[None, :]).astype(jnp.bfloat16)
    my_sources = lax.dynamic_index_in_dim(unit_sources(routes), shard_index, 0, keepdims=False)
    incoming = (my_sources[:, None] == shard_ids[None, :]).astype(jnp.bfloat16)

    def spread(block):
        units_view = block.reshape(unit_count, unit_rows, block.shape[1])
        return jnp.einsum(
            "gj,jrw->grw", outgoing, units_view, preferred_element_type=jnp.float32
        ).astype(jnp.bfloat16)

    def collect(arrived):
        placed = jnp.einsum("js,srw->jrw", incoming, arrived, preferred_element_type=jnp.float32)
        return placed.astype(jnp.bfloat16).reshape(per_shard, arrived.shape[2])

    arrived_queries, arrived_keys = (
        lax.all_to_all(spread(queries[0]), "ctx", split_axis=0, concat_axis=0, tiled=True),
        lax.all_to_all(spread(keys_values[0]), "ctx", split_axis=0, concat_axis=0, tiled=True),
    )
    my_queries = collect(arrived_queries)
    balanced_keys = lax.all_gather(collect(arrived_keys), "ctx", axis=0, tiled=True)
    key_rows = balanced_keys[place_units(routes, per_shard, unit_rows)]
    query_pos = lax.dynamic_slice_in_dim(positions, shard_index * per_shard, per_shard).reshape(
        unit_count, unit_rows
    )
    win_start = jnp.clip(query_pos[:, 0] - longest, 0, total_rows - width)
    key_pos = win_start[:, None] + jnp.arange(width, dtype=jnp.int32)[None, :]
    windows = jax.vmap(lambda start: lax.dynamic_slice_in_dim(key_rows, start, width, 0))(win_start)
    allowed = window_mask(query_pos, key_pos, lengths, tiles)
    q_units = my_queries.reshape(unit_count, unit_rows, QUERY_HEADS * HEAD_WIDTH)
    grad_rows = grad_out[0]
    grad_context = jnp.einsum(
        "td,rd->tr",
        grad_rows,
        lax.all_gather(out_proj, "dp", axis=0, tiled=True),
        preferred_element_type=jnp.float32,
    ).astype(jnp.bfloat16)

    def group_probs(query_head_group):
        q_part = q_units[
            :,
            :,
            query_head_group
            * group_ratio
            * HEAD_WIDTH : (query_head_group + 1)
            * group_ratio
            * HEAD_WIDTH,
        ].reshape(unit_count, unit_rows, group_ratio, HEAD_WIDTH)
        keys_part = windows[
            :, :, query_head_group * HEAD_WIDTH : (query_head_group + 1) * HEAD_WIDTH
        ]
        raw = (
            jnp.einsum("uchd,uwd->uhcw", q_part, keys_part, preferred_element_type=jnp.float32)
            * scale
        )
        masked = jnp.where(allowed[:, None], raw, -1e30)
        top = jnp.max(masked, axis=3, keepdims=True)
        expo = jnp.exp(masked - top)
        return (expo / jnp.sum(expo, axis=3, keepdims=True), q_part, keys_part)

    contexts = []
    for query_head_group in range(KEY_VALUE_HEADS):
        probs, q_part, keys_part = group_probs(query_head_group)
        values_part = windows[
            :,
            :,
            key_head_width
            + query_head_group * HEAD_WIDTH : key_head_width
            + (query_head_group + 1) * HEAD_WIDTH,
        ]
        mixed = jnp.einsum(
            "uhcw,uwd->uchd",
            probs.astype(jnp.bfloat16),
            values_part,
            preferred_element_type=jnp.float32,
        )
        contexts.append(mixed.astype(jnp.bfloat16).reshape(per_shard, group_ratio * HEAD_WIDTH))
    context = jnp.concatenate(contexts, axis=1)
    attn_sum = jnp.dot(
        context,
        lax.all_gather(out_proj, "dp", axis=0, tiled=True),
        preferred_element_type=jnp.float32,
    )
    delta = jnp.sum(
        grad_context.astype(jnp.float32).reshape(per_shard, QUERY_HEADS, HEAD_WIDTH)
        * context.astype(jnp.float32).reshape(per_shard, QUERY_HEADS, HEAD_WIDTH),
        axis=2,
    )
    delta_units = delta.reshape(unit_count, unit_rows, QUERY_HEADS)
    q_grads = []
    key_terms = []
    value_terms = []
    for query_head_group in range(KEY_VALUE_HEADS):
        probs, q_part, keys_part = group_probs(query_head_group)
        values_part = windows[
            :,
            :,
            key_head_width
            + query_head_group * HEAD_WIDTH : key_head_width
            + (query_head_group + 1) * HEAD_WIDTH,
        ]
        grad_part = grad_context[
            :,
            query_head_group
            * group_ratio
            * HEAD_WIDTH : (query_head_group + 1)
            * group_ratio
            * HEAD_WIDTH,
        ].reshape(unit_count, unit_rows, group_ratio, HEAD_WIDTH)
        delta_part = jnp.transpose(
            delta_units[
                :, :, query_head_group * group_ratio : (query_head_group + 1) * group_ratio
            ],
            (0, 2, 1),
        )
        grad_probs = jnp.einsum(
            "uchd,uwd->uhcw", grad_part, values_part, preferred_element_type=jnp.float32
        )
        grad_scores = (probs * (grad_probs - delta_part[:, :, :, None]) * scale).astype(
            jnp.bfloat16
        )
        q_grads.append(
            jnp.einsum("uhcw,uwd->uchd", grad_scores, keys_part, preferred_element_type=jnp.float32)
            .astype(jnp.bfloat16)
            .reshape(per_shard, group_ratio * HEAD_WIDTH)
        )
        key_terms.append(
            jnp.einsum("uhcw,uchd->uwd", grad_scores, q_part, preferred_element_type=jnp.float32)
        )
        value_terms.append(
            jnp.einsum(
                "uhcw,uchd->uwd",
                probs.astype(jnp.bfloat16),
                grad_part,
                preferred_element_type=jnp.float32,
            )
        )
    unit_terms = jnp.concatenate(key_terms + value_terms, axis=2)

    def add_unit(index, total):
        start = win_start[index]
        current = lax.dynamic_slice_in_dim(total, start, width, 0)
        return lax.dynamic_update_slice_in_dim(total, current + unit_terms[index], start, 0)

    packed_terms = lax.fori_loop(
        0, unit_count, add_unit, jnp.zeros((total_rows, 2 * key_head_width), jnp.float32)
    )
    grad_terms = packed_terms[positions]
    kv_grad = lax.psum_scatter(
        grad_terms.astype(jnp.bfloat16), "ctx", scatter_dimension=0, tiled=True
    )
    q_grad = jnp.concatenate(q_grads, axis=1)
    return (attn_sum.astype(jnp.bfloat16)[None], q_grad[None], kv_grad[None])


def solution(mesh):
    return jax.shard_map(
        on_device,
        mesh=mesh,
        in_specs=(
            P("dp", "ctx", None),
            P("dp", "ctx", None),
            P("dp", "ctx", None),
            P("dp", None),
            P("dp", None),
            P("dp", None, None),
            P("dp", None, None),
        ),
        out_specs=(P("dp", "ctx", None), P("dp", "ctx", None), P("dp", "ctx", None)),
        check_vma=False,
    )
```

profile of v0, /device:TPU:0, one launch (start us, length us, event | category | flops | bytes accessed | tf_op | source)
XLA Modules:
  0.0 301.0 jit_solution(10137831981564030627)
XLA Ops:
  7.2 0.9 dynamic-slice_reduce_fusion
  8.1 1.5 convolution_convert_fusion.4
  9.7 1.0 copy.117
  10.6 5.2 %all-to-all-start = ((bf16[4,64,1024]{2,1,0:T(8,128)(2,1)}), bf16[4,64,1024]{2,1,0:T(8,128)(2,1)S(1)}, u32[]{:S(2)}, u32[]{:S(2)}) async-start(bf16[4,64,1024]{2,1,0:T(8,128)(2,1)} %copy.117), calls=%async_computation | async-start | bytes 1048576 | tf_op jit(solution)/shard_map/all_to_all | solution.py:79
  16.1 7.7 %all-to-all-done = bf16[4,64,1024]{2,1,0:T(8,128)(2,1)S(1)} async-done(((bf16[4,64,1024]{2,1,0:T(8,128)(2,1)}), bf16[4,64,1024]{2,1,0:T(8,128)(2,1)S(1)}, u32[]{:S(2)}, u32[]{:S(2)}) %all-to-all-start) | async-done | bytes 524320 | tf_op jit(solution)/shard_map/all_to_all | solution.py:79
  23.8 0.5 convolution_convert_fusion.5
  24.4 0.8 copy.119
  25.2 0.7 all-gather.5.cloned.1.call-update
  25.9 1.2 convolution_convert_fusion.1
  27.2 1.5 copy.125
  28.7 3.5 %all-to-all-start.1 = ((bf16[4,64,2048]{2,1,0:T(8,128)(2,1)}), bf16[4,64,2048]{2,1,0:T(8,128)(2,1)S(1)}, u32[]{:S(2)}, u32[]{:S(2)}) async-start(bf16[4,64,2048]{2,1,0:T(8,128)(2,1)} %copy.125), calls=%async_computation.1 | async-start | bytes 2097152 | tf_op jit(solution)/shard_map/all_to_all | solution.py:78
  33.9 0.4 fusion.54
  34.3 13.5 %all-to-all-done.1 = bf16[4,64,2048]{2,1,0:T(8,128)(2,1)S(1)} async-done(((bf16[4,64,2048]{2,1,0:T(8,128)(2,1)}), bf16[4,64,2048]{2,1,0:T(8,128)(2,1)S(1)}, u32[]{:S(2)}, u32[]{:S(2)}) %all-to-all-start.1) | async-done | bytes 1048608 | tf_op jit(solution)/shard_map/all_to_all | solution.py:78
  47.8 1.0 convolution_convert_fusion.3
  48.7 0.4 fusion.257
  49.5 9.5 %all-gather.3.cloned.1.call-done = bf16[512,1024]{1,0:T(8,128)(2,1)} async-done(((bf16[128,1024]{1,0:T(8,128)(2,1)}), bf16[512,1024]{1,0:T(8,128)(2,1)}) %all-gather.3.cloned.1.call-update) | async-done | bytes 1048592 | tf_op jit(solution)/shard_map/all_gather | solution.py:82
  59.0 4.1 %gather_fusion = bf16[512,1024]{1,0:T(8,128)(2,1)S(1)} fusion(bf16[512,1024]{1,0:T(8,128)(2,1)} %all-gather.3.cloned.1.call-done, s32[1024]{0:T(1024)S(1)} %pad_clamp_fusion.1), kind=kCustom, calls=%fused_computation | custom fusion | bytes 2099200 | tf_op jit(solution)/shard_map/gather | solution.py:83
  63.1 0.5 while.15
  63.5 1.0 fusion.258
  64.6 1.0 fusion.40
  65.7 1.0 fusion.263
  66.7 1.0 fusion.39
  67.8 1.0 fusion.268
  68.9 1.0 fusion.38
  70.0 0.7 copy.137
  70.6 1.7 fusion.273
  72.4 1.7 fusion.37
  74.2 0.7 copy.136
  74.9 0.7 copy_bitcast_fusion.6
  75.6 136.1 %all-gather.5.cloned.1.call-done = bf16[2048,4096]{1,0:T(8,128)(2,1)} async-done(((bf16[256,4096]{1,0:T(8,128)(2,1)}), bf16[2048,4096]{1,0:T(8,128)(2,1)}) %all-gather.5.cloned.1.call-update) | async-done | bytes 16777232 | tf_op jit(solution)/shard_map/all_gather | solution.py:142
  211.7 11.4 %convolution_convert_fusion.2 = bf16[128,2048]{1,0:T(8,128)(2,1)S(1)} fusion(bf16[2048,4096]{1,0:T(8,128)(2,1)} %all-gather.5.cloned.1.call-done, bf16[1,128,4096]{2,1,0:T(8,128)(2,1)S(1)} %copy-done), kind=kOutput, calls=%fused_computation.13 | convolution fusion | flops 2147745792 | bytes 18350080 | tf_op jit(solution)/shard_map/td,rd->tr/dot_general | solution.py:93
  223.2 0.3 fusion.57
  223.7 1.2 fusion.36
  224.9 1.0 fusion.44
  226.0 0.8 copy.151
  226.8 1.2 fusion.35
  228.1 0.8 copy.148
  229.0 1.2 fusion.33
  230.2 0.9 fusion.52
  231.1 1.2 fusion.34
  232.3 0.9 fusion.51
  233.2 0.9 fusion.50
  234.0 0.9 fusion.49
  234.9 2.4 fusion.48
  237.3 2.4 fusion.47
  239.8 2.4 fusion.46
  242.2 2.4 fusion.45
  244.9 20.7 %while.14 = (s32[]{:T(128)}, f32[512,1024]{1,0:T(8,128)S(1)}, s32[2]{0:T(128)S(1)}, f32[2,128,1024]{1,2,0:T(8,128)}, s32[]{:T(128)}, /*index=5*/s32[]{:T(128)}, s32[]{:T(128)}) while((s32[]{:T(128)}, f32[512,1024]{1,0:T(8,128)S(1)}, s32[2]{0:T(128)S(1)}, f32[2,128,1024]{1,2,0:T(8,128)}, s32[]{:T(128)}, /*index=5*/s32[]{:T(128)}, ...), condition=%wide.region_14.15_spmd, body=%wide.region_13.14_spmd.sunk | while | flops 131077 | bytes 4718735 | solution.py:206
  244.9 1.9 constant_dynamic-slice_fusion.4
  246.7 2.1 copy.295
  248.8 0.6 dynamic_slice.43
  251.3 1.9 bitcast_add_fusion.2
  253.2 2.0 dynamic_update_slice.8
  255.2 1.9 constant_dynamic-slice_fusion.4
  257.1 2.1 copy.295
  259.1 0.6 dynamic_slice.43
  261.7 1.9 bitcast_add_fusion.2
  263.6 1.9 dynamic_update_slice.8
  265.5 2.7 gather_fusion.1
  268.3 1.2 fusion.42
  269.6 1.1 fusion.41
  270.9 0.8 maximum_bitcast_fusion
  271.7 9.3 %fusion.4 = bf16[1,128,4096]{2,1,0:T(8,128)(2,1)} fusion(bf16[2048,4096]{1,0:T(8,128)(2,1)} %all-gather.5.cloned.1.call-done, bf16[128,512]{1,0:T(8,128)(2,1)S(1)} %get-tuple-element.150, bf16[128,512]{1,0:T(8,128)(2,1)S(1)} %get-tuple-element.151, bf16[128,512]{1,0:T(8,128)(2,1)S(1)} %get-tuple-element.152, bf16[128,512]{1,0:T(8,128)(2,1)S(1)} %copy-done.1), kind=kOutput, calls=%fused_computation.11 | convolution fusion | flops 2150105088 | bytes 18350080 | tf_op jit(solution)/shard_map/dot_general | solution.py:140
  281.0 13.4 %reduce-scatter.2.cloned.1.call-done = bf16[128,1024]{1,0:T(8,128)(2,1)} async-done(((bf16[512,1024]{1,0:T(8,128)(2,1)}), bf16[128,1024]{1,0:T(8,128)(2,1)}) %reduce-scatter.2.cloned.1.call-update) | async-done | bytes 262160 | tf_op jit(solution)/shard_map/reduce_scatter | solution.py:210
  (113 shorter events, 4.1 us)
Async XLA Ops:
  7.2 204.5 %copy-start = (bf16[1,128,4096]{2,1,0:T(8,128)(2,1)S(1)}, bf16[1,128,4096]{2,1,0:T(8,128)(2,1)}, u32[]{:S(2)}) copy-start(bf16[1,128,4096]{2,1,0:T(8,128)(2,1)} %param.11) | copy-start | bytes 3145732
  7.2 8.6 %copy-start.10 = (s32[1,4,2]{1,2,0:T(2,128)S(1)}, s32[1,4,2]{1,2,0:T(2,128)}, u32[]{:S(2)}) copy-start(s32[1,4,2]{1,2,0:T(2,128)} %param.15) | copy-start | bytes 100
  10.6 13.2 %all-to-all-start = ((bf16[4,64,1024]{2,1,0:T(8,128)(2,1)}), bf16[4,64,1024]{2,1,0:T(8,128)(2,1)S(1)}, u32[]{:S(2)}, u32[]{:S(2)}) async-start(bf16[4,64,1024]{2,1,0:T(8,128)(2,1)} %copy.117), calls=%async_computation | async-start | bytes 1048576 | tf_op jit(solution)/shard_map/all_to_all | solution.py:79
  15.8 10.1 %copy-start.14 = (bf16[1,128,2048]{2,1,0:T(8,128)(2,1)S(1)}, bf16[1,128,2048]{2,1,0:T(8,128)(2,1)}, u32[]{:S(2)}) copy-start(bf16[1,128,2048]{2,1,0:T(8,128)(2,1)} %param.9) | copy-start | bytes 1572868
  15.8 43.2 %all-gather.3.cloned.1.call-start = ((), (), s32[]{:S(2)}) async-start(), calls=%async_computation.3 | async-start | bytes 1310720 | tf_op jit(solution)/shard_map/all_gather | solution.py:82
  25.2 186.5 %all-gather.5.cloned.1.call-start = ((), (), s32[]{:S(2)}) async-start(), calls=%async_computation.4 | async-start | bytes 18874368 | tf_op jit(solution)/shard_map/all_gather | solution.py:142
  27.1 6.1 %copy-start.13 = (s32[1,16]{1,0:T(1,128)S(1)}, s32[1,16]{1,0:T(1,128)}, u32[]{:S(2)}) copy-start(s32[1,16]{1,0:T(1,128)} %param.13) | copy-start | bytes 196
  27.1 6.8 %copy-start.15 = (s32[1,4,4]{2,1,0:T(4,128)S(1)}, s32[1,4,4]{2,1,0:T(4,128)}, u32[]{:S(2)}) copy-start(s32[1,4,4]{2,1,0:T(4,128)} %param.14) | copy-start | bytes 196
  28.7 19.1 %all-to-all-start.1 = ((bf16[4,64,2048]{2,1,0:T(8,128)(2,1)}), bf16[4,64,2048]{2,1,0:T(8,128)(2,1)S(1)}, u32[]{:S(2)}, u32[]{:S(2)}) async-start(bf16[4,64,2048]{2,1,0:T(8,128)(2,1)} %copy.125), calls=%async_computation.1 | async-start | bytes 2097152 | tf_op jit(solution)/shard_map/all_to_all | solution.py:78
  32.2 262.2 %reduce-scatter.2.cloned.1.call-start = ((), (), s32[]{:S(2)}) async-start(), calls=%async_computation.5 | async-start | bytes 1310720 | tf_op jit(solution)/shard_map/reduce_scatter | solution.py:210
  33.2 15.9 %copy-start.11 = (s32[2]{0:T(128)}, s32[2]{0:T(128)S(1)}, u32[]{:S(2)}) copy-start(s32[2]{0:T(128)S(1)} %get-tuple-element.225) | copy-start | bytes 28
  34.3 34.6 %copy-start.16 = (pred[2,64,128]{2,1,0:T(8,128)(4,1)}, pred[2,64,128]{2,1,0:T(8,128)(4,1)S(1)}, u32[]{:S(2)}) copy-start(pred[2,64,128]{2,1,0:T(8,128)(4,1)S(1)} %fusion.54) | copy-start | bytes 49156
  63.5 8.8 %copy-start.8 = (bf16[2,128,1024]{2,1,0:T(8,128)(2,1)}, bf16[2,128,1024]{2,1,0:T(8,128)(2,1)S(1)}, u32[]{:S(2)}) copy-start(bf16[2,128,1024]{2,1,0:T(8,128)(2,1)S(1)} %get-tuple-element.90) | copy-start | bytes 1572868
  64.6 159.1 %copy-start.17 = (f32[2,4,64]{2,1,0:T(4,128)}, f32[2,4,64]{2,1,0:T(4,128)S(1)}, u32[]{:S(2)}) copy-start(f32[2,4,64]{2,1,0:T(4,128)S(1)} %get-tuple-element.142) | copy-start | bytes 6148
  66.7 3.9 %copy-start.19 = (f32[2,4,64]{2,1,0:T(4,128)}, f32[2,4,64]{2,1,0:T(4,128)S(1)}, u32[]{:S(2)}) copy-start(f32[2,4,64]{2,1,0:T(4,128)S(1)} %get-tuple-element.144) | copy-start | bytes 6148
  68.9 6.0 %copy-start.21 = (f32[2,4,64]{2,1,0:T(4,128)}, f32[2,4,64]{2,1,0:T(4,128)S(1)}, u32[]{:S(2)}) copy-start(f32[2,4,64]{2,1,0:T(4,128)S(1)} %get-tuple-element.146) | copy-start | bytes 6148
  72.4 139.3 %copy-start.23 = (f32[2,4,64]{2,1,0:T(4,128)}, f32[2,4,64]{2,1,0:T(4,128)S(1)}, u32[]{:S(2)}) copy-start(f32[2,4,64]{2,1,0:T(4,128)S(1)} %get-tuple-element.148) | copy-start | bytes 6148
  75.6 147.6 %copy-start.6 = (bf16[2,64,4,128]{3,1,0,2:T(8,128)(2,1)S(1)}, bf16[2,64,4,128]{3,1,0,2:T(8,128)(2,1)}, u32[]{:S(2)}) copy-start(bf16[2,64,4,128]{3,1,0,2:T(8,128)(2,1)} %copy.137) | copy-start | bytes 393220
  75.6 147.6 %copy-start.7 = (bf16[2,64,4,128]{3,1,0,2:T(8,128)(2,1)S(1)}, bf16[2,64,4,128]{3,1,0,2:T(8,128)(2,1)}, u32[]{:S(2)}) copy-start(bf16[2,64,4,128]{3,1,0,2:T(8,128)(2,1)} %copy.136) | copy-start | bytes 393220
  223.5 4.4 %copy-start.9 = (bf16[2,128,1024]{2,1,0:T(8,128)(2,1)S(1)}, bf16[2,128,1024]{2,1,0:T(8,128)(2,1)}, u32[]{:S(2)}) copy-start(bf16[2,128,1024]{2,1,0:T(8,128)(2,1)} %copy-done.8) | copy-start | bytes 1572868
  230.2 7.2 %copy-start.2 = (bf16[2,4,64,128]{3,2,1,0:T(8,128)(2,1)}, bf16[2,4,64,128]{3,2,1,0:T(8,128)(2,1)S(1)}, u32[]{:S(2)}) copy-start(bf16[2,4,64,128]{3,2,1,0:T(8,128)(2,1)S(1)} %fusion.33) | copy-start | bytes 393220
  230.2 7.2 %copy-start.22 = (f32[2,4,64]{2,1,0:T(4,128)S(1)}, f32[2,4,64]{2,1,0:T(4,128)}, u32[]{:S(2)}) copy-start(f32[2,4,64]{2,1,0:T(4,128)} %copy-done.21) | copy-start | bytes 6148
  232.2 9.9 %copy-start.3 = (bf16[2,4,64,128]{3,2,1,0:T(8,128)(2,1)}, bf16[2,4,64,128]{3,2,1,0:T(8,128)(2,1)S(1)}, u32[]{:S(2)}) copy-start(bf16[2,4,64,128]{3,2,1,0:T(8,128)(2,1)S(1)} %fusion.34) | copy-start | bytes 393220
  232.3 7.5 %copy-start.20 = (f32[2,4,64]{2,1,0:T(4,128)S(1)}, f32[2,4,64]{2,1,0:T(4,128)}, u32[]{:S(2)}) copy-start(f32[2,4,64]{2,1,0:T(4,128)} %copy-done.19) | copy-start | bytes 6148
  234.9 7.3 %copy-start.18 = (f32[2,4,64]{2,1,0:T(4,128)S(1)}, f32[2,4,64]{2,1,0:T(4,128)}, u32[]{:S(2)}) copy-start(f32[2,4,64]{2,1,0:T(4,128)} %copy-done.17) | copy-start | bytes 6148
  239.8 5.1 %copy-start.12 = (s32[2]{0:T(128)S(1)}, s32[2]{0:T(128)}, u32[]{:S(2)}) copy-start(s32[2]{0:T(128)} %copy-done.11) | copy-start | bytes 28
  268.2 2.6 copy-start.4
  268.2 2.6 copy-start.5
  268.2 3.5 %copy-start.1 = (bf16[128,512]{1,0:T(8,128)(2,1)S(1)}, bf16[128,512]{1,0:T(8,128)(2,1)}, u32[]{:S(2)}) copy-start(bf16[128,512]{1,0:T(8,128)(2,1)} %get-tuple-element.153) | copy-start | bytes 393220
Sparse Core Ops, SparseCore 0:
  25.3 33.6 all-gather.2
  60.6 151.0 all-gather.4
  268.4 26.0 reduce-scatter.1
where the time goes:
time: 302 us; the launch traced here: 301 us
  waiting for transfers between devices  181 us (60%)
  matrix products  56.2 us (19%)
  local copies, waits for them, and re-layouts  30.8 us (10%)
  between operations  14.3 us (5%)
  starting transfers between devices  8.77 us (3%)
  other arithmetic  5.79 us (2%)
  loops' own time  4.18 us (1%)
    all_gather x1, waiting for transfers between devices, on_device(): lax.all_gather(out_proj, 'dp', axis=0, tiled=True)  136 us
    all_to_all x1, waiting for transfers between devices, on_device(): lax.all_to_all(spread(queries[0]), 'ctx', split_axis=0, concat_axis=0, ti...  13.5 us
    reduce_scatter x1, waiting for transfers between devices, on_device(): lax.psum_scatter(grad_terms.astype(jnp.bfloat16), 'ctx', scatter_dimensio...  13.4 us
    dot_general x1, matrix products, on_device(): jnp.einsum('td,rd->tr', grad_rows, lax.all_gather(out_proj, 'dp', axis=0,...  11.4 us
    dot_general x4, matrix products, on_device(): jnp.einsum('uhcw,uchd->uwd', probs.astype(jnp.bfloat16), grad_part, prefe...  9.66 us
    all_gather x1, waiting for transfers between devices, on_device(): lax.all_gather(collect(arrived_keys), 'ctx', axis=0, tiled=True)  9.46 us
    dot_general x1, matrix products, on_device(): jnp.dot(context, lax.all_gather(out_proj, 'dp', axis=0, tiled=True), pref...  9.28 us
    dynamic_slice x4, local copies, waits for them, and re-layouts, add_unit(): unit_terms[index]  7.84 us
  transfers between devices with their start and end apart: 5, of which 5 were waited for; matrix products, arithmetic and copies ran while one was open for 12% of the time, Pallas kernels for 0%

commit v1 on v0

v1 whole, which is shorter than its diff:
```python
import functools
import math

import jax
import jax.numpy as jnp
from jax import lax
from jax.experimental import pallas as pl
from jax.experimental.pallas import tpu as pltpu
from jax.sharding import PartitionSpec as P

QUERY_HEADS = 16
KEY_VALUE_HEADS = 4
HEAD_WIDTH = 128
TILE = 128
RATIO = QUERY_HEADS // KEY_VALUE_HEADS
GROUP_WIDTH = RATIO * HEAD_WIDTH
KEY_WIDTH = KEY_VALUE_HEADS * HEAD_WIDTH
SCALE = 1.0 / math.sqrt(HEAD_WIDTH)
F32 = jnp.float32
BF16 = jnp.bfloat16
NT_DIMS = (((1,), (1,)), ((), ()))
TN_DIMS = (((0,), (0,)), ((), ()))
VMEM_BYTES = 40 * 1024 * 1024


def whole():
    return pl.BlockSpec(memory_space=pltpu.VMEM)


def in_smem():
    return pl.BlockSpec(memory_space=pltpu.SMEM)


def anywhere():
    return pl.BlockSpec(memory_space=pl.ANY)


def dialogue_of(positions, lengths):
    bounds = jnp.cumsum(lengths)[:-1]
    return jnp.sum((positions[:, None] >= bounds[None, :]).astype(jnp.int32), axis=1)


def window_mask(query_pos, key_pos, lengths, tiles):
    query_doc = dialogue_of(query_pos.reshape(-1), lengths).reshape(query_pos.shape)
    key_doc = dialogue_of(key_pos.reshape(-1), lengths).reshape(key_pos.shape)
    tile_ids = jnp.arange(tiles.shape[0], dtype=jnp.int32)
    query_tiles = (query_pos[:, :, None] // TILE == tile_ids[None, None, :]).astype(F32)
    key_tiles = (key_pos[:, :, None] // TILE == tile_ids[None, None, :]).astype(F32)
    tile_rows = jnp.einsum("ucn,nm->ucm", query_tiles, tiles.astype(F32))
    tile_open = jnp.einsum("ucm,uwm->ucw", tile_rows, key_tiles) > 0.5
    same_doc = query_doc[:, :, None] == key_doc[:, None, :]
    causal = key_pos[:, None, :] <= query_pos[:, :, None]
    return tile_open & same_doc & causal


def stack_heads(block):
    return jnp.concatenate(
        [block[:, h * HEAD_WIDTH : (h + 1) * HEAD_WIDTH] for h in range(RATIO)], axis=0
    )


def forward_kernel(groups, units, rows, width, per_shard, *refs):
    meta, q_ref, allowed_ref = refs[:3]
    kv_parts = refs[3 : 3 + groups]
    context_ref, probs_ref, windows_ref = refs[3 + groups : 6 + groups]
    kv_ref, sems = refs[6 + groups :]
    me = meta[0]
    copies = []
    for t in range(groups):
        start = pl.multiple_of(jnp.bitwise_xor(me, t) * per_shard, per_shard)
        copies.append(
            pltpu.make_async_copy(kv_parts[t], kv_ref.at[pl.ds(start, per_shard)], sems.at[t])
        )
    for copy in copies:
        copy.start()
    for copy in copies:
        copy.wait()
    for u in range(units):
        start = pl.multiple_of(meta[3 + units + u], rows)
        window = kv_ref[pl.ds(start, width), :]
        windows_ref[u] = window
        mask = jnp.concatenate([allowed_ref[u]] * RATIO, axis=0) > 0.5
        for g in range(KEY_VALUE_HEADS):
            q_part = stack_heads(
                q_ref[u * rows : (u + 1) * rows, g * GROUP_WIDTH : (g + 1) * GROUP_WIDTH]
            )
            keys = window[:, g * HEAD_WIDTH : (g + 1) * HEAD_WIDTH]
            values = window[:, KEY_WIDTH + g * HEAD_WIDTH : KEY_WIDTH + (g + 1) * HEAD_WIDTH]
            raw = lax.dot_general(q_part, keys, NT_DIMS, preferred_element_type=F32) * SCALE
            masked = jnp.where(mask, raw, -1e30)
            top = jnp.max(masked, axis=1, keepdims=True)
            expo = jnp.exp(masked - top)
            probs = expo / jnp.sum(expo, axis=1, keepdims=True)
            probs_ref[g, u] = probs
            mixed = jnp.dot(probs.astype(BF16), values, preferred_element_type=F32).astype(BF16)
            for h in range(RATIO):
                col = (g * RATIO + h) * HEAD_WIDTH
                context_ref[u * rows : (u + 1) * rows, col : col + HEAD_WIDTH] = mixed[
                    h * rows : (h + 1) * rows
                ]


def group_of(meta, slot, swapped):
    return jnp.bitwise_xor(meta[1], slot) if swapped else slot


def grad_kernel(groups, units, rows, width, per_shard, slot, swapped, plan, with_q, *refs):
    meta, grad_ref, q_ref, context_ref, probs_ref, windows_ref = refs[:6]
    parts = refs[6 : 6 + len(plan)]
    rest = refs[6 + len(plan) :]
    if with_q:
        rest = rest[1:]
    q_grad_ref = rest[0]
    outs = rest[1 : 1 + groups]
    grad_context_ref, q_block, terms, sem = rest[1 + groups :]
    g = group_of(meta, slot, swapped)
    depth = parts[0].shape[0]
    sums = {}
    for part, (row_key, row_fn, col_fn) in zip(parts, plan):
        wide = part.shape[1]
        start = pl.multiple_of(col_fn(meta) * wide, wide)
        term = lax.dot_general(
            grad_ref[:, pl.ds(start, wide)], part[...], NT_DIMS, preferred_element_type=F32
        )
        sums[row_key] = (sums[row_key][0] + term if row_key in sums else term, row_fn)
    for total, row_fn in sums.values():
        grad_context_ref[row_fn(meta)] = total.astype(BF16)
    blocks = GROUP_WIDTH // depth
    grad_context = jnp.concatenate([grad_context_ref[b] for b in range(blocks)], axis=1)
    wide_start = pl.multiple_of(g * GROUP_WIDTH, GROUP_WIDTH)
    q_all = q_ref[:, pl.ds(wide_start, GROUP_WIDTH)]
    context_all = context_ref[:, pl.ds(wide_start, GROUP_WIDTH)]
    key_start = pl.multiple_of(g * HEAD_WIDTH, HEAD_WIDTH)
    value_start = pl.multiple_of(KEY_WIDTH + g * HEAD_WIDTH, HEAD_WIDTH)
    terms[...] = jnp.zeros_like(terms)
    for u in range(units):
        span = slice(u * rows, (u + 1) * rows)
        q_part = stack_heads(q_all[span])
        grad_part = stack_heads(grad_context[span])
        context_part = stack_heads(context_all[span])
        keys = windows_ref[u, :, pl.ds(key_start, HEAD_WIDTH)]
        values = windows_ref[u, :, pl.ds(value_start, HEAD_WIDTH)]
        probs = probs_ref[g, u]
        delta = jnp.sum(
            grad_part.astype(F32) * context_part.astype(F32), axis=1, keepdims=True
        )
        grad_probs = lax.dot_general(grad_part, values, NT_DIMS, preferred_element_type=F32)
        grad_scores = (probs * (grad_probs - delta) * SCALE).astype(BF16)
        q_part_grad = jnp.dot(grad_scores, keys, preferred_element_type=F32).astype(BF16)
        for h in range(RATIO):
            q_block[span, h * HEAD_WIDTH : (h + 1) * HEAD_WIDTH] = q_part_grad[
                h * rows : (h + 1) * rows
            ]
        key_term = lax.dot_general(grad_scores, q_part, TN_DIMS, preferred_element_type=F32)
        value_term = lax.dot_general(
            probs.astype(BF16), grad_part, TN_DIMS, preferred_element_type=F32
        )
        place = pl.ds(pl.multiple_of(meta[3 + units + u], rows), width)
        terms[place, :] += jnp.concatenate([key_term, value_term], axis=1)
    copy = pltpu.make_async_copy(q_block, q_grad_ref.at[:, pl.ds(wide_start, GROUP_WIDTH)], sem)
    copy.start()
    for t in range(groups):
        owner = jnp.bitwise_xor(meta[0], t)
        for u in range(units):
            shard = lax.rem(owner - meta[3 + u] + groups, groups)
            start = pl.multiple_of(shard * per_shard + u * rows, rows)
            outs[t][u * rows : (u + 1) * rows, :] = terms[pl.ds(start, rows), :].astype(BF16)
    copy.wait()


def project_kernel(slot, swapped, plan, first, meta, context_ref, *refs):
    parts = refs[: len(plan)]
    out_ref = refs[-1]
    total_ref = None if first else refs[len(plan)]
    g = group_of(meta, slot, swapped)
    by_columns = {}
    for part, (row_key, row_fn, col_fn) in zip(parts, plan):
        depth, wide = part.shape
        start = pl.multiple_of(g * GROUP_WIDTH + row_fn(meta) * depth, depth)
        term = jnp.dot(context_ref[:, pl.ds(start, depth)], part[...], preferred_element_type=F32)
        key = (id(col_fn), wide)
        if key in by_columns:
            by_columns[key] = (by_columns[key][0] + term, col_fn, wide)
        else:
            by_columns[key] = (term, col_fn, wide)
    for term, col_fn, wide in by_columns.values():
        span = pl.ds(pl.multiple_of(col_fn(meta) * wide, wide), wide)
        if not first:
            term = term + total_ref[:, span]
        out_ref[:, span] = term.astype(out_ref.dtype)


def combine_kernel(groups, order, swapped, meta, *refs):
    out_ref = refs[-1]
    for index, slot in enumerate(order):
        g = group_of(meta, slot, swapped)
        parts = refs[index * groups : (index + 1) * groups]
        total = parts[0][...].astype(F32)
        for part in parts[1:]:
            total = total + part[...].astype(F32)
        total = total.astype(BF16)
        out_ref[:, pl.ds(pl.multiple_of(g * HEAD_WIDTH, HEAD_WIDTH), HEAD_WIDTH)] = total[
            :, :HEAD_WIDTH
        ]
        out_ref[
            :, pl.ds(pl.multiple_of(KEY_WIDTH + g * HEAD_WIDTH, HEAD_WIDTH), HEAD_WIDTH)
        ] = total[:, HEAD_WIDTH:]


def zero_of(meta):
    return 0


def same_core(meta):
    return meta[2]


def other_core(meta):
    return 1 - meta[2]


def on_device(queries, keys_values, grad_out, out_proj, doc_lengths, tile_mask, unit_dest):
    groups = lax.axis_size("ctx")
    batches = lax.axis_size("dp")
    me = lax.axis_index("ctx").astype(jnp.int32)
    row = lax.axis_index("dp").astype(jnp.int32)
    per_shard = queries.shape[1]
    model = grad_out.shape[2]
    unit_count = unit_dest.shape[2]
    rows = per_shard // unit_count
    total_rows = per_shard * groups
    longest = total_rows // 8
    width = longest + rows
    lengths, tiles, routes = doc_lengths[0], tile_mask[0], unit_dest[0]
    offsets = routes[0]

    def move(block, fn):
        pairs = []
        for d in range(batches):
            for c in range(groups):
                d2, c2 = fn(d, c)
                pairs.append((d * groups + c, d2 * groups + c2))
        return lax.ppermute(block, ("dp", "ctx"), pairs)

    def to_ctx(block, t):
        return move(block, lambda d, c: (d, c ^ t))

    def to_core(block):
        return move(block, lambda d, c: (d ^ 1, c))

    def to_chip(block, j):
        return move(block, lambda d, c: (d ^ (2 * j), c))

    swapped = (batches // 2) * GROUP_WIDTH == QUERY_HEADS * HEAD_WIDTH and groups == 4
    slots = []
    if swapped:
        quarter = model // groups
        column_fns = [functools.partial(lambda t, meta: jnp.bitwise_xor(meta[0], t), t) for t in range(groups)]
        far = lax.dynamic_slice_in_dim(out_proj, me * quarter, quarter, 1)
        two = to_chip(far, 2)
        three = to_chip(two, 1)
        one = to_chip(out_proj, 1)
        for block in (out_proj, one):
            slots.append(
                [
                    (block, ("own", same_core, zero_of)),
                    (to_core(block), ("other", other_core, zero_of)),
                ]
            )
        for piece in (two, three):
            parts = []
            for t in range(groups):
                got = piece if t == 0 else to_ctx(piece, t)
                parts.append((got, ("own", same_core, column_fns[t])))
                parts.append((to_core(got), ("other", other_core, column_fns[t])))
            slots.append(parts)
    else:
        full = lax.all_gather(out_proj, "dp", axis=0, tiled=True)
        for g in range(KEY_VALUE_HEADS):
            part = full[g * GROUP_WIDTH : (g + 1) * GROUP_WIDTH]
            slots.append([(part, ("own", zero_of, zero_of))])

    q_units = queries[0].reshape(unit_count, rows, QUERY_HEADS * HEAD_WIDTH)
    dests = lax.rem(me + offsets, groups)
    sources = lax.rem(me - offsets + groups, groups)
    my_units = [q_units[j] for j in range(unit_count)]
    for t in range(1, groups):
        chosen = q_units[0]
        for j in range(1, unit_count):
            chosen = jnp.where(dests[j] == (me ^ t), q_units[j], chosen)
        got = to_ctx(chosen, t)
        my_units = [
            jnp.where(sources[j] == (me ^ t), got, my_units[j]) for j in range(unit_count)
        ]
    my_queries = jnp.concatenate(my_units, axis=0)
    kv_parts = [keys_values[0]] + [to_ctx(keys_values[0], t) for t in range(1, groups)]

    unit_ids = jnp.arange(unit_count, dtype=jnp.int32)
    first_pos = sources * per_shard + unit_ids * rows
    query_pos = first_pos[:, None] + jnp.arange(rows, dtype=jnp.int32)[None, :]
    win_start = jnp.clip(first_pos - longest, 0, total_rows - width)
    key_pos = win_start[:, None] + jnp.arange(width, dtype=jnp.int32)[None, :]
    allowed = window_mask(query_pos, key_pos, lengths, tiles).astype(F32)
    meta = jnp.concatenate(
        [jnp.stack([me, row // 2, lax.rem(row, 2)]), offsets, win_start]
    ).astype(jnp.int32)

    params = pltpu.CompilerParams(vmem_limit_bytes=VMEM_BYTES)
    sizes = (groups, unit_count, rows, width, per_shard)
    stacked = RATIO * rows
    context, probs, windows = pl.pallas_call(
        functools.partial(forward_kernel, *sizes),
        out_shape=(
            jax.ShapeDtypeStruct((per_shard, QUERY_HEADS * HEAD_WIDTH), BF16),
            jax.ShapeDtypeStruct((KEY_VALUE_HEADS, unit_count, stacked, width), F32),
            jax.ShapeDtypeStruct((unit_count, width, 2 * KEY_WIDTH), BF16),
        ),
        in_specs=[in_smem(), whole(), whole()] + [anywhere()] * groups,
        out_specs=(whole(), whole(), whole()),
        scratch_shapes=[
            pltpu.VMEM((total_rows, 2 * KEY_WIDTH), BF16),
            pltpu.SemaphoreType.DMA((groups,)),
        ],
        compiler_params=params,
        cost_estimate=pl.CostEstimate(
            flops=4 * unit_count * QUERY_HEADS * rows * width * HEAD_WIDTH * 8,
            bytes_accessed=8 * 1024 * 1024,
            transcendentals=unit_count * QUERY_HEADS * rows * width,
        ),
        name="forward",
    )(meta, my_queries, allowed, *kv_parts)

    q_grad = None
    total = None
    shares = []
    count = len(slots)
    for slot, parts in enumerate(slots):
        arrays = [part for part, _ in parts]
        plan = [entry for _, entry in parts]
        depth = arrays[0].shape[0]
        weight_bytes = GROUP_WIDTH * model * 2
        with_q = q_grad is not None
        results = pl.pallas_call(
            functools.partial(grad_kernel, *sizes, slot, swapped, plan, with_q),
            out_shape=(jax.ShapeDtypeStruct((per_shard, QUERY_HEADS * HEAD_WIDTH), BF16),)
            + tuple(
                jax.ShapeDtypeStruct((per_shard, 2 * HEAD_WIDTH), BF16) for _ in range(groups)
            ),
            in_specs=[in_smem()]
            + [whole()] * (5 + len(arrays))
            + ([anywhere()] if with_q else []),
            out_specs=(anywhere(),) + (whole(),) * groups,
            scratch_shapes=[
                pltpu.VMEM((GROUP_WIDTH // depth, per_shard, depth), BF16),
                pltpu.VMEM((per_shard, GROUP_WIDTH), BF16),
                pltpu.VMEM((total_rows, 2 * HEAD_WIDTH), F32),
                pltpu.SemaphoreType.DMA,
            ],
            input_output_aliases={6 + len(arrays): 0} if with_q else {},
            compiler_params=params,
            cost_estimate=pl.CostEstimate(
                flops=2 * per_shard * GROUP_WIDTH * model * 2,
                bytes_accessed=3 * weight_bytes,
                transcendentals=0,
            ),
            name=f"grad_{slot}",
        )(
            meta, grad_out[0], my_queries, context, probs, windows, *arrays,
            *([q_grad] if with_q else []),
        )
        q_grad = results[0]
        shares.append(
            [results[1]] + [to_ctx(results[1 + t], t) for t in range(1, groups)]
        )
        first = total is None
        last = slot == count - 1
        total = pl.pallas_call(
            functools.partial(project_kernel, slot, swapped, plan, first),
            out_shape=jax.ShapeDtypeStruct((per_shard, model), BF16 if last else F32),
            in_specs=[in_smem()] + [whole()] * (1 + len(arrays) + (0 if first else 1)),
            out_specs=whole(),
            compiler_params=params,
            cost_estimate=pl.CostEstimate(
                flops=2 * per_shard * GROUP_WIDTH * model,
                bytes_accessed=2 * weight_bytes,
                transcendentals=0,
            ),
            name=f"project_{slot}",
        )(meta, context, *arrays, *([] if first else [total]))

    kv_grad = pl.pallas_call(
        functools.partial(combine_kernel, groups, list(range(count)), swapped),
        out_shape=jax.ShapeDtypeStruct((per_shard, 2 * KEY_WIDTH), BF16),
        in_specs=[in_smem()] + [whole()] * (groups * count),
        out_specs=whole(),
        compiler_params=params,
        name="combine",
    )(meta, *[part for share in shares for part in share])
    return (total[None], q_grad[None], kv_grad[None])


def solution(mesh):
    return jax.shard_map(
        on_device,
        mesh=mesh,
        in_specs=(
            P("dp", "ctx", None),
            P("dp", "ctx", None),
            P("dp", "ctx", None),
            P("dp", None),
            P("dp", None),
            P("dp", None, None),
            P("dp", None, None),
        ),
        out_specs=(P("dp", "ctx", None), P("dp", "ctx", None), P("dp", "ctx", None)),
        check_vma=False,
    )
```

time: 302 us -> 196 us (0.65)
  waiting for transfers between devices: 181 us -> 107 us
  matrix products: 56.2 us -> 0.38 us
  Pallas kernels: 0 us -> 32.2 us
  starting transfers between devices: 8.77 us -> 40.6 us
  local copies, waits for them, and re-layouts: 30.8 us -> 5.82 us
  between operations: 14.3 us -> 6.77 us
  loops' own time: 4.18 us -> 0 us
    all_gather x2 -> x0, waiting for transfers between devices: 146 us -> none  [the longest x1 136 us: on_device(): lax.all_gather(out_proj, 'dp', axis=0, tiled=True)]
    ppermute x0 -> x37, waiting for transfers between devices: none -> 107 us  [move(): return lax.ppermute(block, ('dp', 'ctx'), pairs)]
    dot_general x26 -> x0, matrix products: 51.1 us -> none  [the longest x1 11.4 us: on_device(): jnp.einsum('td,rd->tr', grad_rows, lax.all_gather(out_proj, 'dp', axis=0,...]
    ppermute x0 -> x37, starting transfers between devices: none -> 40.6 us  [move(): return lax.ppermute(block, ('dp', 'ctx'), pairs)]
    pallas_call x0 -> x10, Pallas kernels: none -> 32.2 us  [the longest x4 17.9 us: on_device(): pl.pallas_call(functools.partial(grad_kernel, *sizes, slot, swapped, plan...]
    all_to_all x2 -> x0, waiting for transfers between devices: 21.2 us -> none  [the longest x1 13.5 us: on_device(): lax.all_to_all(spread(queries[0]), 'ctx', split_axis=0, concat_axis=0, ti...]
    reduce_scatter x1 -> x0, waiting for transfers between devices: 13.4 us -> none  [on_device(): lax.psum_scatter(grad_terms.astype(jnp.bfloat16), 'ctx', scatter_dimensio...]
    dynamic_slice x9 -> x1, local copies, waits for them, and re-layouts: 10.2 us -> 1.11 us  [on_device(): far = lax.dynamic_slice_in_dim(out_proj, me * quarter, quarter, 1)]
  transfers between devices with their start and end apart: 5 -> 37, of which waited for: 5 -> 7; matrix products, arithmetic and copies ran while one was open for 12% -> 4% of each run, Pallas kernels for 0% -> 16%
where the time goes in v1:
time: 196 us
  waiting for transfers between devices  107 us (55%)
  starting transfers between devices  40.6 us (21%)
  Pallas kernels  32.2 us (16%)
  between operations  6.77 us (3%)
  local copies, waits for them, and re-layouts  5.82 us (3%)
  other arithmetic  2.93 us (1%)
    ppermute x37, waiting for transfers between devices, move(): return lax.ppermute(block, ('dp', 'ctx'), pairs)  107 us
    ppermute x37, starting transfers between devices, move(): return lax.ppermute(block, ('dp', 'ctx'), pairs)  40.6 us
    pallas_call x4, Pallas kernels, on_device(): pl.pallas_call(functools.partial(grad_kernel, *sizes, slot, swapped, plan...  17.9 us
    pallas_call x4, Pallas kernels, on_device(): pl.pallas_call(functools.partial(project_kernel, slot, swapped, plan, fir...  10.9 us
  transfers between devices with their start and end apart: 37, of which 7 were waited for; matrix products, arithmetic and copies ran while one was open for 4% of the time, Pallas kernels for 16%

profile of v1, /device:TPU:0, one launch (start us, length us, event | category | flops | bytes accessed | tf_op | source)
XLA Modules:
  0.0 195.5 jit_solution(10472121838390238646)
XLA Ops:
  0.7 3.1 %collective-permute-start.22 = (bf16[256,4096]{1,0:T(8,128)(2,1)}, bf16[256,4096]{1,0:T(8,128)(2,1)}, u32[]{:S(2)}, u32[]{:S(2)}) collective-permute-start(bf16[256,4096]{1,0:T(8,128)(2,1)} %refs_6_.1), channel_id=1, source_target_pairs={{0,8},{1,9},{2,10},{3,11},{4,12},{5,13},{6,14},{7,15},{8,0},{9,1},... | collective-permute-start | bytes 6291464 | tf_op jit(solution)/shard_map/ppermute | solution.py:243
  3.8 1.1 constant_dynamic-slice_fusion
  4.9 2.7 %collective-permute-start.6 = (bf16[256,1024]{1,0:T(8,128)(2,1)S(1)}, bf16[256,1024]{1,0:T(8,128)(2,1)S(1)}, u32[]{:S(2)}, u32[]{:S(2)}) collective-permute-start(bf16[256,1024]{1,0:T(8,128)(2,1)S(1)} %constant_dynamic-slice_fusion), channel_id=1, source_target_pairs={{0,16},{1,17},{2,18},{3,19},{4,20},{5,21},{6,22},{7,23},{8,24},{9,... | collective-permute-start | bytes 1572872 | tf_op jit(solution)/shard_map/ppermute | solution.py:243
  7.5 0.8 slice_reduce_fusion.1
  8.3 0.6 slice.40
  10.9 1.1 bitcast_select_fusion.1
  12.0 2.5 %collective-permute-start = (bf16[64,2048]{1,0:T(8,128)(2,1)S(1)}, bf16[64,2048]{1,0:T(8,128)(2,1)S(1)}, u32[]{:S(2)}, u32[]{:S(2)}) collective-permute-start(bf16[64,2048]{1,0:T(8,128)(2,1)S(1)} %get-tuple-element.55), channel_id=1, source_target_pairs={{0,3},{1,2},{2,1},{3,0},{4,7},{5,6},{6,5},{7,4},{8,11},{9,10},{10,... | collective-permute-start | bytes 786440 | tf_op jit(solution)/shard_map/ppermute | solution.py:243
  14.5 0.5 collective-permute-start.1
  15.0 0.5 collective-permute-start.2
  15.5 44.6 %collective-permute-done.6.refs_0_.refs_6_ = bf16[256,1024]{1,0:T(8,128)(2,1)S(1)} collective-permute-done((bf16[256,1024]{1,0:T(8,128)(2,1)S(1)}, bf16[256,1024]{1,0:T(8,128)(2,1)S(1)}, u32[]{:S(2)}, u32[]{:S(2)}) %collective-permute-start.6) | collective-permute-done | bytes 524320 | tf_op jit(solution)/shard_map/ppermute | solution.py:243
  60.1 1.5 collective-permute-start.16
  61.6 0.6 collective-permute-start.3
  62.2 0.1 copy-done.9
  62.3 1.5 collective-permute-start.4
  63.8 1.5 collective-permute-start.5
  65.4 15.2 %collective-permute-done.3.refs_4_ = bf16[128,1024]{1,0:T(8,128)(2,1)S(1)} collective-permute-done((bf16[128,1024]{1,0:T(8,128)(2,1)S(1)}, bf16[128,1024]{1,0:T(8,128)(2,1)S(1)}, u32[]{:S(2)}, u32[]{:S(2)}) %collective-permute-start.3) | collective-permute-done | bytes 262176 | tf_op jit(solution)/shard_map/ppermute | solution.py:243
  80.6 0.7 copy-done.3
  81.3 0.5 collective-permute-start.23
  81.8 0.7 copy-done.5
  82.5 1.5 collective-permute-start.18
  84.0 1.1 collective-permute-done.5.refs_6_
  85.1 0.7 copy-done.7
  85.8 1.4 collective-permute-start.20
  87.3 0.1 copy.16
  87.5 0.1 slice_reduce_fusion
  87.6 0.1 convert_reduce_fusion.1
  87.7 0.1 eq.85
  87.8 19.9 %collective-permute-done.18.refs_4_.refs_10_ = bf16[256,1024]{1,0:T(8,128)(2,1)} collective-permute-done((bf16[256,1024]{1,0:T(8,128)(2,1)S(1)}, bf16[256,1024]{1,0:T(8,128)(2,1)}, u32[]{:S(2)}, u32[]{:S(2)}) %collective-permute-start.18) | collective-permute-done | bytes 524320 | tf_op jit(solution)/shard_map/ppermute | solution.py:243
  107.7 3.5 %collective-permute-start.7 = (bf16[256,1024]{1,0:T(8,128)(2,1)S(1)}, bf16[256,1024]{1,0:T(8,128)(2,1)}, u32[]{:S(2)}, u32[]{:S(2)}) collective-permute-start(bf16[256,1024]{1,0:T(8,128)(2,1)S(1)} %collective-permute-done.6.refs_0_.refs_6_), channel_id=1, source_target_pairs={{0,8},{1,9},{2,10},{3,11},{4,12},{5,13},{6,14},{7,15},{8,0},{9,1},... | collective-permute-start | bytes 1572872 | tf_op jit(solution)/shard_map/ppermute | solution.py:243
  111.2 0.5 collective-permute-start.19
  111.8 0.1 convert_reduce_fusion
  111.9 0.4 fusion.2.refs_2_
  112.3 10.3 %collective-permute-done.7.refs_0_.refs_6_ = bf16[256,1024]{1,0:T(8,128)(2,1)} collective-permute-done((bf16[256,1024]{1,0:T(8,128)(2,1)S(1)}, bf16[256,1024]{1,0:T(8,128)(2,1)}, u32[]{:S(2)}, u32[]{:S(2)}) %collective-permute-start.7) | collective-permute-done | bytes 524320 | tf_op jit(solution)/shard_map/ppermute | solution.py:243
  122.6 1.5 collective-permute-start.9
  124.1 1.5 collective-permute-start.11
  125.7 0.5 collective-permute-start.13
  126.1 0.6 fusion.19
  130.8 1.4 fusion.6
  132.2 5.6 %collective-permute-done.9.refs_2_.refs_8_ = bf16[256,1024]{1,0:T(8,128)(2,1)} collective-permute-done((bf16[256,1024]{1,0:T(8,128)(2,1)}, bf16[256,1024]{1,0:T(8,128)(2,1)}, u32[]{:S(2)}, u32[]{:S(2)}) %collective-permute-start.9) | collective-permute-done | bytes 524320 | tf_op jit(solution)/shard_map/ppermute | solution.py:243
  137.8 10.0 %collective-permute-done.11.refs_4_.refs_10_ = bf16[256,1024]{1,0:T(8,128)(2,1)} collective-permute-done((bf16[256,1024]{1,0:T(8,128)(2,1)}, bf16[256,1024]{1,0:T(8,128)(2,1)}, u32[]{:S(2)}, u32[]{:S(2)}) %collective-permute-start.11) | collective-permute-done | bytes 524320 | tf_op jit(solution)/shard_map/ppermute | solution.py:243
  147.8 0.5 collective-permute-start.10
  148.4 0.4 collective-permute-start.14
  148.9 2.0 %forward.1 = (bf16[128,2048]{1,0:T(8,128)(2,1)S(1)}, f32[4,2,256,128]{3,2,1,0:T(8,128)S(1)}, bf16[2,128,1024]{2,1,0:T(8,128)(2,1)S(1)}) custom-call(s32[7]{0:T(128)S(1)} %concatenate.6.refs_0_.meta, bf16[128,2048]{1,0:T(8,128)(2,1)S(1)} %pad_maximum_fusion.refs_1_.refs_2_, f32[2,64,128]{2,1,0:T(8,128)S(1)} %fusion.2.refs_2_, bf16[128,1024]{1,0:T(8,128)(2,1)S(1)} %bitcast.46, ...), custom_call_target="tpu_custom_call" | custom-call | flops 1073741824 | bytes 8388608 | tf_op jit(solution)/shard_map/forward/pallas_call | solution.py:311
  151.0 4.3 %grad_0.1 = (bf16[128,2048]{1,0:T(8,128)(2,1)}, bf16[128,256]{1,0:T(8,128)(2,1)S(1)}, bf16[128,256]{1,0:T(8,128)(2,1)S(1)}, bf16[128,256]{1,0:T(8,128)(2,1)S(1)}, bf16[128,256]{1,0:T(8,128)(2,1)S(1)}) custom-call(s32[7]{0:T(128)S(1)} %concatenate.6.refs_0_.meta, bf16[128,4096]{1,0:T(8,128)(2,1)S(1)} %bitcast.39, ...), custom_call_target="tpu_custom_call" | custom-call | flops 1073741824 | bytes 12582912 | tf_op jit(solution)/shard_map/grad_0/pallas_call | solution.py:343
  155.3 4.9 %grad_1.1 = (bf16[128,2048]{1,0:T(8,128)(2,1)}, bf16[128,256]{1,0:T(8,128)(2,1)S(1)}, bf16[128,256]{1,0:T(8,128)(2,1)S(1)}, bf16[128,256]{1,0:T(8,128)(2,1)S(1)}, bf16[128,256]{1,0:T(8,128)(2,1)S(1)}) custom-call(s32[7]{0:T(128)S(1)} %concatenate.6.refs_0_.meta, bf16[128,4096]{1,0:T(8,128)(2,1)S(1)} %bitcast.40, ...), custom_call_target="tpu_custom_call", output_to_operand_aliasing={{0}: (8, {})} | custom-call | flops 1073741824 | bytes 12582912 | tf_op jit(solution)/shard_map/grad_1/pallas_call | solution.py:343
  160.3 0.9 collective-permute-start.25
  161.1 4.4 %grad_2.1 = (bf16[128,2048]{1,0:T(8,128)(2,1)}, bf16[128,256]{1,0:T(8,128)(2,1)S(1)}, bf16[128,256]{1,0:T(8,128)(2,1)S(1)}, bf16[128,256]{1,0:T(8,128)(2,1)S(1)}, bf16[128,256]{1,0:T(8,128)(2,1)S(1)}) custom-call(s32[7]{0:T(128)S(1)} %concatenate.6.refs_0_.meta, bf16[128,4096]{1,0:T(8,128)(2,1)S(1)} %bitcast.41, ...), custom_call_target="tpu_custom_call", output_to_operand_aliasing={{0}: (14, {})} | custom-call | flops 1073741824 | bytes 12582912 | tf_op jit(solution)/shard_map/grad_2/pallas_call | solution.py:343
  165.5 1.3 collective-permute-start.26
  166.9 1.4 collective-permute-start.27
  168.3 4.2 %grad_3.1 = (bf16[128,2048]{1,0:T(8,128)(2,1)}, bf16[128,256]{1,0:T(8,128)(2,1)S(1)}, bf16[128,256]{1,0:T(8,128)(2,1)S(1)}, bf16[128,256]{1,0:T(8,128)(2,1)S(1)}, bf16[128,256]{1,0:T(8,128)(2,1)S(1)}) custom-call(s32[7]{0:T(128)S(1)} %concatenate.6.refs_0_.meta, bf16[128,4096]{1,0:T(8,128)(2,1)S(1)} %bitcast.42, ...), custom_call_target="tpu_custom_call", output_to_operand_aliasing={{0}: (14, {})} | custom-call | flops 1073741824 | bytes 12582912 | tf_op jit(solution)/shard_map/grad_3/pallas_call | solution.py:343
  172.5 0.9 collective-permute-start.34
  173.4 1.3 collective-permute-start.35
  174.7 1.4 collective-permute-start.36
  176.1 0.8 collective-permute-start.31
  176.9 2.3 %project_0.1.refs_2_ = f32[128,4096]{1,0:T(8,128)S(1)} custom-call(s32[7]{0:T(128)S(1)} %concatenate.6.refs_0_.meta, bf16[128,2048]{1,0:T(8,128)(2,1)S(1)} %get-tuple-element.26.context_ref.refs_3_, bf16[256,4096]{1,0:T(8,128)(2,1)S(1)} %copy-done.1, bf16[256,4096]{1,0:T(8,128)(2,1)} %collective-permute-done.24.refs_1_.refs_7_), custom_call_target="tpu_custom_call" | custom-call | flops 536870912 | bytes 8388608 | tf_op jit(solution)/shard_map/project_0/pallas_call | solution.py:377
  179.2 3.0 %project_1.1.refs_8_ = f32[128,4096]{1,0:T(8,128)S(1)} custom-call(s32[7]{0:T(128)S(1)} %concatenate.6.refs_0_.meta, bf16[128,2048]{1,0:T(8,128)(2,1)S(1)} %get-tuple-element.26.context_ref.refs_3_, bf16[256,4096]{1,0:T(8,128)(2,1)} %collective-permute-done.22.refs_0_.refs_6_, bf16[256,4096]{1,0:T(8,128)(2,1)} %collective-permute-done.23.refs_1_.refs_7_, ...), custom_call_target="tpu_custom_call" | custom-call | flops 536870912 | bytes 8388608 | tf_op jit(solution)/shard_map/project_1/pallas_call | solution.py:377
  182.2 1.3 collective-permute-start.32
  183.5 1.4 collective-permute-start.33
  184.9 0.8 collective-permute-start.28
  185.7 1.3 collective-permute-start.29
  187.0 1.4 collective-permute-start.30
  188.4 2.4 %project_2.1.refs_8_ = f32[128,4096]{1,0:T(8,128)S(1)} custom-call(s32[7]{0:T(128)S(1)} %concatenate.6.refs_0_.meta, bf16[128,2048]{1,0:T(8,128)(2,1)S(1)} %get-tuple-element.26.context_ref.refs_3_, bf16[256,1024]{1,0:T(8,128)(2,1)S(1)} %collective-permute-done.6.refs_0_.refs_6_, bf16[256,1024]{1,0:T(8,128)(2,1)} %collective-permute-done.15.refs_1_.refs_7_, ...), custom_call_target="tpu_custom_call" | custom-call | flops 536870912 | bytes 8388608 | tf_op jit(solution)/shard_map/project_2/pallas_call | solution.py:377
  190.8 3.2 %project_3.1 = bf16[128,4096]{1,0:T(8,128)(2,1)} custom-call(s32[7]{0:T(128)S(1)} %concatenate.6.refs_0_.meta, bf16[128,2048]{1,0:T(8,128)(2,1)S(1)} %get-tuple-element.26.context_ref.refs_3_, bf16[256,1024]{1,0:T(8,128)(2,1)} %collective-permute-done.7.refs_0_.refs_6_, bf16[256,1024]{1,0:T(8,128)(2,1)S(1)} %collective-permute-done.8.refs_1_.refs_7_, ...), custom_call_target="tpu_custom_call" | custom-call | flops 536870912 | bytes 8388608 | tf_op jit(solution)/shard_map/project_3/pallas_call | solution.py:377
  194.1 1.4 combine.1
  (68 shorter events, 0.6 us)
Async XLA Ops:
  0.6 80.6 %copy-start.1 = (bf16[256,4096]{1,0:T(8,128)(2,1)S(1)}, bf16[256,4096]{1,0:T(8,128)(2,1)}, u32[]{:S(2)}) copy-start(bf16[256,4096]{1,0:T(8,128)(2,1)} %refs_6_.1) | copy-start | bytes 6291460
  0.6 61.0 %copy-start.2 = (bf16[1,128,1024]{2,1,0:T(8,128)(2,1)S(1)}, bf16[1,128,1024]{2,1,0:T(8,128)(2,1)}, u32[]{:S(2)}) copy-start(bf16[1,128,1024]{2,1,0:T(8,128)(2,1)} %param.8) | copy-start | bytes 786436
  0.7 86.7 %copy-start.12 = (s32[1,16]{1,0:T(1,128)S(1)}, s32[1,16]{1,0:T(1,128)}, u32[]{:S(2)}) copy-start(s32[1,16]{1,0:T(1,128)} %param.11) | copy-start | bytes 196
  0.7 111.2 %copy-start.13 = (s32[1,4,4]{2,1,0:T(4,128)S(1)}, s32[1,4,4]{2,1,0:T(4,128)}, u32[]{:S(2)}) copy-start(s32[1,4,4]{2,1,0:T(4,128)} %param.12) | copy-start | bytes 196
  0.7 80.6 %collective-permute-start.22 = (bf16[256,4096]{1,0:T(8,128)(2,1)}, bf16[256,4096]{1,0:T(8,128)(2,1)}, u32[]{:S(2)}, u32[]{:S(2)}) collective-permute-start(bf16[256,4096]{1,0:T(8,128)(2,1)} %refs_6_.1), channel_id=1, source_target_pairs={{0,8},{1,9},{2,10},{3,11},{4,12},{5,13},{6,14},{7,15},{8,0},{9,1},... | collective-permute-start | bytes 6291464 | tf_op jit(solution)/shard_map/ppermute | solution.py:243
  4.9 55.2 %collective-permute-start.6 = (bf16[256,1024]{1,0:T(8,128)(2,1)S(1)}, bf16[256,1024]{1,0:T(8,128)(2,1)S(1)}, u32[]{:S(2)}, u32[]{:S(2)}) collective-permute-start(bf16[256,1024]{1,0:T(8,128)(2,1)S(1)} %constant_dynamic-slice_fusion), channel_id=1, source_target_pairs={{0,16},{1,17},{2,18},{3,19},{4,20},{5,21},{6,22},{7,23},{8,24},{9,... | collective-permute-start | bytes 1572872 | tf_op jit(solution)/shard_map/ppermute | solution.py:243
  12.0 49.6 %collective-permute-start = (bf16[64,2048]{1,0:T(8,128)(2,1)S(1)}, bf16[64,2048]{1,0:T(8,128)(2,1)S(1)}, u32[]{:S(2)}, u32[]{:S(2)}) collective-permute-start(bf16[64,2048]{1,0:T(8,128)(2,1)S(1)} %get-tuple-element.55), channel_id=1, source_target_pairs={{0,3},{1,2},{2,1},{3,0},{4,7},{5,6},{6,5},{7,4},{8,11},{9,10},{10,... | collective-permute-start | bytes 786440 | tf_op jit(solution)/shard_map/ppermute | solution.py:243
  14.5 47.8 %collective-permute-start.1 = (bf16[64,2048]{1,0:T(8,128)(2,1)S(1)}, bf16[64,2048]{1,0:T(8,128)(2,1)S(1)}, u32[]{:S(2)}, u32[]{:S(2)}) collective-permute-start(bf16[64,2048]{1,0:T(8,128)(2,1)S(1)} %get-tuple-element.54), channel_id=1, source_target_pairs={{0,2},{1,3},{2,0},{3,1},{4,6},{5,7},{6,4},{7,5},{8,10},{9,11},{10,... | collective-permute-start | bytes 786440 | tf_op jit(solution)/shard_map/ppermute | solution.py:243
  15.0 48.8 %collective-permute-start.2 = (bf16[64,2048]{1,0:T(8,128)(2,1)S(1)}, bf16[64,2048]{1,0:T(8,128)(2,1)S(1)}, u32[]{:S(2)}, u32[]{:S(2)}) collective-permute-start(bf16[64,2048]{1,0:T(8,128)(2,1)S(1)} %get-tuple-element.53), channel_id=1, source_target_pairs={{0,1},{1,0},{2,3},{3,2},{4,5},{5,4},{6,7},{7,6},{8,9},{9,8},{10,11... | collective-permute-start | bytes 786440 | tf_op jit(solution)/shard_map/ppermute | solution.py:243
  60.1 27.1 %collective-permute-start.16 = (bf16[256,1024]{1,0:T(8,128)(2,1)S(1)}, bf16[256,1024]{1,0:T(8,128)(2,1)S(1)}, u32[]{:S(2)}, u32[]{:S(2)}) collective-permute-start(bf16[256,1024]{1,0:T(8,128)(2,1)S(1)} %collective-permute-done.6.refs_0_.refs_6_), channel_id=1, source_target_pairs={{0,1},{1,0},{2,3},{3,2},{4,5},{5,4},{6,7},{7,6},{8,9},{9,8},{10,11... | collective-permute-start | bytes 1572872 | tf_op jit(solution)/shard_map/ppermute | solution.py:243
  61.6 0.7 copy-start.9
  61.6 19.0 %collective-permute-start.3 = (bf16[128,1024]{1,0:T(8,128)(2,1)S(1)}, bf16[128,1024]{1,0:T(8,128)(2,1)S(1)}, u32[]{:S(2)}, u32[]{:S(2)}) collective-permute-start(bf16[128,1024]{1,0:T(8,128)(2,1)S(1)} %bitcast.43), channel_id=1, source_target_pairs={{0,1},{1,0},{2,3},{3,2},{4,5},{5,4},{6,7},{7,6},{8,9},{9,8},{10,11... | collective-permute-start | bytes 786440 | tf_op jit(solution)/shard_map/ppermute | solution.py:243
  62.3 1.5 copy-start.10
  62.3 19.5 %collective-permute-start.4 = (bf16[128,1024]{1,0:T(8,128)(2,1)S(1)}, bf16[128,1024]{1,0:T(8,128)(2,1)S(1)}, u32[]{:S(2)}, u32[]{:S(2)}) collective-permute-start(bf16[128,1024]{1,0:T(8,128)(2,1)S(1)} %bitcast.44), channel_id=1, source_target_pairs={{0,2},{1,3},{2,0},{3,1},{4,6},{5,7},{6,4},{7,5},{8,10},{9,11},{10,... | collective-permute-start | bytes 786440 | tf_op jit(solution)/shard_map/ppermute | solution.py:243
  63.8 23.4 %copy-start.11 = (bf16[64,2048]{1,0:T(8,128)(2,1)}, bf16[64,2048]{1,0:T(8,128)(2,1)S(1)}, u32[]{:S(2)}) copy-start(bf16[64,2048]{1,0:T(8,128)(2,1)S(1)} %collective-permute-done.2) | copy-start | bytes 786436
  63.8 21.3 %collective-permute-start.5 = (bf16[128,1024]{1,0:T(8,128)(2,1)S(1)}, bf16[128,1024]{1,0:T(8,128)(2,1)S(1)}, u32[]{:S(2)}, u32[]{:S(2)}) collective-permute-start(bf16[128,1024]{1,0:T(8,128)(2,1)S(1)} %bitcast.45), channel_id=1, source_target_pairs={{0,3},{1,2},{2,1},{3,0},{4,7},{5,6},{6,5},{7,4},{8,11},{9,10},{10,... | collective-permute-start | bytes 786440 | tf_op jit(solution)/shard_map/ppermute | solution.py:243
  80.6 0.7 copy-start.3
  81.3 67.1 %collective-permute-start.24 = (bf16[256,4096]{1,0:T(8,128)(2,1)S(1)}, bf16[256,4096]{1,0:T(8,128)(2,1)}, u32[]{:S(2)}, u32[]{:S(2)}) collective-permute-start(bf16[256,4096]{1,0:T(8,128)(2,1)S(1)} %copy-done.1), channel_id=1, source_target_pairs={{0,4},{1,5},{2,6},{3,7},{4,0},{5,1},{6,2},{7,3},{8,12},{9,13},{10,... | collective-permute-start | bytes 6291464 | tf_op jit(solution)/shard_map/ppermute | solution.py:243
  81.3 67.1 %collective-permute-start.23 = (bf16[256,4096]{1,0:T(8,128)(2,1)}, bf16[256,4096]{1,0:T(8,128)(2,1)}, u32[]{:S(2)}, u32[]{:S(2)}) collective-permute-start(bf16[256,4096]{1,0:T(8,128)(2,1)} %collective-permute-done.22.refs_0_.refs_6_), channel_id=1, source_target_pairs={{0,4},{1,5},{2,6},{3,7},{4,0},{5,1},{6,2},{7,3},{8,12},{9,13},{10,... | collective-permute-start | bytes 6291464 | tf_op jit(solution)/shard_map/ppermute | solution.py:243
  81.8 0.7 copy-start.5
  82.5 25.2 %collective-permute-start.18 = (bf16[256,1024]{1,0:T(8,128)(2,1)S(1)}, bf16[256,1024]{1,0:T(8,128)(2,1)}, u32[]{:S(2)}, u32[]{:S(2)}) collective-permute-start(bf16[256,1024]{1,0:T(8,128)(2,1)S(1)} %collective-permute-done.6.refs_0_.refs_6_), channel_id=1, source_target_pairs={{0,2},{1,3},{2,0},{3,1},{4,6},{5,7},{6,4},{7,5},{8,10},{9,11},{10,... | collective-permute-start | bytes 1572872 | tf_op jit(solution)/shard_map/ppermute | solution.py:243
  85.1 0.7 copy-start.7
  85.8 25.4 %collective-permute-start.20 = (bf16[256,1024]{1,0:T(8,128)(2,1)S(1)}, bf16[256,1024]{1,0:T(8,128)(2,1)}, u32[]{:S(2)}, u32[]{:S(2)}) collective-permute-start(bf16[256,1024]{1,0:T(8,128)(2,1)S(1)} %collective-permute-done.6.refs_0_.refs_6_), channel_id=1, source_target_pairs={{0,3},{1,2},{2,1},{3,0},{4,7},{5,6},{6,5},{7,4},{8,11},{9,10},{10,... | collective-permute-start | bytes 1572872 | tf_op jit(solution)/shard_map/ppermute | solution.py:243
  87.2 24.0 %collective-permute-start.15 = (bf16[256,1024]{1,0:T(8,128)(2,1)S(1)}, bf16[256,1024]{1,0:T(8,128)(2,1)}, u32[]{:S(2)}, u32[]{:S(2)}) collective-permute-start(bf16[256,1024]{1,0:T(8,128)(2,1)S(1)} %collective-permute-done.6.refs_0_.refs_6_), channel_id=1, source_target_pairs={{0,4},{1,5},{2,6},{3,7},{4,0},{5,1},{6,2},{7,3},{8,12},{9,13},{10,... | collective-permute-start | bytes 1572872 | tf_op jit(solution)/shard_map/ppermute | solution.py:243
  107.7 14.9 %collective-permute-start.7 = (bf16[256,1024]{1,0:T(8,128)(2,1)S(1)}, bf16[256,1024]{1,0:T(8,128)(2,1)}, u32[]{:S(2)}, u32[]{:S(2)}) collective-permute-start(bf16[256,1024]{1,0:T(8,128)(2,1)S(1)} %collective-permute-done.6.refs_0_.refs_6_), channel_id=1, source_target_pairs={{0,8},{1,9},{2,10},{3,11},{4,12},{5,13},{6,14},{7,15},{8,0},{9,1},... | collective-permute-start | bytes 1572872 | tf_op jit(solution)/shard_map/ppermute | solution.py:243
  111.2 12.9 %collective-permute-start.17 = (bf16[256,1024]{1,0:T(8,128)(2,1)S(1)}, bf16[256,1024]{1,0:T(8,128)(2,1)}, u32[]{:S(2)}, u32[]{:S(2)}) collective-permute-start(bf16[256,1024]{1,0:T(8,128)(2,1)S(1)} %collective-permute-done.16.refs_2_.refs_8_), channel_id=1, source_target_pairs={{0,4},{1,5},{2,6},{3,7},{4,0},{5,1},{6,2},{7,3},{8,12},{9,13},{10,... | collective-permute-start | bytes 1572872 | tf_op jit(solution)/shard_map/ppermute | solution.py:243
  111.2 14.4 %collective-permute-start.19 = (bf16[256,1024]{1,0:T(8,128)(2,1)}, bf16[256,1024]{1,0:T(8,128)(2,1)}, u32[]{:S(2)}, u32[]{:S(2)}) collective-permute-start(bf16[256,1024]{1,0:T(8,128)(2,1)} %collective-permute-done.18.refs_4_.refs_10_), channel_id=1, source_target_pairs={{0,4},{1,5},{2,6},{3,7},{4,0},{5,1},{6,2},{7,3},{8,12},{9,13},{10,... | collective-permute-start | bytes 1572872 | tf_op jit(solution)/shard_map/ppermute | solution.py:243
  122.6 15.2 %collective-permute-start.9 = (bf16[256,1024]{1,0:T(8,128)(2,1)}, bf16[256,1024]{1,0:T(8,128)(2,1)}, u32[]{:S(2)}, u32[]{:S(2)}) collective-permute-start(bf16[256,1024]{1,0:T(8,128)(2,1)} %collective-permute-done.7.refs_0_.refs_6_), channel_id=1, source_target_pairs={{0,1},{1,0},{2,3},{3,2},{4,5},{5,4},{6,7},{7,6},{8,9},{9,8},{10,11... | collective-permute-start | bytes 1572872 | tf_op jit(solution)/shard_map/ppermute | solution.py:243
  124.1 23.7 %collective-permute-start.11 = (bf16[256,1024]{1,0:T(8,128)(2,1)}, bf16[256,1024]{1,0:T(8,128)(2,1)}, u32[]{:S(2)}, u32[]{:S(2)}) collective-permute-start(bf16[256,1024]{1,0:T(8,128)(2,1)} %collective-permute-done.7.refs_0_.refs_6_), channel_id=1, source_target_pairs={{0,2},{1,3},{2,0},{3,1},{4,6},{5,7},{6,4},{7,5},{8,10},{9,11},{10,... | collective-permute-start | bytes 1572872 | tf_op jit(solution)/shard_map/ppermute | solution.py:243
  125.7 22.2 %collective-permute-start.13 = (bf16[256,1024]{1,0:T(8,128)(2,1)}, bf16[256,1024]{1,0:T(8,128)(2,1)}, u32[]{:S(2)}, u32[]{:S(2)}) collective-permute-start(bf16[256,1024]{1,0:T(8,128)(2,1)} %collective-permute-done.7.refs_0_.refs_6_), channel_id=1, source_target_pairs={{0,3},{1,2},{2,1},{3,0},{4,7},{5,6},{6,5},{7,4},{8,11},{9,10},{10,... | collective-permute-start | bytes 1572872 | tf_op jit(solution)/shard_map/ppermute | solution.py:243
  130.8 18.1 %copy-start.4 = (bf16[128,1024]{1,0:T(8,128)(2,1)S(1)}, bf16[128,1024]{1,0:T(8,128)(2,1)}, u32[]{:S(2)}) copy-start(bf16[128,1024]{1,0:T(8,128)(2,1)} %copy-done.3) | copy-start | bytes 786436
  130.8 18.1 %copy-start.6 = (bf16[128,1024]{1,0:T(8,128)(2,1)S(1)}, bf16[128,1024]{1,0:T(8,128)(2,1)}, u32[]{:S(2)}) copy-start(bf16[128,1024]{1,0:T(8,128)(2,1)} %copy-done.5) | copy-start | bytes 786436
  130.8 18.2 %copy-start.8 = (bf16[128,1024]{1,0:T(8,128)(2,1)S(1)}, bf16[128,1024]{1,0:T(8,128)(2,1)}, u32[]{:S(2)}) copy-start(bf16[128,1024]{1,0:T(8,128)(2,1)} %copy-done.7) | copy-start | bytes 786436
  137.8 27.7 %collective-permute-start.8 = (bf16[256,1024]{1,0:T(8,128)(2,1)}, bf16[256,1024]{1,0:T(8,128)(2,1)S(1)}, u32[]{:S(2)}, u32[]{:S(2)}) collective-permute-start(bf16[256,1024]{1,0:T(8,128)(2,1)} %collective-permute-done.7.refs_0_.refs_6_), channel_id=1, source_target_pairs={{0,4},{1,5},{2,6},{3,7},{4,0},{5,1},{6,2},{7,3},{8,12},{9,13},{10,... | collective-permute-start | bytes 1572872 | tf_op jit(solution)/shard_map/ppermute | solution.py:243
  147.8 12.4 %collective-permute-start.21 = (bf16[256,1024]{1,0:T(8,128)(2,1)}, bf16[256,1024]{1,0:T(8,128)(2,1)S(1)}, u32[]{:S(2)}, u32[]{:S(2)}) collective-permute-start(bf16[256,1024]{1,0:T(8,128)(2,1)} %collective-permute-done.20.refs_6_.refs_12_), channel_id=1, source_target_pairs={{0,4},{1,5},{2,6},{3,7},{4,0},{5,1},{6,2},{7,3},{8,12},{9,13},{10,... | collective-permute-start | bytes 1572872 | tf_op jit(solution)/shard_map/ppermute | solution.py:243
  147.8 19.0 %collective-permute-start.10 = (bf16[256,1024]{1,0:T(8,128)(2,1)}, bf16[256,1024]{1,0:T(8,128)(2,1)S(1)}, u32[]{:S(2)}, u32[]{:S(2)}) collective-permute-start(bf16[256,1024]{1,0:T(8,128)(2,1)} %collective-permute-done.9.refs_2_.refs_8_), channel_id=1, source_target_pairs={{0,4},{1,5},{2,6},{3,7},{4,0},{5,1},{6,2},{7,3},{8,12},{9,13},{10,... | collective-permute-start | bytes 1572872 | tf_op jit(solution)/shard_map/ppermute | solution.py:243
  148.3 19.9 %collective-permute-start.12 = (bf16[256,1024]{1,0:T(8,128)(2,1)}, bf16[256,1024]{1,0:T(8,128)(2,1)S(1)}, u32[]{:S(2)}, u32[]{:S(2)}) collective-permute-start(bf16[256,1024]{1,0:T(8,128)(2,1)} %collective-permute-done.11.refs_4_.refs_10_), channel_id=1, source_target_pairs={{0,4},{1,5},{2,6},{3,7},{4,0},{5,1},{6,2},{7,3},{8,12},{9,13},{10,... | collective-permute-start | bytes 1572872 | tf_op jit(solution)/shard_map/ppermute | solution.py:243
  148.4 19.9 %collective-permute-start.14 = (bf16[256,1024]{1,0:T(8,128)(2,1)}, bf16[256,1024]{1,0:T(8,128)(2,1)S(1)}, u32[]{:S(2)}, u32[]{:S(2)}) collective-permute-start(bf16[256,1024]{1,0:T(8,128)(2,1)} %collective-permute-done.13.refs_6_.refs_12_), channel_id=1, source_target_pairs={{0,4},{1,5},{2,6},{3,7},{4,0},{5,1},{6,2},{7,3},{8,12},{9,13},{10,... | collective-permute-start | bytes 1572872 | tf_op jit(solution)/shard_map/ppermute | solution.py:243
  148.9 2.0 %copy-start = (bf16[1,128,4096]{2,1,0:T(8,128)(2,1)S(1)}, bf16[1,128,4096]{2,1,0:T(8,128)(2,1)}, u32[]{:S(2)}) copy-start(bf16[1,128,4096]{2,1,0:T(8,128)(2,1)} %param.9) | copy-start | bytes 3145732
  160.3 14.4 %collective-permute-start.25 = (bf16[128,256]{1,0:T(8,128)(2,1)S(1)}, bf16[128,256]{1,0:T(8,128)(2,1)S(1)}, u32[]{:S(2)}, u32[]{:S(2)}) collective-permute-start(bf16[128,256]{1,0:T(8,128)(2,1)S(1)} %get-tuple-element.34), channel_id=1, source_target_pairs={{0,1},{1,0},{2,3},{3,2},{4,5},{5,4},{6,7},{7,6},{8,9},{9,8},{10,11... | collective-permute-start | bytes 196616 | tf_op jit(solution)/shard_map/ppermute | solution.py:243
  165.5 10.6 %collective-permute-start.26 = (bf16[128,256]{1,0:T(8,128)(2,1)S(1)}, bf16[128,256]{1,0:T(8,128)(2,1)S(1)}, u32[]{:S(2)}, u32[]{:S(2)}) collective-permute-start(bf16[128,256]{1,0:T(8,128)(2,1)S(1)} %get-tuple-element.35), channel_id=1, source_target_pairs={{0,2},{1,3},{2,0},{3,1},{4,6},{5,7},{6,4},{7,5},{8,10},{9,11},{10,... | collective-permute-start | bytes 196616 | tf_op jit(solution)/shard_map/ppermute | solution.py:243
  166.9 15.3 %collective-permute-start.27 = (bf16[128,256]{1,0:T(8,128)(2,1)S(1)}, bf16[128,256]{1,0:T(8,128)(2,1)S(1)}, u32[]{:S(2)}, u32[]{:S(2)}) collective-permute-start(bf16[128,256]{1,0:T(8,128)(2,1)S(1)} %get-tuple-element.36), channel_id=1, source_target_pairs={{0,3},{1,2},{2,1},{3,0},{4,7},{5,6},{6,5},{7,4},{8,11},{9,10},{10,... | collective-permute-start | bytes 196616 | tf_op jit(solution)/shard_map/ppermute | solution.py:243
  172.5 11.0 %collective-permute-start.34 = (bf16[128,256]{1,0:T(8,128)(2,1)S(1)}, bf16[128,256]{1,0:T(8,128)(2,1)S(1)}, u32[]{:S(2)}, u32[]{:S(2)}) collective-permute-start(bf16[128,256]{1,0:T(8,128)(2,1)S(1)} %get-tuple-element.46), channel_id=1, source_target_pairs={{0,1},{1,0},{2,3},{3,2},{4,5},{5,4},{6,7},{7,6},{8,9},{9,8},{10,11... | collective-permute-start | bytes 196616 | tf_op jit(solution)/shard_map/ppermute | solution.py:243
  173.4 11.6 %collective-permute-start.35 = (bf16[128,256]{1,0:T(8,128)(2,1)S(1)}, bf16[128,256]{1,0:T(8,128)(2,1)S(1)}, u32[]{:S(2)}, u32[]{:S(2)}) collective-permute-start(bf16[128,256]{1,0:T(8,128)(2,1)S(1)} %get-tuple-element.47), channel_id=1, source_target_pairs={{0,2},{1,3},{2,0},{3,1},{4,6},{5,7},{6,4},{7,5},{8,10},{9,11},{10,... | collective-permute-start | bytes 196616 | tf_op jit(solution)/shard_map/ppermute | solution.py:243
  174.7 11.1 %collective-permute-start.36 = (bf16[128,256]{1,0:T(8,128)(2,1)S(1)}, bf16[128,256]{1,0:T(8,128)(2,1)S(1)}, u32[]{:S(2)}, u32[]{:S(2)}) collective-permute-start(bf16[128,256]{1,0:T(8,128)(2,1)S(1)} %get-tuple-element.48), channel_id=1, source_target_pairs={{0,3},{1,2},{2,1},{3,0},{4,7},{5,6},{6,5},{7,4},{8,11},{9,10},{10,... | collective-permute-start | bytes 196616 | tf_op jit(solution)/shard_map/ppermute | solution.py:243
  176.1 10.9 %collective-permute-start.31 = (bf16[128,256]{1,0:T(8,128)(2,1)S(1)}, bf16[128,256]{1,0:T(8,128)(2,1)S(1)}, u32[]{:S(2)}, u32[]{:S(2)}) collective-permute-start(bf16[128,256]{1,0:T(8,128)(2,1)S(1)} %get-tuple-element.42), channel_id=1, source_target_pairs={{0,1},{1,0},{2,3},{3,2},{4,5},{5,4},{6,7},{7,6},{8,9},{9,8},{10,11... | collective-permute-start | bytes 196616 | tf_op jit(solution)/shard_map/ppermute | solution.py:243
  182.2 11.9 %collective-permute-start.32 = (bf16[128,256]{1,0:T(8,128)(2,1)S(1)}, bf16[128,256]{1,0:T(8,128)(2,1)S(1)}, u32[]{:S(2)}, u32[]{:S(2)}) collective-permute-start(bf16[128,256]{1,0:T(8,128)(2,1)S(1)} %get-tuple-element.43), channel_id=1, source_target_pairs={{0,2},{1,3},{2,0},{3,1},{4,6},{5,7},{6,4},{7,5},{8,10},{9,11},{10,... | collective-permute-start | bytes 196616 | tf_op jit(solution)/shard_map/ppermute | solution.py:243
  183.5 10.6 %collective-permute-start.33 = (bf16[128,256]{1,0:T(8,128)(2,1)S(1)}, bf16[128,256]{1,0:T(8,128)(2,1)S(1)}, u32[]{:S(2)}, u32[]{:S(2)}) collective-permute-start(bf16[128,256]{1,0:T(8,128)(2,1)S(1)} %get-tuple-element.44), channel_id=1, source_target_pairs={{0,3},{1,2},{2,1},{3,0},{4,7},{5,6},{6,5},{7,4},{8,11},{9,10},{10,... | collective-permute-start | bytes 196616 | tf_op jit(solution)/shard_map/ppermute | solution.py:243
  184.9 9.1 %collective-permute-start.28 = (bf16[128,256]{1,0:T(8,128)(2,1)S(1)}, bf16[128,256]{1,0:T(8,128)(2,1)S(1)}, u32[]{:S(2)}, u32[]{:S(2)}) collective-permute-start(bf16[128,256]{1,0:T(8,128)(2,1)S(1)} %get-tuple-element.38), channel_id=1, source_target_pairs={{0,1},{1,0},{2,3},{3,2},{4,5},{5,4},{6,7},{7,6},{8,9},{9,8},{10,11... | collective-permute-start | bytes 196616 | tf_op jit(solution)/shard_map/ppermute | solution.py:243
  185.7 8.4 %collective-permute-start.29 = (bf16[128,256]{1,0:T(8,128)(2,1)S(1)}, bf16[128,256]{1,0:T(8,128)(2,1)S(1)}, u32[]{:S(2)}, u32[]{:S(2)}) collective-permute-start(bf16[128,256]{1,0:T(8,128)(2,1)S(1)} %get-tuple-element.39), channel_id=1, source_target_pairs={{0,2},{1,3},{2,0},{3,1},{4,6},{5,7},{6,4},{7,5},{8,10},{9,11},{10,... | collective-permute-start | bytes 196616 | tf_op jit(solution)/shard_map/ppermute | solution.py:243
  187.0 7.1 %collective-permute-start.30 = (bf16[128,256]{1,0:T(8,128)(2,1)S(1)}, bf16[128,256]{1,0:T(8,128)(2,1)S(1)}, u32[]{:S(2)}, u32[]{:S(2)}) collective-permute-start(bf16[128,256]{1,0:T(8,128)(2,1)S(1)} %get-tuple-element.40), channel_id=1, source_target_pairs={{0,3},{1,2},{2,1},{3,0},{4,7},{5,6},{6,5},{7,4},{8,11},{9,10},{10,... | collective-permute-start | bytes 196616 | tf_op jit(solution)/shard_map/ppermute | solution.py:243

commit v2 on v1

--- a/solution.py
+++ b/solution.py
@@ -69,7 +69,8 @@
     for t in range(groups):
         start = pl.multiple_of(jnp.bitwise_xor(me, t) * per_shard, per_shard)
         copies.append(
-            pltpu.make_async_copy(kv_parts[t], kv_ref.at[pl.ds(start, per_shard)], sems.at[t])
+            pltpu.make_async_copy(
+                kv_parts[t].at[pl.ds(0, per_shard)], kv_ref.at[pl.ds(start, per_shard)], sems.at[t])
         )
     for copy in copies:
         copy.start()
@@ -211,6 +212,10 @@
     return 0
 
 
+def one_of(meta):
+    return 1
+
+
 def same_core(meta):
     return meta[2]
 
@@ -251,49 +256,48 @@
     def to_chip(block, j):
         return move(block, lambda d, c: (d ^ (2 * j), c))
 
+    def after(block, *others):
+        return lax.optimization_barrier((block,) + others)[0]
+
     swapped = (batches // 2) * GROUP_WIDTH == QUERY_HEADS * HEAD_WIDTH and groups == 4
-    slots = []
+    source = queries[0]
     if swapped:
         quarter = model // groups
-        column_fns = [functools.partial(lambda t, meta: jnp.bitwise_xor(meta[0], t), t) for t in range(groups)]
         far = lax.dynamic_slice_in_dim(out_proj, me * quarter, quarter, 1)
         two = to_chip(far, 2)
-        three = to_chip(two, 1)
-        one = to_chip(out_proj, 1)
-        for block in (out_proj, one):
-            slots.append(
-                [
-                    (block, ("own", same_core, zero_of)),
-                    (to_core(block), ("other", other_core, zero_of)),
-                ]
-            )
-        for piece in (two, three):
-            parts = []
-            for t in range(groups):
-                got = piece if t == 0 else to_ctx(piece, t)
-                parts.append((got, ("own", same_core, column_fns[t])))
-                parts.append((to_core(got), ("other", other_core, column_fns[t])))
-            slots.append(parts)
-    else:
-        full = lax.all_gather(out_proj, "dp", axis=0, tiled=True)
-        for g in range(KEY_VALUE_HEADS):
-            part = full[g * GROUP_WIDTH : (g + 1) * GROUP_WIDTH]
-            slots.append([(part, ("own", zero_of, zero_of))])
-
-    q_units = queries[0].reshape(unit_count, rows, QUERY_HEADS * HEAD_WIDTH)
+        source = after(source, far)
+
+    q_units = source.reshape(unit_count, rows, QUERY_HEADS * HEAD_WIDTH)
     dests = lax.rem(me + offsets, groups)
     sources = lax.rem(me - offsets + groups, groups)
     my_units = [q_units[j] for j in range(unit_count)]
+    kv_parts = [keys_values[0]]
+    kv_rows = keys_values.shape[1]
     for t in range(1, groups):
         chosen = q_units[0]
         for j in range(1, unit_count):
             chosen = jnp.where(dests[j] == (me ^ t), q_units[j], chosen)
-        got = to_ctx(chosen, t)
+        fold = QUERY_HEADS * HEAD_WIDTH // (2 * KEY_WIDTH)
+        chosen = jnp.concatenate(
+            [chosen[:, f * 2 * KEY_WIDTH : (f + 1) * 2 * KEY_WIDTH] for f in range(fold)], axis=0
+        )
+        sent = jnp.concatenate([keys_values[0], chosen], axis=0)
+        if t == 1:
+            first_sent = sent
+        got = to_ctx(sent, t)
+        kv_parts.append(got)
+        got = jnp.concatenate(
+            [got[kv_rows + f * rows : kv_rows + (f + 1) * rows] for f in range(fold)], axis=1
+        )
         my_units = [
             jnp.where(sources[j] == (me ^ t), got, my_units[j]) for j in range(unit_count)
         ]
     my_queries = jnp.concatenate(my_units, axis=0)
-    kv_parts = [keys_values[0]] + [to_ctx(keys_values[0], t) for t in range(1, groups)]
+    if swapped:
+        half = model // 2
+        one_a = to_chip(after(out_proj[:, :half], first_sent), 1)
+        own_other = to_core(after(out_proj, kv_parts[1]))
+        my_queries = after(my_queries, one_a)
 
     unit_ids = jnp.arange(unit_count, dtype=jnp.int32)
     first_pos = sources * per_shard + unit_ids * rows
@@ -332,13 +336,11 @@
 
     q_grad = None
     total = None
-    shares = []
-    count = len(slots)
-    for slot, parts in enumerate(slots):
+
+    def grad_step(slot, parts, q_grad):
         arrays = [part for part, _ in parts]
         plan = [entry for _, entry in parts]
         depth = arrays[0].shape[0]
-        weight_bytes = GROUP_WIDTH * model * 2
         with_q = q_grad is not None
         results = pl.pallas_call(
             functools.partial(grad_kernel, *sizes, slot, swapped, plan, with_q),
@@ -360,7 +362,7 @@
             compiler_params=params,
             cost_estimate=pl.CostEstimate(
                 flops=2 * per_shard * GROUP_WIDTH * model * 2,
-                bytes_accessed=3 * weight_bytes,
+                bytes_accessed=3 * GROUP_WIDTH * model * 2,
                 transcendentals=0,
             ),
             name=f"grad_{slot}",
@@ -368,13 +370,16 @@
             meta, grad_out[0], my_queries, context, probs, windows, *arrays,
             *([q_grad] if with_q else []),
         )
-        q_grad = results[0]
-        shares.append(
-            [results[1]] + [to_ctx(results[1 + t], t) for t in range(1, groups)]
-        )
+        return results[0], results[1:]
+
+    def send_shares(mine):
+        return [mine[0]] + [to_ctx(mine[t], t) for t in range(1, groups)]
+
+    def project_step(slot, parts, total, last):
+        arrays = [part for part, _ in parts]
+        plan = [entry for _, entry in parts]
         first = total is None
-        last = slot == count - 1
-        total = pl.pallas_call(
+        return pl.pallas_call(
             functools.partial(project_kernel, slot, swapped, plan, first),
             out_shape=jax.ShapeDtypeStruct((per_shard, model), BF16 if last else F32),
             in_specs=[in_smem()] + [whole()] * (1 + len(arrays) + (0 if first else 1)),
@@ -382,11 +387,77 @@
             compiler_params=params,
             cost_estimate=pl.CostEstimate(
                 flops=2 * per_shard * GROUP_WIDTH * model,
-                bytes_accessed=2 * weight_bytes,
+                bytes_accessed=2 * GROUP_WIDTH * model * 2,
                 transcendentals=0,
             ),
             name=f"project_{slot}",
         )(meta, context, *arrays, *([] if first else [total]))
+
+    shares = {}
+    count = KEY_VALUE_HEADS
+    if swapped:
+        order = (0, 2, 1, 3)
+        columns = [
+            functools.partial(lambda t, meta: jnp.bitwise_xor(meta[0], t), t)
+            for t in range(groups)
+        ]
+
+        def pair(block, column):
+            return [
+                (block, ("own", same_core, column)),
+                (to_core(block), ("other", other_core, column)),
+            ]
+
+        parts_0 = [
+            (out_proj, ("own", same_core, zero_of)),
+            (own_other, ("other", other_core, zero_of)),
+        ]
+        three = to_chip(after(two, one_a, context, own_other), 1)
+        q_grad, mine_0 = grad_step(0, parts_0, None)
+        total = project_step(0, parts_0, None, False)
+        twos = [two] + [to_ctx(after(two, *kv_parts[1:]), t) for t in range(1, groups)]
+        one_b = to_chip(after(out_proj[:, half:], one_a, context), 1)
+        middle = to_core(jnp.concatenate(twos + [one_a, three], axis=1))
+        parts_2 = []
+        for t in range(groups):
+            parts_2.append((twos[t], ("own", same_core, columns[t])))
+        for t in range(groups):
+            parts_2.append(
+                (middle[:, t * quarter : (t + 1) * quarter], ("other", other_core, columns[t]))
+            )
+        threes = [three] + [to_ctx(after(three, *twos[1:]), t) for t in range(1, groups)]
+        parts_3 = [
+            (three, ("own", same_core, columns[0])),
+            (middle[:, model + half :], ("other", other_core, columns[0])),
+        ]
+        for t in range(1, groups):
+            parts_3 += pair(threes[t], columns[t])
+        q_grad, mine_2 = grad_step(2, parts_2, q_grad)
+        total = project_step(2, parts_2, total, False)
+        parts_1 = [
+            (one_a, ("own", same_core, zero_of)),
+            (middle[:, model : model + half], ("other", other_core, zero_of)),
+        ]
+        parts_1 += pair(after(one_b, total, mine_2[0], *threes[1:]), one_of)
+        q_grad, mine_1 = grad_step(1, parts_1, q_grad)
+        total = project_step(1, parts_1, total, False)
+        merged = [
+            jnp.concatenate([mine_0[t], mine_2[t], mine_1[t]], axis=1) for t in range(groups)
+        ]
+        early = send_shares(merged)
+        for index, slot in enumerate((0, 2, 1)):
+            span = slice(index * 2 * HEAD_WIDTH, (index + 1) * 2 * HEAD_WIDTH)
+            shares[slot] = [part[:, span] for part in early]
+        q_grad, mine_3 = grad_step(3, parts_3, q_grad)
+        shares[3] = send_shares(mine_3)
+        total = project_step(3, parts_3, total, True)
+    else:
+        full = lax.all_gather(out_proj, "dp", axis=0, tiled=True)
+        for g in range(count):
+            parts = [(full[g * GROUP_WIDTH : (g + 1) * GROUP_WIDTH], ("own", zero_of, zero_of))]
+            q_grad, mine = grad_step(g, parts, q_grad)
+            shares[g] = send_shares(mine)
+            total = project_step(g, parts, total, g == count - 1)
 
     kv_grad = pl.pallas_call(
         functools.partial(combine_kernel, groups, list(range(count)), swapped),
@@ -395,7 +466,7 @@
         out_specs=whole(),
         compiler_params=params,
         name="combine",
-    )(meta, *[part for share in shares for part in share])
+    )(meta, *[part for slot in range(count) for part in shares[slot]])
     return (total[None], q_grad[None], kv_grad[None])
 
 

time: 196 us -> 123 us (0.63)
  waiting for transfers between devices: 107 us -> 42.5 us
  starting transfers between devices: 40.6 us -> 27.8 us
  local copies, waits for them, and re-layouts: 5.82 us -> 13.7 us
  Pallas kernels: 32.2 us -> 26.4 us
  other arithmetic: 2.93 us -> 5.09 us
    ppermute x37 -> x25, waiting for transfers between devices: 107 us -> 42.5 us  [move(): return lax.ppermute(block, ('dp', 'ctx'), pairs)]
    ppermute x37 -> x25, starting transfers between devices: 40.6 us -> 27.8 us  [move(): return lax.ppermute(block, ('dp', 'ctx'), pairs)]
    slice x0 -> x11, local copies, waits for them, and re-layouts: none -> 7.89 us  [the longest x3 2.96 us: on_device(): got[kv_rows + f * rows:kv_rows + (f + 1) * rows]]
    pallas_call x8, Pallas kernels: 28.8 us -> 22.2 us  [the longest x4 14.6 us: grad_step(): pl.pallas_call(functools.partial(grad_kernel, *sizes, slot, swapped, plan...]
  transfers between devices with their start and end apart: 37 -> 25, of which waited for: 7 -> 7; matrix products, arithmetic and copies ran while one was open for 4% -> 14% of each run, Pallas kernels for 16% -> 20%
where the time goes in v2:
time: 123 us
  waiting for transfers between devices  42.5 us (35%)
  starting transfers between devices  27.8 us (23%)
  Pallas kernels  26.4 us (21%)
  local copies, waits for them, and re-layouts  13.7 us (11%)
  between operations  6.92 us (6%)
  other arithmetic  5.09 us (4%)
    ppermute x25, waiting for transfers between devices, move(): return lax.ppermute(block, ('dp', 'ctx'), pairs)  42.5 us
    ppermute x25, starting transfers between devices, move(): return lax.ppermute(block, ('dp', 'ctx'), pairs)  27.8 us
    pallas_call x4, Pallas kernels, grad_step(): pl.pallas_call(functools.partial(grad_kernel, *sizes, slot, swapped, plan...  14.6 us
    pallas_call x4, Pallas kernels, project_step(): pl.pallas_call(functools.partial(project_kernel, slot, swapped, plan, fir...  7.61 us
    slice x3, local copies, waits for them, and re-layouts, on_device(): got[kv_rows + f * rows:kv_rows + (f + 1) * rows]  2.96 us
    pallas_call x1, Pallas kernels, on_device(): pl.pallas_call(functools.partial(forward_kernel, *sizes), out_shape=(jax....  2.88 us
  transfers between devices with their start and end apart: 25, of which 7 were waited for; matrix products, arithmetic and copies ran while one was open for 14% of the time, Pallas kernels for 20%

profile of v2, /device:TPU:0, one launch (start us, length us, event | category | flops | bytes accessed | tf_op | source)
XLA Modules:
  0.0 122.8 jit_solution(15577776397878728991)
XLA Ops:
  0.7 2.0 %constant_dynamic-slice_fusion = bf16[256,1024]{1,0:T(8,128)(2,1)} fusion(bf16[256,4096]{1,0:T(8,128)(2,1)} %refs_6_.1, s32[]{:T(128)S(6)} %select_n.87), kind=kLoop, calls=%fused_computation.58 | loop fusion | bytes 1048580 | tf_op jit(solution)/shard_map/dynamic_slice | solution.py:266
  2.7 4.0 %collective-permute-start.4 = (bf16[256,1024]{1,0:T(8,128)(2,1)}, bf16[256,1024]{1,0:T(8,128)(2,1)}, u32[]{:S(2)}, u32[]{:S(2)}) collective-permute-start(bf16[256,1024]{1,0:T(8,128)(2,1)} %constant_dynamic-slice_fusion), channel_id=1, source_target_pairs={{0,16},{1,17},{2,18},{3,19},{4,20},{5,21},{6,22},{7,23},{8,24},{9,... | collective-permute-start | bytes 1572872 | tf_op jit(solution)/shard_map/ppermute | solution.py:248
  6.7 0.8 slice_reduce_fusion.1
  7.5 0.6 slice.127
  10.1 1.1 broadcast_select_fusion.2
  11.3 1.3 %fusion.5 = (bf16[256,1024]{1,0:T(8,128)(2,1)}, bf16[256,1024]{1,0:T(8,128)(2,1)}, bf16[256,1024]{1,0:T(8,128)(2,1)}) fusion(bf16[128,1024]{1,0:T(8,128)(2,1)S(1)} %bitcast.26, bf16[64,1024]{1,0:T(8,128)(2,1)S(1)} %get-tuple-element.89, bf16[64,1024]{1,0:T(8,128)(2,1)S(1)} %get-tuple-element.88, bf16[64,1024]{1,0:T(8,128)(2,1)S(1)} %get-tuple-element.111, ...), kind=kLoop, calls=%fused_computation.8 | loop fusion | flops 4194304 | bytes 2621440 | tf_op jit(solution)/shard_map/concatenate | solution.py:284
  12.5 2.4 %collective-permute-start = (bf16[256,1024]{1,0:T(8,128)(2,1)}, bf16[256,1024]{1,0:T(8,128)(2,1)}, u32[]{:S(2)}, u32[]{:S(2)}) collective-permute-start(bf16[256,1024]{1,0:T(8,128)(2,1)} %get-tuple-element.85), channel_id=1, source_target_pairs={{0,3},{1,2},{2,1},{3,0},{4,7},{5,6},{6,5},{7,4},{8,11},{9,10},{10,... | collective-permute-start | bytes 1572872 | tf_op jit(solution)/shard_map/ppermute | solution.py:248
  15.0 0.5 collective-permute-start.1
  15.5 0.5 collective-permute-start.2
  16.0 1.6 %fusion.19 = (bf16[256,2048]{1,0:T(8,128)(2,1)}, bf16[256,2048]{1,0:T(8,128)(2,1)}) fusion(bf16[256,4096]{1,0:T(8,128)(2,1)S(1)} %copy-done), kind=kLoop, calls=%fused_computation.60 | loop fusion | bytes 4194304 | tf_op jit(solution)/shard_map/slice | solution.py:419
  17.6 1.6 %collective-permute-start.3 = (bf16[256,2048]{1,0:T(8,128)(2,1)}, bf16[256,2048]{1,0:T(8,128)(2,1)S(1)}, u32[]{:S(2)}, u32[]{:S(2)}) collective-permute-start(bf16[256,2048]{1,0:T(8,128)(2,1)} %get-tuple-element.36), channel_id=1, source_target_pairs={{0,8},{1,9},{2,10},{3,11},{4,12},{5,13},{6,14},{7,15},{8,0},{9,1},... | collective-permute-start | bytes 3145736 | tf_op jit(solution)/shard_map/ppermute | solution.py:248
  19.2 0.1 and_select_fusion
  19.3 0.1 copy.16
  19.4 0.1 and_select_fusion.1
  19.5 0.1 add.110
  19.6 0.1 slice_reduce_fusion
  19.7 0.1 convert_reduce_fusion.1
  19.8 0.1 eq.85
  19.8 0.1 convert_reduce_fusion
  19.9 0.4 fusion.2.refs_2_
  20.3 18.2 %collective-permute-done.2.refs_4_ = bf16[256,1024]{1,0:T(8,128)(2,1)} collective-permute-done((bf16[256,1024]{1,0:T(8,128)(2,1)}, bf16[256,1024]{1,0:T(8,128)(2,1)}, u32[]{:S(2)}, u32[]{:S(2)}) %collective-permute-start.2) | collective-permute-done | bytes 524320 | tf_op jit(solution)/shard_map/ppermute | solution.py:248
  38.5 0.6 fusion.29
  43.0 0.1 concatenate.36.refs_0_.meta
  43.1 1.6 %collective-permute-start.7 = (bf16[256,1024]{1,0:T(8,128)(2,1)}, bf16[256,1024]{1,0:T(8,128)(2,1)S(1)}, u32[]{:S(2)}, u32[]{:S(2)}) collective-permute-start(bf16[256,1024]{1,0:T(8,128)(2,1)} %collective-permute-done.4.refs_0_.refs_6_), channel_id=1, source_target_pairs={{0,1},{1,0},{2,3},{3,2},{4,5},{5,4},{6,7},{7,6},{8,9},{9,8},{10,11... | collective-permute-start | bytes 1572872 | tf_op jit(solution)/shard_map/ppermute | solution.py:248
  44.7 0.5 collective-permute-start.8
  45.2 1.5 %collective-permute-start.9 = (bf16[256,1024]{1,0:T(8,128)(2,1)}, bf16[256,1024]{1,0:T(8,128)(2,1)S(1)}, u32[]{:S(2)}, u32[]{:S(2)}) collective-permute-start(bf16[256,1024]{1,0:T(8,128)(2,1)} %collective-permute-done.4.refs_0_.refs_6_), channel_id=1, source_target_pairs={{0,3},{1,2},{2,1},{3,0},{4,7},{5,6},{6,5},{7,4},{8,11},{9,10},{10,... | collective-permute-start | bytes 1572872 | tf_op jit(solution)/shard_map/ppermute | solution.py:248
  46.7 1.0 fusion.20
  47.7 1.0 fusion.21
  48.7 1.0 fusion.22
  49.7 1.1 select_select_fusion.1
  50.8 1.1 select_select_fusion
  52.0 1.1 constant_dynamic-update-slice_fusion.5
  53.0 2.9 %forward.1 = (bf16[128,2048]{1,0:T(8,128)(2,1)S(1)}, f32[4,2,256,128]{3,2,1,0:T(8,128)S(1)}, bf16[2,128,1024]{2,1,0:T(8,128)(2,1)S(1)}) custom-call(s32[7]{0:T(128)S(1)} %concatenate.36.refs_0_.meta, bf16[128,2048]{1,0:T(8,128)(2,1)S(1)} %pad_maximum_fusion.3.refs_1_.refs_2_, f32[2,64,128]{2,1,0:T(8,128)S(1)} %fusion.2.refs_2_, ...), custom_call_target="tpu_custom_call" | custom-call | flops 1073741824 | bytes 8388608 | tf_op jit(solution)/shard_map/forward/pallas_call | solution.py:315
  56.0 1.6 %collective-permute-start.6 = (bf16[256,1024]{1,0:T(8,128)(2,1)}, bf16[256,1024]{1,0:T(8,128)(2,1)S(1)}, u32[]{:S(2)}, u32[]{:S(2)}) collective-permute-start(bf16[256,1024]{1,0:T(8,128)(2,1)} %collective-permute-done.4.refs_0_.refs_6_), channel_id=1, source_target_pairs={{0,8},{1,9},{2,10},{3,11},{4,12},{5,13},{6,14},{7,15},{8,0},{9,1},... | collective-permute-start | bytes 1572872 | tf_op jit(solution)/shard_map/ppermute | solution.py:248
  57.6 0.5 collective-permute-done.7.refs_1_.refs_7_
  58.2 12.0 %collective-permute-done.8.refs_2_.refs_8_ = bf16[256,1024]{1,0:T(8,128)(2,1)S(1)} collective-permute-done((bf16[256,1024]{1,0:T(8,128)(2,1)}, bf16[256,1024]{1,0:T(8,128)(2,1)S(1)}, u32[]{:S(2)}, u32[]{:S(2)}) %collective-permute-start.8) | collective-permute-done | bytes 524320 | tf_op jit(solution)/shard_map/ppermute | solution.py:248
  70.3 0.1 constant_dynamic-update-slice_fusion.1
  70.5 1.6 %collective-permute-start.17 = (bf16[256,2048]{1,0:T(8,128)(2,1)S(1)}, bf16[256,2048]{1,0:T(8,128)(2,1)S(1)}, u32[]{:S(2)}, u32[]{:S(2)}) collective-permute-start(bf16[256,2048]{1,0:T(8,128)(2,1)S(1)} %copy-done.3), channel_id=1, source_target_pairs={{0,8},{1,9},{2,10},{3,11},{4,12},{5,13},{6,14},{7,15},{8,0},{9,1},... | collective-permute-start | bytes 3145736 | tf_op jit(solution)/shard_map/ppermute | solution.py:248
  72.2 0.8 collective-permute-start.11
  73.0 0.9 collective-permute-start.13
  73.9 1.8 %collective-permute-start.15 = (bf16[256,1024]{1,0:T(8,128)(2,1)S(1)}, bf16[256,1024]{1,0:T(8,128)(2,1)S(1)}, u32[]{:S(2)}, u32[]{:S(2)}) collective-permute-start(bf16[256,1024]{1,0:T(8,128)(2,1)S(1)} %collective-permute-done.6.refs_0_.refs_6_), channel_id=1, source_target_pairs={{0,3},{1,2},{2,1},{3,0},{4,7},{5,6},{6,5},{7,4},{8,11},{9,10},{10,... | collective-permute-start | bytes 1572872 | tf_op jit(solution)/shard_map/ppermute | solution.py:248
  75.7 4.3 %grad_0.1 = (bf16[128,2048]{1,0:T(8,128)(2,1)}, bf16[128,256]{1,0:T(8,128)(2,1)S(1)}, bf16[128,256]{1,0:T(8,128)(2,1)S(1)}, bf16[128,256]{1,0:T(8,128)(2,1)S(1)}, bf16[128,256]{1,0:T(8,128)(2,1)S(1)}) custom-call(s32[7]{0:T(128)S(1)} %concatenate.36.refs_0_.meta, bf16[128,4096]{1,0:T(8,128)(2,1)S(1)} %bitcast.22, ...), custom_call_target="tpu_custom_call" | custom-call | flops 1073741824 | bytes 12582912 | tf_op jit(solution)/shard_map/grad_0/pallas_call | solution.py:345
  79.9 2.3 %project_0.1.refs_8_ = f32[128,4096]{1,0:T(8,128)S(1)} custom-call(s32[7]{0:T(128)S(1)} %concatenate.36.refs_0_.meta, bf16[128,2048]{1,0:T(8,128)(2,1)S(1)} %get-tuple-element.38.context_ref.refs_3_, bf16[256,4096]{1,0:T(8,128)(2,1)S(1)} %copy-done, bf16[256,4096]{1,0:T(8,128)(2,1)} %collective-permute-done.5.refs_1_.refs_7_), custom_call_target="tpu_custom_call" | custom-call | flops 536870912 | bytes 8388608 | tf_op jit(solution)/shard_map/project_0/pallas_call | solution.py:382
  82.3 1.9 %fusion.18 = (bf16[256,1024]{1,0:T(8,128)(2,1)S(1)}, bf16[256,1024]{1,0:T(8,128)(2,1)S(1)}, bf16[256,1024]{1,0:T(8,128)(2,1)S(1)}, bf16[256,1024]{1,0:T(8,128)(2,1)S(1)}, bf16[256,1024]{1,0:T(8,128)(2,1)S(1)}) fusion(bf16[256,7168]{1,0:T(8,128)(2,1)} %collective-permute-done.10), kind=kLoop, calls=%fused_computation.59 | loop fusion | bytes 5242880 | tf_op jit(solution)/shard_map/slice | solution.py:426
  84.2 1.8 %project_2.1.refs_4_ = f32[128,4096]{1,0:T(8,128)S(1)} custom-call(s32[7]{0:T(128)S(1)} %concatenate.36.refs_0_.meta, bf16[128,2048]{1,0:T(8,128)(2,1)S(1)} %get-tuple-element.38.context_ref.refs_3_, bf16[256,1024]{1,0:T(8,128)(2,1)} %collective-permute-done.4.refs_0_.refs_6_, bf16[256,1024]{1,0:T(8,128)(2,1)S(1)} %collective-permute-done.7.refs_1_.refs_7_, ...), custom_call_target="tpu_custom_call" | custom-call | flops 536870912 | bytes 8388608 | tf_op jit(solution)/shard_map/project_2/pallas_call | solution.py:382
  86.0 3.8 %grad_2.1 = (bf16[128,2048]{1,0:T(8,128)(2,1)}, bf16[128,256]{1,0:T(8,128)(2,1)S(1)}, bf16[128,256]{1,0:T(8,128)(2,1)S(1)}, bf16[128,256]{1,0:T(8,128)(2,1)S(1)}, bf16[128,256]{1,0:T(8,128)(2,1)S(1)}) custom-call(s32[7]{0:T(128)S(1)} %concatenate.36.refs_0_.meta, bf16[128,4096]{1,0:T(8,128)(2,1)S(1)} %bitcast.23, ...), custom_call_target="tpu_custom_call", output_to_operand_aliasing={{0}: (14, {})} | custom-call | flops 1073741824 | bytes 12582912 | tf_op jit(solution)/shard_map/grad_2/pallas_call | solution.py:345
  89.8 6.3 %collective-permute-done.17.refs_2_.refs_8_ = bf16[256,2048]{1,0:T(8,128)(2,1)S(1)} collective-permute-done((bf16[256,2048]{1,0:T(8,128)(2,1)S(1)}, bf16[256,2048]{1,0:T(8,128)(2,1)S(1)}, u32[]{:S(2)}, u32[]{:S(2)}) %collective-permute-start.17) | collective-permute-done | bytes 1048608 | tf_op jit(solution)/shard_map/ppermute | solution.py:248
  96.1 1.8 %collective-permute-done.13.refs_4_.refs_10_ = bf16[256,1024]{1,0:T(8,128)(2,1)S(1)} collective-permute-done((bf16[256,1024]{1,0:T(8,128)(2,1)S(1)}, bf16[256,1024]{1,0:T(8,128)(2,1)S(1)}, u32[]{:S(2)}, u32[]{:S(2)}) %collective-permute-start.13) | collective-permute-done | bytes 524320 | tf_op jit(solution)/shard_map/ppermute | solution.py:248
  97.9 0.5 collective-permute-start.12
  98.5 0.5 collective-permute-start.16
  99.0 1.3 %slice.175.refs_1_.refs_7_ = bf16[256,2048]{1,0:T(8,128)(2,1)S(1)} slice(bf16[256,7168]{1,0:T(8,128)(2,1)} %collective-permute-done.10), slice={[0:256], [4096:6144]} | slice | bytes 2097152 | tf_op jit(solution)/shard_map/slice | solution.py:439
  100.3 0.3 collective-permute-done.18.refs_3_.refs_9_
  100.6 3.3 %grad_1.1 = (bf16[128,2048]{1,0:T(8,128)(2,1)}, bf16[128,256]{1,0:T(8,128)(2,1)S(1)}, bf16[128,256]{1,0:T(8,128)(2,1)S(1)}, bf16[128,256]{1,0:T(8,128)(2,1)S(1)}, bf16[128,256]{1,0:T(8,128)(2,1)S(1)}) custom-call(s32[7]{0:T(128)S(1)} %concatenate.36.refs_0_.meta, bf16[128,4096]{1,0:T(8,128)(2,1)S(1)} %bitcast.24, ...), custom_call_target="tpu_custom_call", output_to_operand_aliasing={{0}: (10, {})} | custom-call | flops 1073741824 | bytes 12582912 | tf_op jit(solution)/shard_map/grad_1/pallas_call | solution.py:345
  103.9 1.2 %collective-permute-start.21 = (bf16[128,768]{1,0:T(8,128)(2,1)S(1)}, bf16[128,768]{1,0:T(8,128)(2,1)S(1)}, u32[]{:S(2)}, u32[]{:S(2)}) collective-permute-start(bf16[128,768]{1,0:T(8,128)(2,1)S(1)} %pad_maximum_fusion.9), channel_id=1, source_target_pairs={{0,3},{1,2},{2,1},{3,0},{4,7},{5,6},{6,5},{7,4},{8,11},{9,10},{10,... | collective-permute-start | bytes 589832 | tf_op jit(solution)/shard_map/ppermute | solution.py:248
  105.2 1.6 %collective-permute-start.20 = (bf16[128,768]{1,0:T(8,128)(2,1)S(1)}, bf16[128,768]{1,0:T(8,128)(2,1)S(1)}, u32[]{:S(2)}, u32[]{:S(2)}) collective-permute-start(bf16[128,768]{1,0:T(8,128)(2,1)S(1)} %pad_maximum_fusion.8), channel_id=1, source_target_pairs={{0,2},{1,3},{2,0},{3,1},{4,6},{5,7},{6,4},{7,5},{8,10},{9,11},{10,... | collective-permute-start | bytes 589832 | tf_op jit(solution)/shard_map/ppermute | solution.py:248
  106.7 0.9 collective-permute-start.19
  107.6 3.3 %grad_3.1 = (bf16[128,2048]{1,0:T(8,128)(2,1)}, bf16[128,256]{1,0:T(8,128)(2,1)S(1)}, bf16[128,256]{1,0:T(8,128)(2,1)S(1)}, bf16[128,256]{1,0:T(8,128)(2,1)S(1)}, bf16[128,256]{1,0:T(8,128)(2,1)S(1)}) custom-call(s32[7]{0:T(128)S(1)} %concatenate.36.refs_0_.meta, bf16[128,4096]{1,0:T(8,128)(2,1)S(1)} %bitcast.25, ...), custom_call_target="tpu_custom_call", output_to_operand_aliasing={{0}: (14, {})} | custom-call | flops 1073741824 | bytes 12582912 | tf_op jit(solution)/shard_map/grad_3/pallas_call | solution.py:345
  110.9 1.3 %collective-permute-start.22 = (bf16[128,256]{1,0:T(8,128)(2,1)S(1)}, bf16[128,256]{1,0:T(8,128)(2,1)S(1)}, u32[]{:S(2)}, u32[]{:S(2)}) collective-permute-start(bf16[128,256]{1,0:T(8,128)(2,1)S(1)} %get-tuple-element.64), channel_id=1, source_target_pairs={{0,1},{1,0},{2,3},{3,2},{4,5},{5,4},{6,7},{7,6},{8,9},{9,8},{10,11... | collective-permute-start | bytes 196616 | tf_op jit(solution)/shard_map/ppermute | solution.py:248
  112.2 0.5 collective-permute-start.23
  112.7 1.3 %project_1.1.refs_8_ = f32[128,4096]{1,0:T(8,128)S(1)} custom-call(s32[7]{0:T(128)S(1)} %concatenate.36.refs_0_.meta, bf16[128,2048]{1,0:T(8,128)(2,1)S(1)} %get-tuple-element.38.context_ref.refs_3_, bf16[256,2048]{1,0:T(8,128)(2,1)S(1)} %collective-permute-done.3.refs_0_.refs_6_, bf16[256,2048]{1,0:T(8,128)(2,1)S(1)} %slice.175.refs_1_.refs_7_, ...), custom_call_target="tpu_custom_call" | custom-call | flops 536870912 | bytes 8388608 | tf_op jit(solution)/shard_map/project_1/pallas_call | solution.py:382
  114.0 2.2 %project_3.1 = bf16[128,4096]{1,0:T(8,128)(2,1)} custom-call(s32[7]{0:T(128)S(1)} %concatenate.36.refs_0_.meta, bf16[128,2048]{1,0:T(8,128)(2,1)S(1)} %get-tuple-element.38.context_ref.refs_3_, bf16[256,1024]{1,0:T(8,128)(2,1)S(1)} %collective-permute-done.6.refs_0_.refs_6_, bf16[256,1024]{1,0:T(8,128)(2,1)S(1)} %get-tuple-element.73.refs_1_.refs_7_, ...), custom_call_target="tpu_custom_call" | custom-call | flops 536870912 | bytes 8388608 | tf_op jit(solution)/shard_map/project_3/pallas_call | solution.py:382
  116.2 1.8 %collective-permute-start.24 = (bf16[128,256]{1,0:T(8,128)(2,1)S(1)}, bf16[128,256]{1,0:T(8,128)(2,1)S(1)}, u32[]{:S(2)}, u32[]{:S(2)}) collective-permute-start(bf16[128,256]{1,0:T(8,128)(2,1)S(1)} %get-tuple-element.66), channel_id=1, source_target_pairs={{0,3},{1,2},{2,1},{3,0},{4,7},{5,6},{6,5},{7,4},{8,11},{9,10},{10,... | collective-permute-start | bytes 196616 | tf_op jit(solution)/shard_map/ppermute | solution.py:248
  118.1 3.3 %collective-permute-done.24.refs_15_ = bf16[128,256]{1,0:T(8,128)(2,1)S(1)} collective-permute-done((bf16[128,256]{1,0:T(8,128)(2,1)S(1)}, bf16[128,256]{1,0:T(8,128)(2,1)S(1)}, u32[]{:S(2)}, u32[]{:S(2)}) %collective-permute-start.24) | collective-permute-done | bytes 65568 | tf_op jit(solution)/shard_map/ppermute | solution.py:248
  121.4 1.4 %combine.1 = bf16[128,1024]{1,0:T(8,128)(2,1)} custom-call(s32[7]{0:T(128)S(1)} %concatenate.36.refs_0_.meta, bf16[128,256]{1,0:T(8,128)(2,1)S(1)} %get-tuple-element.52.refs_0_, bf16[128,256]{1,0:T(8,128)(2,1)S(1)} %get-tuple-element.102.refs_1_, bf16[128,256]{1,0:T(8,128)(2,1)S(1)} %get-tuple-element.99.refs_2_, ...), custom_call_target="tpu_custom_call" | custom-call | tf_op jit(solution)/shard_map/combine/pallas_call | solution.py:462
  (50 shorter events, 0.5 us)
Async XLA Ops:
  0.6 15.4 %copy-start = (bf16[256,4096]{1,0:T(8,128)(2,1)S(1)}, bf16[256,4096]{1,0:T(8,128)(2,1)}, u32[]{:S(2)}) copy-start(bf16[256,4096]{1,0:T(8,128)(2,1)} %refs_6_.1) | copy-start | bytes 6291460
  0.6 10.6 %copy-start.2 = (bf16[1,128,1024]{2,1,0:T(8,128)(2,1)S(1)}, bf16[1,128,1024]{2,1,0:T(8,128)(2,1)}, u32[]{:S(2)}) copy-start(bf16[1,128,1024]{2,1,0:T(8,128)(2,1)} %param.8) | copy-start | bytes 786436
  2.7 40.5 %collective-permute-start.4 = (bf16[256,1024]{1,0:T(8,128)(2,1)}, bf16[256,1024]{1,0:T(8,128)(2,1)}, u32[]{:S(2)}, u32[]{:S(2)}) collective-permute-start(bf16[256,1024]{1,0:T(8,128)(2,1)} %constant_dynamic-slice_fusion), channel_id=1, source_target_pairs={{0,16},{1,17},{2,18},{3,19},{4,20},{5,21},{6,22},{7,23},{8,24},{9,... | collective-permute-start | bytes 1572872 | tf_op jit(solution)/shard_map/ppermute | solution.py:248
  11.2 8.1 %copy-start.4 = (s32[1,16]{1,0:T(1,128)S(1)}, s32[1,16]{1,0:T(1,128)}, u32[]{:S(2)}) copy-start(s32[1,16]{1,0:T(1,128)} %param.11) | copy-start | bytes 196
  11.2 8.7 %copy-start.5 = (s32[1,4,4]{2,1,0:T(4,128)S(1)}, s32[1,4,4]{2,1,0:T(4,128)}, u32[]{:S(2)}) copy-start(s32[1,4,4]{2,1,0:T(4,128)} %param.12) | copy-start | bytes 196
  12.5 30.6 %collective-permute-start = (bf16[256,1024]{1,0:T(8,128)(2,1)}, bf16[256,1024]{1,0:T(8,128)(2,1)}, u32[]{:S(2)}, u32[]{:S(2)}) collective-permute-start(bf16[256,1024]{1,0:T(8,128)(2,1)} %get-tuple-element.85), channel_id=1, source_target_pairs={{0,3},{1,2},{2,1},{3,0},{4,7},{5,6},{6,5},{7,4},{8,11},{9,10},{10,... | collective-permute-start | bytes 1572872 | tf_op jit(solution)/shard_map/ppermute | solution.py:248
  15.0 28.1 %collective-permute-start.1 = (bf16[256,1024]{1,0:T(8,128)(2,1)}, bf16[256,1024]{1,0:T(8,128)(2,1)}, u32[]{:S(2)}, u32[]{:S(2)}) collective-permute-start(bf16[256,1024]{1,0:T(8,128)(2,1)} %get-tuple-element.86), channel_id=1, source_target_pairs={{0,2},{1,3},{2,0},{3,1},{4,6},{5,7},{6,4},{7,5},{8,10},{9,11},{10,... | collective-permute-start | bytes 1572872 | tf_op jit(solution)/shard_map/ppermute | solution.py:248
  15.5 23.0 %collective-permute-start.2 = (bf16[256,1024]{1,0:T(8,128)(2,1)}, bf16[256,1024]{1,0:T(8,128)(2,1)}, u32[]{:S(2)}, u32[]{:S(2)}) collective-permute-start(bf16[256,1024]{1,0:T(8,128)(2,1)} %get-tuple-element.87), channel_id=1, source_target_pairs={{0,1},{1,0},{2,3},{3,2},{4,5},{5,4},{6,7},{7,6},{8,9},{9,8},{10,11... | collective-permute-start | bytes 1572872 | tf_op jit(solution)/shard_map/ppermute | solution.py:248
  17.6 35.4 %collective-permute-start.3 = (bf16[256,2048]{1,0:T(8,128)(2,1)}, bf16[256,2048]{1,0:T(8,128)(2,1)S(1)}, u32[]{:S(2)}, u32[]{:S(2)}) collective-permute-start(bf16[256,2048]{1,0:T(8,128)(2,1)} %get-tuple-element.36), channel_id=1, source_target_pairs={{0,8},{1,9},{2,10},{3,11},{4,12},{5,13},{6,14},{7,15},{8,0},{9,1},... | collective-permute-start | bytes 3145736 | tf_op jit(solution)/shard_map/ppermute | solution.py:248
  38.5 17.5 %collective-permute-start.5 = (bf16[256,4096]{1,0:T(8,128)(2,1)S(1)}, bf16[256,4096]{1,0:T(8,128)(2,1)}, u32[]{:S(2)}, u32[]{:S(2)}) collective-permute-start(bf16[256,4096]{1,0:T(8,128)(2,1)S(1)} %copy-done), channel_id=1, source_target_pairs={{0,4},{1,5},{2,6},{3,7},{4,0},{5,1},{6,2},{7,3},{8,12},{9,13},{10,... | collective-permute-start | bytes 6291464 | tf_op jit(solution)/shard_map/ppermute | solution.py:248
  43.1 15.0 %collective-permute-start.7 = (bf16[256,1024]{1,0:T(8,128)(2,1)}, bf16[256,1024]{1,0:T(8,128)(2,1)S(1)}, u32[]{:S(2)}, u32[]{:S(2)}) collective-permute-start(bf16[256,1024]{1,0:T(8,128)(2,1)} %collective-permute-done.4.refs_0_.refs_6_), channel_id=1, source_target_pairs={{0,1},{1,0},{2,3},{3,2},{4,5},{5,4},{6,7},{7,6},{8,9},{9,8},{10,11... | collective-permute-start | bytes 1572872 | tf_op jit(solution)/shard_map/ppermute | solution.py:248
  44.7 25.5 %collective-permute-start.8 = (bf16[256,1024]{1,0:T(8,128)(2,1)}, bf16[256,1024]{1,0:T(8,128)(2,1)S(1)}, u32[]{:S(2)}, u32[]{:S(2)}) collective-permute-start(bf16[256,1024]{1,0:T(8,128)(2,1)} %collective-permute-done.4.refs_0_.refs_6_), channel_id=1, source_target_pairs={{0,2},{1,3},{2,0},{3,1},{4,6},{5,7},{6,4},{7,5},{8,10},{9,11},{10,... | collective-permute-start | bytes 1572872 | tf_op jit(solution)/shard_map/ppermute | solution.py:248
  45.2 25.0 %collective-permute-start.9 = (bf16[256,1024]{1,0:T(8,128)(2,1)}, bf16[256,1024]{1,0:T(8,128)(2,1)S(1)}, u32[]{:S(2)}, u32[]{:S(2)}) collective-permute-start(bf16[256,1024]{1,0:T(8,128)(2,1)} %collective-permute-done.4.refs_0_.refs_6_), channel_id=1, source_target_pairs={{0,3},{1,2},{2,1},{3,0},{4,7},{5,6},{6,5},{7,4},{8,11},{9,10},{10,... | collective-permute-start | bytes 1572872 | tf_op jit(solution)/shard_map/ppermute | solution.py:248
  55.9 14.6 %copy-start.3 = (bf16[256,2048]{1,0:T(8,128)(2,1)S(1)}, bf16[256,2048]{1,0:T(8,128)(2,1)}, u32[]{:S(2)}) copy-start(bf16[256,2048]{1,0:T(8,128)(2,1)} %get-tuple-element.43) | copy-start | bytes 3145732
  55.9 19.7 %copy-start.1 = (bf16[1,128,4096]{2,1,0:T(8,128)(2,1)S(1)}, bf16[1,128,4096]{2,1,0:T(8,128)(2,1)}, u32[]{:S(2)}) copy-start(bf16[1,128,4096]{2,1,0:T(8,128)(2,1)} %param.9) | copy-start | bytes 3145732
  56.0 14.4 %collective-permute-start.6 = (bf16[256,1024]{1,0:T(8,128)(2,1)}, bf16[256,1024]{1,0:T(8,128)(2,1)S(1)}, u32[]{:S(2)}, u32[]{:S(2)}) collective-permute-start(bf16[256,1024]{1,0:T(8,128)(2,1)} %collective-permute-done.4.refs_0_.refs_6_), channel_id=1, source_target_pairs={{0,8},{1,9},{2,10},{3,11},{4,12},{5,13},{6,14},{7,15},{8,0},{9,1},... | collective-permute-start | bytes 1572872 | tf_op jit(solution)/shard_map/ppermute | solution.py:248
  70.4 11.8 %collective-permute-start.10 = (bf16[256,7168]{1,0:T(8,128)(2,1)S(1)}, bf16[256,7168]{1,0:T(8,128)(2,1)}, u32[]{:S(2)}, u32[]{:S(2)}) collective-permute-start(bf16[256,7168]{1,0:T(8,128)(2,1)S(1)} %constant_dynamic-update-slice_fusion), channel_id=1, source_target_pairs={{0,4},{1,5},{2,6},{3,7},{4,0},{5,1},{6,2},{7,3},{8,12},{9,13},{10,... | collective-permute-start | bytes 11010056 | tf_op jit(solution)/shard_map/ppermute | solution.py:248
  70.5 25.6 %collective-permute-start.17 = (bf16[256,2048]{1,0:T(8,128)(2,1)S(1)}, bf16[256,2048]{1,0:T(8,128)(2,1)S(1)}, u32[]{:S(2)}, u32[]{:S(2)}) collective-permute-start(bf16[256,2048]{1,0:T(8,128)(2,1)S(1)} %copy-done.3), channel_id=1, source_target_pairs={{0,8},{1,9},{2,10},{3,11},{4,12},{5,13},{6,14},{7,15},{8,0},{9,1},... | collective-permute-start | bytes 3145736 | tf_op jit(solution)/shard_map/ppermute | solution.py:248
  72.2 23.9 %collective-permute-start.11 = (bf16[256,1024]{1,0:T(8,128)(2,1)S(1)}, bf16[256,1024]{1,0:T(8,128)(2,1)S(1)}, u32[]{:S(2)}, u32[]{:S(2)}) collective-permute-start(bf16[256,1024]{1,0:T(8,128)(2,1)S(1)} %collective-permute-done.6.refs_0_.refs_6_), channel_id=1, source_target_pairs={{0,1},{1,0},{2,3},{3,2},{4,5},{5,4},{6,7},{7,6},{8,9},{9,8},{10,11... | collective-permute-start | bytes 1572872 | tf_op jit(solution)/shard_map/ppermute | solution.py:248
  73.0 24.9 %collective-permute-start.13 = (bf16[256,1024]{1,0:T(8,128)(2,1)S(1)}, bf16[256,1024]{1,0:T(8,128)(2,1)S(1)}, u32[]{:S(2)}, u32[]{:S(2)}) collective-permute-start(bf16[256,1024]{1,0:T(8,128)(2,1)S(1)} %collective-permute-done.6.refs_0_.refs_6_), channel_id=1, source_target_pairs={{0,2},{1,3},{2,0},{3,1},{4,6},{5,7},{6,4},{7,5},{8,10},{9,11},{10,... | collective-permute-start | bytes 1572872 | tf_op jit(solution)/shard_map/ppermute | solution.py:248
  73.9 24.1 %collective-permute-start.15 = (bf16[256,1024]{1,0:T(8,128)(2,1)S(1)}, bf16[256,1024]{1,0:T(8,128)(2,1)S(1)}, u32[]{:S(2)}, u32[]{:S(2)}) collective-permute-start(bf16[256,1024]{1,0:T(8,128)(2,1)S(1)} %collective-permute-done.6.refs_0_.refs_6_), channel_id=1, source_target_pairs={{0,3},{1,2},{2,1},{3,0},{4,7},{5,6},{6,5},{7,4},{8,11},{9,10},{10,... | collective-permute-start | bytes 1572872 | tf_op jit(solution)/shard_map/ppermute | solution.py:248
  97.9 2.7 %collective-permute-start.18 = (bf16[256,2048]{1,0:T(8,128)(2,1)S(1)}, bf16[256,2048]{1,0:T(8,128)(2,1)S(1)}, u32[]{:S(2)}, u32[]{:S(2)}) collective-permute-start(bf16[256,2048]{1,0:T(8,128)(2,1)S(1)} %collective-permute-done.17.refs_2_.refs_8_), channel_id=1, source_target_pairs={{0,4},{1,5},{2,6},{3,7},{4,0},{5,1},{6,2},{7,3},{8,12},{9,13},{10,... | collective-permute-start | bytes 3145736 | tf_op jit(solution)/shard_map/ppermute | solution.py:248
  97.9 8.8 %collective-permute-start.12 = (bf16[256,1024]{1,0:T(8,128)(2,1)S(1)}, bf16[256,1024]{1,0:T(8,128)(2,1)S(1)}, u32[]{:S(2)}, u32[]{:S(2)}) collective-permute-start(bf16[256,1024]{1,0:T(8,128)(2,1)S(1)} %collective-permute-done.11.refs_2_.refs_8_), channel_id=1, source_target_pairs={{0,4},{1,5},{2,6},{3,7},{4,0},{5,1},{6,2},{7,3},{8,12},{9,13},{10,... | collective-permute-start | bytes 1572872 | tf_op jit(solution)/shard_map/ppermute | solution.py:248
  98.5 9.2 %collective-permute-start.14 = (bf16[256,1024]{1,0:T(8,128)(2,1)S(1)}, bf16[256,1024]{1,0:T(8,128)(2,1)S(1)}, u32[]{:S(2)}, u32[]{:S(2)}) collective-permute-start(bf16[256,1024]{1,0:T(8,128)(2,1)S(1)} %collective-permute-done.13.refs_4_.refs_10_), channel_id=1, source_target_pairs={{0,4},{1,5},{2,6},{3,7},{4,0},{5,1},{6,2},{7,3},{8,12},{9,13},{10,... | collective-permute-start | bytes 1572872 | tf_op jit(solution)/shard_map/ppermute | solution.py:248
  98.5 9.2 %collective-permute-start.16 = (bf16[256,1024]{1,0:T(8,128)(2,1)S(1)}, bf16[256,1024]{1,0:T(8,128)(2,1)S(1)}, u32[]{:S(2)}, u32[]{:S(2)}) collective-permute-start(bf16[256,1024]{1,0:T(8,128)(2,1)S(1)} %collective-permute-done.15.refs_6_.refs_12_), channel_id=1, source_target_pairs={{0,4},{1,5},{2,6},{3,7},{4,0},{5,1},{6,2},{7,3},{8,12},{9,13},{10,... | collective-permute-start | bytes 1572872 | tf_op jit(solution)/shard_map/ppermute | solution.py:248
  103.9 12.3 %collective-permute-start.21 = (bf16[128,768]{1,0:T(8,128)(2,1)S(1)}, bf16[128,768]{1,0:T(8,128)(2,1)S(1)}, u32[]{:S(2)}, u32[]{:S(2)}) collective-permute-start(bf16[128,768]{1,0:T(8,128)(2,1)S(1)} %pad_maximum_fusion.9), channel_id=1, source_target_pairs={{0,3},{1,2},{2,1},{3,0},{4,7},{5,6},{6,5},{7,4},{8,11},{9,10},{10,... | collective-permute-start | bytes 589832 | tf_op jit(solution)/shard_map/ppermute | solution.py:248
  105.2 12.8 %collective-permute-start.20 = (bf16[128,768]{1,0:T(8,128)(2,1)S(1)}, bf16[128,768]{1,0:T(8,128)(2,1)S(1)}, u32[]{:S(2)}, u32[]{:S(2)}) collective-permute-start(bf16[128,768]{1,0:T(8,128)(2,1)S(1)} %pad_maximum_fusion.8), channel_id=1, source_target_pairs={{0,2},{1,3},{2,0},{3,1},{4,6},{5,7},{6,4},{7,5},{8,10},{9,11},{10,... | collective-permute-start | bytes 589832 | tf_op jit(solution)/shard_map/ppermute | solution.py:248
  106.7 11.3 %collective-permute-start.19 = (bf16[128,768]{1,0:T(8,128)(2,1)S(1)}, bf16[128,768]{1,0:T(8,128)(2,1)S(1)}, u32[]{:S(2)}, u32[]{:S(2)}) collective-permute-start(bf16[128,768]{1,0:T(8,128)(2,1)S(1)} %pad_maximum_fusion.7), channel_id=1, source_target_pairs={{0,1},{1,0},{2,3},{3,2},{4,5},{5,4},{6,7},{7,6},{8,9},{9,8},{10,11... | collective-permute-start | bytes 589832 | tf_op jit(solution)/shard_map/ppermute | solution.py:248
  110.9 7.2 %collective-permute-start.22 = (bf16[128,256]{1,0:T(8,128)(2,1)S(1)}, bf16[128,256]{1,0:T(8,128)(2,1)S(1)}, u32[]{:S(2)}, u32[]{:S(2)}) collective-permute-start(bf16[128,256]{1,0:T(8,128)(2,1)S(1)} %get-tuple-element.64), channel_id=1, source_target_pairs={{0,1},{1,0},{2,3},{3,2},{4,5},{5,4},{6,7},{7,6},{8,9},{9,8},{10,11... | collective-permute-start | bytes 196616 | tf_op jit(solution)/shard_map/ppermute | solution.py:248
  112.2 5.9 %collective-permute-start.23 = (bf16[128,256]{1,0:T(8,128)(2,1)S(1)}, bf16[128,256]{1,0:T(8,128)(2,1)S(1)}, u32[]{:S(2)}, u32[]{:S(2)}) collective-permute-start(bf16[128,256]{1,0:T(8,128)(2,1)S(1)} %get-tuple-element.65), channel_id=1, source_target_pairs={{0,2},{1,3},{2,0},{3,1},{4,6},{5,7},{6,4},{7,5},{8,10},{9,11},{10,... | collective-permute-start | bytes 196616 | tf_op jit(solution)/shard_map/ppermute | solution.py:248
  116.2 5.2 %collective-permute-start.24 = (bf16[128,256]{1,0:T(8,128)(2,1)S(1)}, bf16[128,256]{1,0:T(8,128)(2,1)S(1)}, u32[]{:S(2)}, u32[]{:S(2)}) collective-permute-start(bf16[128,256]{1,0:T(8,128)(2,1)S(1)} %get-tuple-element.66), channel_id=1, source_target_pairs={{0,3},{1,2},{2,1},{3,0},{4,7},{5,6},{6,5},{7,4},{8,11},{9,10},{10,... | collective-permute-start | bytes 196616 | tf_op jit(solution)/shard_map/ppermute | solution.py:248

commit v3 on v2

--- a/solution.py
+++ b/solution.py
@@ -20,7 +20,7 @@
 BF16 = jnp.bfloat16
 NT_DIMS = (((1,), (1,)), ((), ()))
 TN_DIMS = (((0,), (0,)), ((), ()))
-VMEM_BYTES = 40 * 1024 * 1024
+MIB = 1024 * 1024
 
 
 def whole():
@@ -59,23 +59,83 @@
     )
 
 
-def forward_kernel(groups, units, rows, width, per_shard, *refs):
-    meta, q_ref, allowed_ref = refs[:3]
-    kv_parts = refs[3 : 3 + groups]
-    context_ref, probs_ref, windows_ref = refs[3 + groups : 6 + groups]
-    kv_ref, sems = refs[6 + groups :]
+def column_kernel(wide, meta, block_ref, out_ref, sem):
+    start = pl.multiple_of(meta[0] * wide, wide)
+    copy = pltpu.make_async_copy(block_ref.at[:, pl.ds(start, wide)], out_ref, sem)
+    copy.start()
+    copy.wait()
+
+
+def pack_kernel(groups, units, rows, fold, meta, q_ref, kv_ref, *refs):
+    outs, sems = refs[:-1], refs[-1]
+    per_shard, wide = kv_ref.shape
     me = meta[0]
     copies = []
-    for t in range(groups):
-        start = pl.multiple_of(jnp.bitwise_xor(me, t) * per_shard, per_shard)
-        copies.append(
-            pltpu.make_async_copy(
-                kv_parts[t].at[pl.ds(0, per_shard)], kv_ref.at[pl.ds(start, per_shard)], sems.at[t])
-        )
+    for t in range(1, groups):
+        chosen = 0
+        for j in range(units):
+            dest = lax.rem(me + meta[3 + j], groups)
+            chosen = chosen + jnp.where(dest == jnp.bitwise_xor(me, t), j, 0)
+        start = pl.multiple_of(chosen * rows, rows)
+        copies.append((kv_ref, outs[t - 1].at[pl.ds(0, per_shard)]))
+        for f in range(fold):
+            copies.append(
+                (
+                    q_ref.at[pl.ds(start, rows), pl.ds(f * wide, wide)],
+                    outs[t - 1].at[pl.ds(per_shard + f * rows, rows)],
+                )
+            )
+    copies = [
+        pltpu.make_async_copy(source, target, sems.at[i])
+        for i, (source, target) in enumerate(copies)
+    ]
     for copy in copies:
         copy.start()
     for copy in copies:
         copy.wait()
+
+
+def forward_kernel(groups, units, rows, width, per_shard, fold, *refs):
+    meta, allowed_ref, own_q = refs[:3]
+    kv_parts = refs[3 : 3 + groups]
+    context_ref, probs_ref, windows_ref, q_ref = refs[3 + groups : 7 + groups]
+    kv_ref, kv_sems, q_sems = refs[7 + groups :]
+    me = meta[0]
+    wide = kv_ref.shape[1]
+    for t in range(groups):
+        start = pl.multiple_of(jnp.bitwise_xor(me, t) * per_shard, per_shard)
+        pltpu.make_async_copy(
+            kv_parts[t].at[pl.ds(0, per_shard)], kv_ref.at[pl.ds(start, per_shard)], kv_sems.at[t]
+        ).start()
+    for u in range(units):
+        source = lax.rem(me - meta[3 + u] + groups, groups)
+        for t in range(groups):
+
+            @pl.when(source == jnp.bitwise_xor(me, t))
+            def _():
+                for f in range(fold):
+                    if t == 0:
+                        part = own_q.at[pl.ds(u * rows, rows), pl.ds(f * wide, wide)]
+                    else:
+                        part = kv_parts[t].at[pl.ds(per_shard + f * rows, rows)]
+                    pltpu.make_async_copy(
+                        part,
+                        q_ref.at[pl.ds(u * rows, rows), pl.ds(f * wide, wide)],
+                        q_sems.at[u, f],
+                    ).start()
+
+    for t in range(groups):
+        start = pl.multiple_of(jnp.bitwise_xor(me, t) * per_shard, per_shard)
+        pltpu.make_async_copy(
+            kv_parts[t].at[pl.ds(0, per_shard)], kv_ref.at[pl.ds(start, per_shard)], kv_sems.at[t]
+        ).wait()
+    for u in range(units):
+        for f in range(fold):
+            pltpu.make_async_copy(
+                own_q.at[pl.ds(u * rows, rows), pl.ds(f * wide, wide)],
+                q_ref.at[pl.ds(u * rows, rows), pl.ds(f * wide, wide)],
+                q_sems.at[u, f],
+            ).wait()
     for u in range(units):
         start = pl.multiple_of(meta[3 + units + u], rows)
         window = kv_ref[pl.ds(start, width), :]
@@ -105,23 +165,26 @@
     return jnp.bitwise_xor(meta[1], slot) if swapped else slot
 
 
-def grad_kernel(groups, units, rows, width, per_shard, slot, swapped, plan, with_q, *refs):
+def grad_kernel(groups, units, rows, width, per_shard, slot, swapped, plan, with_q, stack, *refs):
     meta, grad_ref, q_ref, context_ref, probs_ref, windows_ref = refs[:6]
-    parts = refs[6 : 6 + len(plan)]
-    rest = refs[6 + len(plan) :]
+    count = 1 + max(entry[0] for entry in plan)
+    parts = refs[6 : 6 + count]
+    rest = refs[6 + count :]
     if with_q:
         rest = rest[1:]
     q_grad_ref = rest[0]
-    outs = rest[1 : 1 + groups]
-    grad_context_ref, q_block, terms, sem = rest[1 + groups :]
+    outs = rest[1:-4]
+    grad_context_ref, q_block, terms, sem = rest[-4:]
     g = group_of(meta, slot, swapped)
     depth = parts[0].shape[0]
     sums = {}
-    for part, (row_key, row_fn, col_fn) in zip(parts, plan):
-        wide = part.shape[1]
+    for index, offset, wide, row_key, row_fn, col_fn in plan:
         start = pl.multiple_of(col_fn(meta) * wide, wide)
         term = lax.dot_general(
-            grad_ref[:, pl.ds(start, wide)], part[...], NT_DIMS, preferred_element_type=F32
+            grad_ref[:, pl.ds(start, wide)],
+            parts[index][:, offset : offset + wide],
+            NT_DIMS,
+            preferred_element_type=F32,
         )
         sums[row_key] = (sums[row_key][0] + term if row_key in sums else term, row_fn)
     for total, row_fn in sums.values():
@@ -165,20 +228,29 @@
         for u in range(units):
             shard = lax.rem(owner - meta[3 + u] + groups, groups)
             start = pl.multiple_of(shard * per_shard + u * rows, rows)
-            outs[t][u * rows : (u + 1) * rows, :] = terms[pl.ds(start, rows), :].astype(BF16)
+            share = terms[pl.ds(start, rows), :].astype(BF16)
+            if stack:
+                outs[0][owner, u * rows : (u + 1) * rows, :] = share
+            else:
+                outs[t][u * rows : (u + 1) * rows, :] = share
     copy.wait()
 
 
 def project_kernel(slot, swapped, plan, first, meta, context_ref, *refs):
-    parts = refs[: len(plan)]
+    count = 1 + max(entry[0] for entry in plan)
+    parts = refs[:count]
     out_ref = refs[-1]
-    total_ref = None if first else refs[len(plan)]
+    total_ref = None if first else refs[count]
     g = group_of(meta, slot, swapped)
     by_columns = {}
-    for part, (row_key, row_fn, col_fn) in zip(parts, plan):
-        depth, wide = part.shape
+    for index, offset, wide, row_key, row_fn, col_fn in plan:
+        depth = parts[index].shape[0]
         start = pl.multiple_of(g * GROUP_WIDTH + row_fn(meta) * depth, depth)
-        term = jnp.dot(context_ref[:, pl.ds(start, depth)], part[...], preferred_element_type=F32)
+        term = jnp.dot(
+            context_ref[:, pl.ds(start, depth)],
+            parts[index][:, offset : offset + wide],
+            preferred_element_type=F32,
+        )
         key = (id(col_fn), wide)
         if key in by_columns:
             by_columns[key] = (by_columns[key][0] + term, col_fn, wide)
@@ -191,21 +263,32 @@
         out_ref[:, span] = term.astype(out_ref.dtype)
 
 
-def combine_kernel(groups, order, swapped, meta, *refs):
-    out_ref = refs[-1]
+def combine_kernel(groups, order, swapped, with_out, meta, *refs):
+    parts = refs[:groups]
+    out_ref, sums, sems = refs[groups + with_out :]
+    blocks = [part[...] for part in parts]
+    if groups == 1:
+        blocks = [parts[0][i] for i in range(parts[0].shape[0])]
+    total = blocks[0].astype(F32)
+    for block in blocks[1:]:
+        total = total + block.astype(F32)
+    sums[...] = total.astype(BF16)
+    copies = []
     for index, slot in enumerate(order):
         g = group_of(meta, slot, swapped)
-        parts = refs[index * groups : (index + 1) * groups]
-        total = parts[0][...].astype(F32)
-        for part in parts[1:]:
-            total = total + part[...].astype(F32)
-        total = total.astype(BF16)
-        out_ref[:, pl.ds(pl.multiple_of(g * HEAD_WIDTH, HEAD_WIDTH), HEAD_WIDTH)] = total[
-            :, :HEAD_WIDTH
-        ]
-        out_ref[
-            :, pl.ds(pl.multiple_of(KEY_WIDTH + g * HEAD_WIDTH, HEAD_WIDTH), HEAD_WIDTH)
-        ] = total[:, HEAD_WIDTH:]
+        for k in range(2):
+            start = pl.multiple_of(k * KEY_WIDTH + g * HEAD_WIDTH, HEAD_WIDTH)
+            copies.append(
+                pltpu.make_async_copy(
+                    sums.at[:, pl.ds((2 * index + k) * HEAD_WIDTH, HEAD_WIDTH)],
+                    out_ref.at[:, pl.ds(start, HEAD_WIDTH)],
+                    sems.at[2 * index + k],
+                )
+            )
+    for copy in copies:
+        copy.start()
+    for copy in copies:
+        copy.wait()
 
 
 def zero_of(meta):
@@ -260,44 +343,41 @@
         return lax.optimization_barrier((block,) + others)[0]
 
     swapped = (batches // 2) * GROUP_WIDTH == QUERY_HEADS * HEAD_WIDTH and groups == 4
+    dests_meta = jnp.concatenate([jnp.stack([me, row // 2, lax.rem(row, 2)]), offsets])
+    head_width = QUERY_HEADS * HEAD_WIDTH
+    fold = head_width // (2 * KEY_WIDTH)
+    sources = lax.rem(me - offsets + groups, groups)
     source = queries[0]
     if swapped:
         quarter = model // groups
-        far = lax.dynamic_slice_in_dim(out_proj, me * quarter, quarter, 1)
+        half = model // 2
+        far = pl.pallas_call(
+            functools.partial(column_kernel, quarter),
+            out_shape=jax.ShapeDtypeStruct((out_proj.shape[0], quarter), BF16),
+            in_specs=[in_smem(), anywhere()],
+            out_specs=whole(),
+            scratch_shapes=[pltpu.SemaphoreType.DMA],
+            name="far",
+        )(me[None], out_proj)
         two = to_chip(far, 2)
         source = after(source, far)
-
-    q_units = source.reshape(unit_count, rows, QUERY_HEADS * HEAD_WIDTH)
-    dests = lax.rem(me + offsets, groups)
-    sources = lax.rem(me - offsets + groups, groups)
-    my_units = [q_units[j] for j in range(unit_count)]
-    kv_parts = [keys_values[0]]
-    kv_rows = keys_values.shape[1]
-    for t in range(1, groups):
-        chosen = q_units[0]
-        for j in range(1, unit_count):
-            chosen = jnp.where(dests[j] == (me ^ t), q_units[j], chosen)
-        fold = QUERY_HEADS * HEAD_WIDTH // (2 * KEY_WIDTH)
-        chosen = jnp.concatenate(
-            [chosen[:, f * 2 * KEY_WIDTH : (f + 1) * 2 * KEY_WIDTH] for f in range(fold)], axis=0
-        )
-        sent = jnp.concatenate([keys_values[0], chosen], axis=0)
-        if t == 1:
-            first_sent = sent
-        got = to_ctx(sent, t)
-        kv_parts.append(got)
-        got = jnp.concatenate(
-            [got[kv_rows + f * rows : kv_rows + (f + 1) * rows] for f in range(fold)], axis=1
-        )
-        my_units = [
-            jnp.where(sources[j] == (me ^ t), got, my_units[j]) for j in range(unit_count)
-        ]
-    my_queries = jnp.concatenate(my_units, axis=0)
+    sent = pl.pallas_call(
+        functools.partial(pack_kernel, groups, unit_count, rows, fold),
+        out_shape=tuple(
+            jax.ShapeDtypeStruct((per_shard + fold * rows, 2 * KEY_WIDTH), BF16)
+            for _ in range(1, groups)
+        ),
+        in_specs=[in_smem(), anywhere(), anywhere()],
+        out_specs=(whole(),) * (groups - 1),
+        scratch_shapes=[pltpu.SemaphoreType.DMA(((groups - 1) * (1 + fold),))],
+        name="pack",
+    )(dests_meta, source, keys_values[0])
+    sent = list(sent)
     if swapped:
-        half = model // 2
-        one_a = to_chip(after(out_proj[:, :half], first_sent), 1)
-        own_other = to_core(after(out_proj, kv_parts[1]))
-        my_queries = after(my_queries, one_a)
+        own_other = to_core(out_proj)
+        one_a = to_chip(after(out_proj[:, :half], own_other), 1)
+        sent[-1] = after(sent[-1], own_other)
+    kv_parts = [keys_values[0]] + [to_ctx(sent[t - 1], t) for t in range(1, groups)]
 
     unit_ids = jnp.arange(unit_count, dtype=jnp.int32)
     first_pos = sources * per_shard + unit_ids * rows
@@ -305,25 +385,27 @@
     win_start = jnp.clip(first_pos - longest, 0, total_rows - width)
     key_pos = win_start[:, None] + jnp.arange(width, dtype=jnp.int32)[None, :]
     allowed = window_mask(query_pos, key_pos, lengths, tiles).astype(F32)
-    meta = jnp.concatenate(
-        [jnp.stack([me, row // 2, lax.rem(row, 2)]), offsets, win_start]
-    ).astype(jnp.int32)
-
-    params = pltpu.CompilerParams(vmem_limit_bytes=VMEM_BYTES)
+    meta = jnp.concatenate([dests_meta, win_start]).astype(jnp.int32)
+    if swapped:
+        allowed = after(allowed, one_a)
+
+    params = pltpu.CompilerParams(vmem_limit_bytes=(16 if swapped else 40) * MIB)
     sizes = (groups, unit_count, rows, width, per_shard)
     stacked = RATIO * rows
-    context, probs, windows = pl.pallas_call(
-        functools.partial(forward_kernel, *sizes),
+    context, probs, windows, my_queries = pl.pallas_call(
+        functools.partial(forward_kernel, *sizes, fold),
         out_shape=(
             jax.ShapeDtypeStruct((per_shard, QUERY_HEADS * HEAD_WIDTH), BF16),
             jax.ShapeDtypeStruct((KEY_VALUE_HEADS, unit_count, stacked, width), F32),
             jax.ShapeDtypeStruct((unit_count, width, 2 * KEY_WIDTH), BF16),
+            jax.ShapeDtypeStruct((per_shard, head_width), BF16),
         ),
-        in_specs=[in_smem(), whole(), whole()] + [anywhere()] * groups,
-        out_specs=(whole(), whole(), whole()),
+        in_specs=[in_smem(), whole(), anywhere()] + [anywhere()] * groups,
+        out_specs=(whole(),) * 4,
         scratch_shapes=[
             pltpu.VMEM((total_rows, 2 * KEY_WIDTH), BF16),
             pltpu.SemaphoreType.DMA((groups,)),
+            pltpu.SemaphoreType.DMA((unit_count, fold)),
         ],
         compiler_params=params,
         cost_estimate=pl.CostEstimate(
@@ -332,26 +414,36 @@
             transcendentals=unit_count * QUERY_HEADS * rows * width,
         ),
         name="forward",
-    )(meta, my_queries, allowed, *kv_parts)
+    )(meta, allowed, queries[0], *kv_parts)
 
     q_grad = None
     total = None
 
-    def grad_step(slot, parts, q_grad):
-        arrays = [part for part, _ in parts]
-        plan = [entry for _, entry in parts]
+    def arrange(parts):
+        arrays, plan = [], []
+        for block, offset, wide, *entry in parts:
+            found = [i for i, array in enumerate(arrays) if array is block]
+            if not found:
+                arrays.append(block)
+            plan.append((found[0] if found else len(arrays) - 1, offset, wide, *entry))
+        return arrays, plan
+
+    def grad_step(slot, parts, q_grad, stack=False):
+        arrays, plan = arrange(parts)
         depth = arrays[0].shape[0]
         with_q = q_grad is not None
         results = pl.pallas_call(
-            functools.partial(grad_kernel, *sizes, slot, swapped, plan, with_q),
+            functools.partial(grad_kernel, *sizes, slot, swapped, plan, with_q, stack),
             out_shape=(jax.ShapeDtypeStruct((per_shard, QUERY_HEADS * HEAD_WIDTH), BF16),)
-            + tuple(
-                jax.ShapeDtypeStruct((per_shard, 2 * HEAD_WIDTH), BF16) for _ in range(groups)
+            + (
+                (jax.ShapeDtypeStruct((groups, per_shard, 2 * HEAD_WIDTH), BF16),)
+                if stack
+                else (jax.ShapeDtypeStruct((per_shard, 2 * HEAD_WIDTH), BF16),) * groups
             ),
             in_specs=[in_smem()]
             + [whole()] * (5 + len(arrays))
             + ([anywhere()] if with_q else []),
-            out_specs=(anywhere(),) + (whole(),) * groups,
+            out_specs=(anywhere(),) + (whole(),) * (1 if stack else groups),
             scratch_shapes=[
                 pltpu.VMEM((GROUP_WIDTH // depth, per_shard, depth), BF16),
                 pltpu.VMEM((per_shard, GROUP_WIDTH), BF16),
@@ -376,8 +468,7 @@
         return [mine[0]] + [to_ctx(mine[t], t) for t in range(1, groups)]
 
     def project_step(slot, parts, total, last):
-        arrays = [part for part, _ in parts]
-        plan = [entry for _, entry in parts]
+        arrays, plan = arrange(parts)
         first = total is None
         return pl.pallas_call(
             functools.partial(project_kernel, slot, swapped, plan, first),
@@ -393,7 +484,6 @@
             name=f"project_{slot}",
         )(meta, context, *arrays, *([] if first else [total]))
 
-    shares = {}
     count = KEY_VALUE_HEADS
     if swapped:
         order = (0, 2, 1, 3)
@@ -402,71 +492,74 @@
             for t in range(groups)
         ]
 
-        def pair(block, column):
-            return [
-                (block, ("own", same_core, column)),
-                (to_core(block), ("other", other_core, column)),
-            ]
-
-        parts_0 = [
-            (out_proj, ("own", same_core, zero_of)),
-            (own_other, ("other", other_core, zero_of)),
-        ]
-        three = to_chip(after(two, one_a, context, own_other), 1)
+        def own(block, column, offset=0, wide=None):
+            return (block, offset, wide or block.shape[1], "own", same_core, column)
+
+        def other(block, column, offset=0, wide=None):
+            return (block, offset, wide or block.shape[1], "other", other_core, column)
+
+        three = to_chip(two, 1)
+        parts_0 = [own(out_proj, zero_of), other(own_other, zero_of)]
         q_grad, mine_0 = grad_step(0, parts_0, None)
         total = project_step(0, parts_0, None, False)
         twos = [two] + [to_ctx(after(two, *kv_parts[1:]), t) for t in range(1, groups)]
-        one_b = to_chip(after(out_proj[:, half:], one_a, context), 1)
-        middle = to_core(jnp.concatenate(twos + [one_a, three], axis=1))
-        parts_2 = []
-        for t in range(groups):
-            parts_2.append((twos[t], ("own", same_core, columns[t])))
-        for t in range(groups):
-            parts_2.append(
-                (middle[:, t * quarter : (t + 1) * quarter], ("other", other_core, columns[t]))
-            )
+        one_b = to_chip(after(out_proj[:, half:], one_a), 1)
+        middle = to_core(jnp.concatenate([one_a, three] + twos[:3] + [after(twos[3], total, mine_0[0])], axis=1))
+        parts_2 = [own(twos[t], columns[t]) for t in range(groups)]
+        parts_2 += [other(middle, columns[t], half + quarter + t * quarter, quarter) for t in range(groups)]
         threes = [three] + [to_ctx(after(three, *twos[1:]), t) for t in range(1, groups)]
+        q_grad, mine_2 = grad_step(2, parts_2, q_grad)
+        total = project_step(2, parts_2, total, False)
+        one_b_other = to_core(after(one_b, total, mine_2[0], *threes[1:]))
+        parts_1 = [
+            own(one_a, zero_of),
+            other(middle, zero_of, 0, half),
+            own(one_b, one_of),
+            other(one_b_other, one_of),
+        ]
         parts_3 = [
-            (three, ("own", same_core, columns[0])),
-            (middle[:, model + half :], ("other", other_core, columns[0])),
+            own(three, columns[0]),
+            other(middle, columns[0], half, quarter),
         ]
         for t in range(1, groups):
-            parts_3 += pair(threes[t], columns[t])
-        q_grad, mine_2 = grad_step(2, parts_2, q_grad)
-        total = project_step(2, parts_2, total, False)
-        parts_1 = [
-            (one_a, ("own", same_core, zero_of)),
-            (middle[:, model : model + half], ("other", other_core, zero_of)),
-        ]
-        parts_1 += pair(after(one_b, total, mine_2[0], *threes[1:]), one_of)
+            parts_3 += [own(threes[t], columns[t]), other(to_core(threes[t]), columns[t])]
         q_grad, mine_1 = grad_step(1, parts_1, q_grad)
+        q_grad, mine_3 = grad_step(3, parts_3, q_grad)
+        late = send_shares(
+            [
+                jnp.concatenate([mine_0[t], mine_2[t], mine_1[t], mine_3[t]], axis=1)
+                for t in range(groups)
+            ]
+        )
         total = project_step(1, parts_1, total, False)
-        merged = [
-            jnp.concatenate([mine_0[t], mine_2[t], mine_1[t]], axis=1) for t in range(groups)
-        ]
-        early = send_shares(merged)
-        for index, slot in enumerate((0, 2, 1)):
-            span = slice(index * 2 * HEAD_WIDTH, (index + 1) * 2 * HEAD_WIDTH)
-            shares[slot] = [part[:, span] for part in early]
-        q_grad, mine_3 = grad_step(3, parts_3, q_grad)
-        shares[3] = send_shares(mine_3)
         total = project_step(3, parts_3, total, True)
+        batches_of_shares = [((0, 2, 1, 3), late)]
     else:
         full = lax.all_gather(out_proj, "dp", axis=0, tiled=True)
+        batches_of_shares = []
         for g in range(count):
-            parts = [(full[g * GROUP_WIDTH : (g + 1) * GROUP_WIDTH], ("own", zero_of, zero_of))]
+            part = full[g * GROUP_WIDTH : (g + 1) * GROUP_WIDTH]
+            parts = [(part, 0, model, "own", zero_of, zero_of)]
             q_grad, mine = grad_step(g, parts, q_grad)
-            shares[g] = send_shares(mine)
+            batches_of_shares.append(((g,), send_shares(mine)))
             total = project_step(g, parts, total, g == count - 1)
 
-    kv_grad = pl.pallas_call(
-        functools.partial(combine_kernel, groups, list(range(count)), swapped),
-        out_shape=jax.ShapeDtypeStruct((per_shard, 2 * KEY_WIDTH), BF16),
-        in_specs=[in_smem()] + [whole()] * (groups * count),
-        out_specs=whole(),
-        compiler_params=params,
-        name="combine",
-    )(meta, *[part for slot in range(count) for part in shares[slot]])
+    kv_grad = None
+    for order, share in batches_of_shares:
+        with_out = kv_grad is not None
+        kv_grad = pl.pallas_call(
+            functools.partial(combine_kernel, len(share), order, swapped, int(with_out)),
+            out_shape=jax.ShapeDtypeStruct((per_shard, 2 * KEY_WIDTH), BF16),
+            in_specs=[in_smem()] + [whole()] * len(share) + [anywhere()] * int(with_out),
+            out_specs=anywhere(),
+            scratch_shapes=[
+                pltpu.VMEM((per_shard, 2 * HEAD_WIDTH * len(order)), BF16),
+                pltpu.SemaphoreType.DMA((2 * len(order),)),
+            ],
+            input_output_aliases={1 + len(share): 0} if with_out else {},
+            compiler_params=params,
+            name=f"combine_{order[0]}",
+        )(meta, *share, *([kv_grad] if with_out else []))
     return (total[None], q_grad[None], kv_grad[None])
 
 

time: 123 us -> 119 us (0.967)
  waiting for transfers between devices: 42.5 us -> 54.6 us
  local copies, waits for them, and re-layouts: 13.7 us -> 6.31 us
  Pallas kernels: 26.4 us -> 33.4 us
  between operations: 6.92 us -> 0.95 us
  starting transfers between devices: 27.8 us -> 21.9 us
  other arithmetic: 5.09 us -> 1.05 us
    ppermute x25 -> x22, waiting for transfers between devices: 42.5 us -> 54.6 us  [move(): return lax.ppermute(block, ('dp', 'ctx'), pairs)]
    slice x13 -> x1, local copies, waits for them, and re-layouts: 9.08 us -> 1.59 us  [on_device(): one_b = to_chip(after(out_proj[:, half:], one_a), 1)]
    ppermute x25 -> x22, starting transfers between devices: 27.8 us -> 21.9 us  [move(): return lax.ppermute(block, ('dp', 'ctx'), pairs)]
    pallas_call x2 -> x4, Pallas kernels: 4.28 us -> 10.1 us  [the longest x1 3.66 us: on_device(): pl.pallas_call(functools.partial(pack_kernel, groups, unit_count, rows, f...]
    select_n x3 -> x0, other arithmetic: 3.32 us -> none  [the longest x2 2.23 us: on_device(): jnp.where(sources[j] == me ^ t, got, my_units[j])]
    unnamed x17 -> x19, local copies, waits for them, and re-layouts: 1.3 us -> 3.46 us
    dynamic_slice x1 -> x0, local copies, waits for them, and re-layouts: 2.03 us -> none  [on_device(): far = lax.dynamic_slice_in_dim(out_proj, me * quarter, quarter, 1)]
  transfers between devices with their start and end apart: 25 -> 22, of which waited for: 7 -> 9; matrix products, arithmetic and copies ran while one was open for 14% -> 6% of each run, Pallas kernels for 20% -> 24%
where the time goes in v3:
time: 119 us
  waiting for transfers between devices  54.6 us (46%)
  Pallas kernels  33.4 us (28%)
  starting transfers between devices  21.9 us (18%)
  local copies, waits for them, and re-layouts  6.31 us (5%)
    ppermute x22, waiting for transfers between devices, move(): return lax.ppermute(block, ('dp', 'ctx'), pairs)  54.6 us
    ppermute x22, starting transfers between devices, move(): return lax.ppermute(block, ('dp', 'ctx'), pairs)  21.9 us
    pallas_call x4, Pallas kernels, grad_step(): pl.pallas_call(functools.partial(grad_kernel, *sizes, slot, swapped, plan...  15.1 us
    pallas_call x4, Pallas kernels, project_step(): pl.pallas_call(functools.partial(project_kernel, slot, swapped, plan, fir...  8.21 us
    pallas_call x1, Pallas kernels, on_device(): pl.pallas_call(functools.partial(pack_kernel, groups, unit_count, rows, f...  3.66 us
    unnamed x19, local copies, waits for them, and re-layouts  3.46 us
    pallas_call x1, Pallas kernels, on_device(): pl.pallas_call(functools.partial(forward_kernel, *sizes, fold), out_shape...  3 us
  transfers between devices with their start and end apart: 22, of which 9 were waited for; matrix products, arithmetic and copies ran while one was open for 6% of the time, Pallas kernels for 24%

profile of v3, /device:TPU:0, one launch (start us, length us, event | category | flops | bytes accessed | tf_op | source)
XLA Modules:
  0.0 118.5 jit_solution(18083710342215828362)
XLA Ops:
  0.6 0.5 collective-permute-start
  1.2 2.0 %far.1 = bf16[256,1024]{1,0:T(8,128)(2,1)} custom-call(s32[1]{0:T(128)} %bitcast.meta, bf16[256,4096]{1,0:T(8,128)(2,1)} %refs_6_.1), custom_call_target="tpu_custom_call" | custom-call | tf_op jit(solution)/shard_map/far/pallas_call | solution.py:354
  3.2 3.7 %collective-permute-start.5 = (bf16[256,1024]{1,0:T(8,128)(2,1)}, bf16[256,1024]{1,0:T(8,128)(2,1)}, u32[]{:S(2)}, u32[]{:S(2)}) collective-permute-start(bf16[256,1024]{1,0:T(8,128)(2,1)} %far.1), channel_id=1, source_target_pairs={{0,16},{1,17},{2,18},{3,19},{4,20},{5,21},{6,22},{7,23},{8,24},{9,... | collective-permute-start | bytes 1572872 | tf_op jit(solution)/shard_map/ppermute | solution.py:331
  6.9 0.8 slice_reduce_fusion.1
  7.7 0.6 pad_add_fusion.meta
  8.2 3.7 %pack.1 = (bf16[256,1024]{1,0:T(8,128)(2,1)}, bf16[256,1024]{1,0:T(8,128)(2,1)}, bf16[256,1024]{1,0:T(8,128)(2,1)}) custom-call(s32[5]{0:T(128)} %pad_add_fusion.meta, bf16[128,2048]{1,0:T(8,128)(2,1)} %bitcast.23, bf16[128,1024]{1,0:T(8,128)(2,1)} %bitcast.25), custom_call_target="tpu_custom_call" | custom-call | tf_op jit(solution)/shard_map/pack/pallas_call | solution.py:364
  11.9 1.6 %collective-permute-start.2 = (bf16[256,1024]{1,0:T(8,128)(2,1)}, bf16[256,1024]{1,0:T(8,128)(2,1)}, u32[]{:S(2)}, u32[]{:S(2)}) collective-permute-start(bf16[256,1024]{1,0:T(8,128)(2,1)} %get-tuple-element.42), channel_id=1, source_target_pairs={{0,1},{1,0},{2,3},{3,2},{4,5},{5,4},{6,7},{7,6},{8,9},{9,8},{10,11... | collective-permute-start | bytes 1572872 | tf_op jit(solution)/shard_map/ppermute | solution.py:331
  13.5 1.5 %collective-permute-start.3 = (bf16[256,1024]{1,0:T(8,128)(2,1)}, bf16[256,1024]{1,0:T(8,128)(2,1)}, u32[]{:S(2)}, u32[]{:S(2)}) collective-permute-start(bf16[256,1024]{1,0:T(8,128)(2,1)} %get-tuple-element.43), channel_id=1, source_target_pairs={{0,2},{1,3},{2,0},{3,1},{4,6},{5,7},{6,4},{7,5},{8,10},{9,11},{10,... | collective-permute-start | bytes 1572872 | tf_op jit(solution)/shard_map/ppermute | solution.py:331
  15.0 1.6 %fusion.17 = (bf16[256,2048]{1,0:T(8,128)(2,1)}, bf16[256,2048]{1,0:T(8,128)(2,1)}) fusion(bf16[256,4096]{1,0:T(8,128)(2,1)S(1)} %copy-done), kind=kLoop, calls=%fused_computation.43 | loop fusion | bytes 4194304 | tf_op jit(solution)/shard_map/slice | solution.py:506
  16.6 0.0 collective-permute-done.refs_1_.refs_7_
  16.6 1.6 %collective-permute-start.1 = (bf16[256,2048]{1,0:T(8,128)(2,1)}, bf16[256,2048]{1,0:T(8,128)(2,1)S(1)}, u32[]{:S(2)}, u32[]{:S(2)}) collective-permute-start(bf16[256,2048]{1,0:T(8,128)(2,1)} %get-tuple-element.39), channel_id=1, source_target_pairs={{0,8},{1,9},{2,10},{3,11},{4,12},{5,13},{6,14},{7,15},{8,0},{9,1},... | collective-permute-start | bytes 3145736 | tf_op jit(solution)/shard_map/ppermute | solution.py:331
  18.2 0.1 copy.16
  18.3 0.1 and_select_fusion.1
  18.4 0.1 add.101
  18.5 0.1 slice_reduce_fusion
  18.6 0.1 convert_reduce_fusion.1
  18.7 0.1 eq.49
  18.7 0.5 collective-permute-start.4
  19.2 0.1 and_select_fusion
  19.3 0.1 convert_reduce_fusion
  19.4 11.6 %collective-permute-done.5.refs_0_.refs_6_ = bf16[256,1024]{1,0:T(8,128)(2,1)} collective-permute-done((bf16[256,1024]{1,0:T(8,128)(2,1)}, bf16[256,1024]{1,0:T(8,128)(2,1)}, u32[]{:S(2)}, u32[]{:S(2)}) %collective-permute-start.5) | collective-permute-done | bytes 524320 | tf_op jit(solution)/shard_map/ppermute | solution.py:331
  31.0 0.7 collective-permute-start.6
  31.6 0.4 fusion.2.refs_1_
  32.0 0.1 concatenate.22.refs_0_.meta
  32.1 6.7 %collective-permute-done.3.refs_5_ = bf16[256,1024]{1,0:T(8,128)(2,1)} collective-permute-done((bf16[256,1024]{1,0:T(8,128)(2,1)}, bf16[256,1024]{1,0:T(8,128)(2,1)}, u32[]{:S(2)}, u32[]{:S(2)}) %collective-permute-start.3) | collective-permute-done | bytes 524320 | tf_op jit(solution)/shard_map/ppermute | solution.py:331
  38.8 0.0 collective-permute-done.4.refs_6_
  38.8 1.5 %collective-permute-start.9 = (bf16[256,1024]{1,0:T(8,128)(2,1)}, bf16[256,1024]{1,0:T(8,128)(2,1)S(1)}, u32[]{:S(2)}, u32[]{:S(2)}) collective-permute-start(bf16[256,1024]{1,0:T(8,128)(2,1)} %collective-permute-done.5.refs_0_.refs_6_), channel_id=1, source_target_pairs={{0,3},{1,2},{2,1},{3,0},{4,7},{5,6},{6,5},{7,4},{8,11},{9,10},{10,... | collective-permute-start | bytes 1572872 | tf_op jit(solution)/shard_map/ppermute | solution.py:331
  40.2 1.5 %collective-permute-start.7 = (bf16[256,1024]{1,0:T(8,128)(2,1)}, bf16[256,1024]{1,0:T(8,128)(2,1)S(1)}, u32[]{:S(2)}, u32[]{:S(2)}) collective-permute-start(bf16[256,1024]{1,0:T(8,128)(2,1)} %collective-permute-done.5.refs_0_.refs_6_), channel_id=1, source_target_pairs={{0,1},{1,0},{2,3},{3,2},{4,5},{5,4},{6,7},{7,6},{8,9},{9,8},{10,11... | collective-permute-start | bytes 1572872 | tf_op jit(solution)/shard_map/ppermute | solution.py:331
  41.7 0.5 collective-permute-start.8
  42.2 10.6 %collective-permute-done.1.refs_0_.refs_6_ = bf16[256,2048]{1,0:T(8,128)(2,1)S(1)} collective-permute-done((bf16[256,2048]{1,0:T(8,128)(2,1)}, bf16[256,2048]{1,0:T(8,128)(2,1)S(1)}, u32[]{:S(2)}, u32[]{:S(2)}) %collective-permute-start.1) | collective-permute-done | bytes 1048608 | tf_op jit(solution)/shard_map/ppermute | solution.py:331
  52.9 0.1 constant_dynamic-update-slice_fusion.5
  53.0 0.0 copy-start.2
  53.0 1.0 copy-done.2
  54.0 3.0 %forward.1 = (bf16[128,2048]{1,0:T(8,128)(2,1)S(1)}, f32[4,2,256,128]{3,2,1,0:T(8,128)S(1)}, bf16[2,128,1024]{2,1,0:T(8,128)(2,1)S(1)}, bf16[128,2048]{1,0:T(8,128)(2,1)S(1)}) custom-call(s32[7]{0:T(128)S(1)} %concatenate.22.refs_0_.meta, f32[2,64,128]{2,1,0:T(8,128)S(1)} %fusion.2.refs_1_, bf16[128,2048]{1,0:T(8,128)(2,1)S(1)} %bitcast.24, ...), custom_call_target="tpu_custom_call" | custom-call | flops 1073741824 | bytes 8388608 | tf_op jit(solution)/shard_map/forward/pallas_call | solution.py:395
  57.0 0.0 copy-start.1
  57.0 2.4 %project_0.1.refs_5_ = f32[128,4096]{1,0:T(8,128)S(1)} custom-call(s32[7]{0:T(128)S(1)} %concatenate.22.refs_0_.meta, bf16[128,2048]{1,0:T(8,128)(2,1)S(1)} %get-tuple-element.46.context_ref.refs_3_, bf16[256,4096]{1,0:T(8,128)(2,1)S(1)} %copy-done, bf16[256,4096]{1,0:T(8,128)(2,1)} %collective-permute-done.refs_1_.refs_7_), custom_call_target="tpu_custom_call" | custom-call | flops 536870912 | bytes 8388608 | tf_op jit(solution)/shard_map/project_0/pallas_call | solution.py:473
  59.4 4.3 %grad_0.1 = (bf16[128,2048]{1,0:T(8,128)(2,1)}, bf16[128,256]{1,0:T(8,128)(2,1)S(1)}, bf16[128,256]{1,0:T(8,128)(2,1)S(1)}, bf16[128,256]{1,0:T(8,128)(2,1)S(1)}, bf16[128,256]{1,0:T(8,128)(2,1)S(1)}) custom-call(s32[7]{0:T(128)S(1)} %concatenate.22.refs_0_.meta, bf16[128,4096]{1,0:T(8,128)(2,1)S(1)} %bitcast.19, ...), custom_call_target="tpu_custom_call" | custom-call | flops 1073741824 | bytes 12582912 | tf_op jit(solution)/shard_map/grad_0/pallas_call | solution.py:435
  63.7 0.0 copy-start.4
  63.7 1.2 constant_dynamic-update-slice_fusion.4
  64.9 1.1 constant_dynamic-update-slice_fusion.3
  66.2 0.1 collective-permute-start.10
  66.2 0.1 collective-permute-start.17
  66.3 0.8 collective-permute-start.11
  67.1 0.7 collective-permute-start.13
  67.8 2.1 %collective-permute-start.15 = (bf16[256,1024]{1,0:T(8,128)(2,1)}, bf16[256,1024]{1,0:T(8,128)(2,1)S(1)}, u32[]{:S(2)}, u32[]{:S(2)}) collective-permute-start(bf16[256,1024]{1,0:T(8,128)(2,1)} %collective-permute-done.6.refs_0_.refs_6_), channel_id=1, source_target_pairs={{0,3},{1,2},{2,1},{3,0},{4,7},{5,6},{6,5},{7,4},{8,11},{9,10},{10,... | collective-permute-start | bytes 1572872 | tf_op jit(solution)/shard_map/ppermute | solution.py:331
  69.9 2.8 %collective-permute-done.10.refs_4_.refs_10_.refs_1_.refs_7_ = bf16[256,7168]{1,0:T(8,128)(2,1)S(1)} collective-permute-done((bf16[256,7168]{1,0:T(8,128)(2,1)S(1)}, bf16[256,7168]{1,0:T(8,128)(2,1)S(1)}, u32[]{:S(2)}, u32[]{:S(2)}) %collective-permute-start.10) | collective-permute-done | bytes 3670048 | tf_op jit(solution)/shard_map/ppermute | solution.py:331
  72.6 1.8 %project_2.1.refs_4_ = f32[128,4096]{1,0:T(8,128)S(1)} custom-call(s32[7]{0:T(128)S(1)} %concatenate.22.refs_0_.meta, bf16[128,2048]{1,0:T(8,128)(2,1)S(1)} %get-tuple-element.46.context_ref.refs_3_, bf16[256,1024]{1,0:T(8,128)(2,1)} %collective-permute-done.5.refs_0_.refs_6_, bf16[256,1024]{1,0:T(8,128)(2,1)S(1)} %collective-permute-done.7.refs_1_.refs_7_, ...), custom_call_target="tpu_custom_call" | custom-call | flops 536870912 | bytes 8388608 | tf_op jit(solution)/shard_map/project_2/pallas_call | solution.py:473
  74.4 3.8 %grad_2.1 = (bf16[128,2048]{1,0:T(8,128)(2,1)}, bf16[128,256]{1,0:T(8,128)(2,1)S(1)}, bf16[128,256]{1,0:T(8,128)(2,1)S(1)}, bf16[128,256]{1,0:T(8,128)(2,1)S(1)}, bf16[128,256]{1,0:T(8,128)(2,1)S(1)}) custom-call(s32[7]{0:T(128)S(1)} %concatenate.22.refs_0_.meta, bf16[128,4096]{1,0:T(8,128)(2,1)S(1)} %bitcast.20, ...), custom_call_target="tpu_custom_call", output_to_operand_aliasing={{0}: (11, {})} | custom-call | flops 1073741824 | bytes 12582912 | tf_op jit(solution)/shard_map/grad_2/pallas_call | solution.py:435
  78.2 3.2 %collective-permute-done.11.refs_2_.refs_8_ = bf16[256,1024]{1,0:T(8,128)(2,1)S(1)} collective-permute-done((bf16[256,1024]{1,0:T(8,128)(2,1)}, bf16[256,1024]{1,0:T(8,128)(2,1)S(1)}, u32[]{:S(2)}, u32[]{:S(2)}) %collective-permute-start.11) | collective-permute-done | bytes 524320 | tf_op jit(solution)/shard_map/ppermute | solution.py:331
  81.3 11.1 %collective-permute-done.13.refs_4_.refs_10_ = bf16[256,1024]{1,0:T(8,128)(2,1)S(1)} collective-permute-done((bf16[256,1024]{1,0:T(8,128)(2,1)}, bf16[256,1024]{1,0:T(8,128)(2,1)S(1)}, u32[]{:S(2)}, u32[]{:S(2)}) %collective-permute-start.13) | collective-permute-done | bytes 524320 | tf_op jit(solution)/shard_map/ppermute | solution.py:331
  92.4 0.5 collective-permute-start.12
  92.9 0.1 collective-permute-start.14
  93.0 0.4 collective-permute-start.16
  93.4 1.6 %collective-permute-done.18.refs_3_.refs_9_ = bf16[256,2048]{1,0:T(8,128)(2,1)S(1)} collective-permute-done((bf16[256,2048]{1,0:T(8,128)(2,1)S(1)}, bf16[256,2048]{1,0:T(8,128)(2,1)S(1)}, u32[]{:S(2)}, u32[]{:S(2)}) %collective-permute-start.18) | collective-permute-done | bytes 1048608 | tf_op jit(solution)/shard_map/ppermute | solution.py:331
  95.1 3.2 %grad_1.1 = (bf16[128,2048]{1,0:T(8,128)(2,1)}, bf16[128,256]{1,0:T(8,128)(2,1)S(1)}, bf16[128,256]{1,0:T(8,128)(2,1)S(1)}, bf16[128,256]{1,0:T(8,128)(2,1)S(1)}, bf16[128,256]{1,0:T(8,128)(2,1)S(1)}) custom-call(s32[7]{0:T(128)S(1)} %concatenate.22.refs_0_.meta, bf16[128,4096]{1,0:T(8,128)(2,1)S(1)} %bitcast.21, ...), custom_call_target="tpu_custom_call", output_to_operand_aliasing={{0}: (10, {})} | custom-call | flops 1073741824 | bytes 12582912 | tf_op jit(solution)/shard_map/grad_1/pallas_call | solution.py:435
  98.4 3.8 %grad_3.1 = (bf16[128,2048]{1,0:T(8,128)(2,1)}, bf16[128,256]{1,0:T(8,128)(2,1)S(1)}, bf16[128,256]{1,0:T(8,128)(2,1)S(1)}, bf16[128,256]{1,0:T(8,128)(2,1)S(1)}, bf16[128,256]{1,0:T(8,128)(2,1)S(1)}) custom-call(s32[7]{0:T(128)S(1)} %concatenate.22.refs_0_.meta, bf16[128,4096]{1,0:T(8,128)(2,1)S(1)} %bitcast.22, ...), custom_call_target="tpu_custom_call", output_to_operand_aliasing={{0}: (14, {})} | custom-call | flops 1073741824 | bytes 12582912 | tf_op jit(solution)/shard_map/grad_3/pallas_call | solution.py:435
  102.2 1.5 %collective-permute-start.21 = (bf16[128,1024]{1,0:T(8,128)(2,1)S(1)}, bf16[128,1024]{1,0:T(8,128)(2,1)S(1)}, u32[]{:S(2)}, u32[]{:S(2)}) collective-permute-start(bf16[128,1024]{1,0:T(8,128)(2,1)S(1)} %pad_maximum_fusion.3), channel_id=1, source_target_pairs={{0,3},{1,2},{2,1},{3,0},{4,7},{5,6},{6,5},{7,4},{8,11},{9,10},{10,... | collective-permute-start | bytes 786440 | tf_op jit(solution)/shard_map/ppermute | solution.py:331
  103.7 1.4 %collective-permute-start.20 = (bf16[128,1024]{1,0:T(8,128)(2,1)S(1)}, bf16[128,1024]{1,0:T(8,128)(2,1)S(1)}, u32[]{:S(2)}, u32[]{:S(2)}) collective-permute-start(bf16[128,1024]{1,0:T(8,128)(2,1)S(1)} %pad_maximum_fusion.2), channel_id=1, source_target_pairs={{0,2},{1,3},{2,0},{3,1},{4,6},{5,7},{6,4},{7,5},{8,10},{9,11},{10,... | collective-permute-start | bytes 786440 | tf_op jit(solution)/shard_map/ppermute | solution.py:331
  105.2 0.7 collective-permute-start.19
  105.9 1.3 %project_1.1.refs_8_ = f32[128,4096]{1,0:T(8,128)S(1)} custom-call(s32[7]{0:T(128)S(1)} %concatenate.22.refs_0_.meta, bf16[128,2048]{1,0:T(8,128)(2,1)S(1)} %get-tuple-element.46.context_ref.refs_3_, bf16[256,2048]{1,0:T(8,128)(2,1)S(1)} %collective-permute-done.1.refs_0_.refs_6_, ...), custom_call_target="tpu_custom_call" | custom-call | flops 536870912 | bytes 8388608 | tf_op jit(solution)/shard_map/project_1/pallas_call | solution.py:473
  107.2 2.8 %project_3.1 = bf16[128,4096]{1,0:T(8,128)(2,1)} custom-call(s32[7]{0:T(128)S(1)} %concatenate.22.refs_0_.meta, bf16[128,2048]{1,0:T(8,128)(2,1)S(1)} %get-tuple-element.46.context_ref.refs_3_, bf16[256,1024]{1,0:T(8,128)(2,1)} %collective-permute-done.6.refs_0_.refs_6_, bf16[256,7168]{1,0:T(8,128)(2,1)S(1)} %collective-permute-done.10.refs_4_.refs_10_.refs_1_.refs_7_, ...), custom_call_target="tpu_custom_call" | custom-call | flops 536870912 | bytes 8388608 | tf_op jit(solution)/shard_map/project_3/pallas_call | solution.py:473
  110.0 2.4 %collective-permute-done.21.refs_3_ = bf16[128,1024]{1,0:T(8,128)(2,1)S(1)} collective-permute-done((bf16[128,1024]{1,0:T(8,128)(2,1)S(1)}, bf16[128,1024]{1,0:T(8,128)(2,1)S(1)}, u32[]{:S(2)}, u32[]{:S(2)}) %collective-permute-start.21) | collective-permute-done | bytes 262176 | tf_op jit(solution)/shard_map/ppermute | solution.py:331
  112.3 4.8 %collective-permute-done.20.refs_2_ = bf16[128,1024]{1,0:T(8,128)(2,1)S(1)} collective-permute-done((bf16[128,1024]{1,0:T(8,128)(2,1)S(1)}, bf16[128,1024]{1,0:T(8,128)(2,1)S(1)}, u32[]{:S(2)}, u32[]{:S(2)}) %collective-permute-start.20) | collective-permute-done | bytes 262176 | tf_op jit(solution)/shard_map/ppermute | solution.py:331
  117.1 1.4 %combine_0.1 = bf16[128,1024]{1,0:T(8,128)(2,1)} custom-call(s32[7]{0:T(128)S(1)} %concatenate.22.refs_0_.meta, bf16[128,1024]{1,0:T(8,128)(2,1)S(1)} %pad_maximum_fusion.refs_0_, bf16[128,1024]{1,0:T(8,128)(2,1)S(1)} %collective-permute-done.19.refs_1_, bf16[128,1024]{1,0:T(8,128)(2,1)S(1)} %collective-permute-done.20.refs_2_, ...), custom_call_target="tpu_custom_call" | custom-call | tf_op jit(solution)/shard_map/combine_0/pallas_call | solution.py:550
  (31 shorter events, 0.3 us)
Async XLA Ops:
  0.6 14.4 %copy-start = (bf16[256,4096]{1,0:T(8,128)(2,1)S(1)}, bf16[256,4096]{1,0:T(8,128)(2,1)}, u32[]{:S(2)}) copy-start(bf16[256,4096]{1,0:T(8,128)(2,1)} %refs_6_.1) | copy-start | bytes 6291460
  0.6 15.9 %collective-permute-start = (bf16[256,4096]{1,0:T(8,128)(2,1)}, bf16[256,4096]{1,0:T(8,128)(2,1)}, u32[]{:S(2)}, u32[]{:S(2)}) collective-permute-start(bf16[256,4096]{1,0:T(8,128)(2,1)} %refs_6_.1), channel_id=1, source_target_pairs={{0,4},{1,5},{2,6},{3,7},{4,0},{5,1},{6,2},{7,3},{8,12},{9,13},{10,... | collective-permute-start | bytes 6291464 | tf_op jit(solution)/shard_map/ppermute | solution.py:331
  1.2 17.0 %copy-start.5 = (s32[1,16]{1,0:T(1,128)S(1)}, s32[1,16]{1,0:T(1,128)}, u32[]{:S(2)}) copy-start(s32[1,16]{1,0:T(1,128)} %param.11) | copy-start | bytes 196
  1.2 30.5 %copy-start.6 = (s32[1,4,4]{2,1,0:T(4,128)S(1)}, s32[1,4,4]{2,1,0:T(4,128)}, u32[]{:S(2)}) copy-start(s32[1,4,4]{2,1,0:T(4,128)} %param.12) | copy-start | bytes 196
  3.2 27.8 %collective-permute-start.5 = (bf16[256,1024]{1,0:T(8,128)(2,1)}, bf16[256,1024]{1,0:T(8,128)(2,1)}, u32[]{:S(2)}, u32[]{:S(2)}) collective-permute-start(bf16[256,1024]{1,0:T(8,128)(2,1)} %far.1), channel_id=1, source_target_pairs={{0,16},{1,17},{2,18},{3,19},{4,20},{5,21},{6,22},{7,23},{8,24},{9,... | collective-permute-start | bytes 1572872 | tf_op jit(solution)/shard_map/ppermute | solution.py:331
  8.2 44.7 %copy-start.3 = (bf16[1,128,1024]{2,1,0:T(8,128)(2,1)S(1)}, bf16[1,128,1024]{2,1,0:T(8,128)(2,1)}, u32[]{:S(2)}) copy-start(bf16[1,128,1024]{2,1,0:T(8,128)(2,1)} %param.8) | copy-start | bytes 786436
  11.9 20.2 %collective-permute-start.2 = (bf16[256,1024]{1,0:T(8,128)(2,1)}, bf16[256,1024]{1,0:T(8,128)(2,1)}, u32[]{:S(2)}, u32[]{:S(2)}) collective-permute-start(bf16[256,1024]{1,0:T(8,128)(2,1)} %get-tuple-element.42), channel_id=1, source_target_pairs={{0,1},{1,0},{2,3},{3,2},{4,5},{5,4},{6,7},{7,6},{8,9},{9,8},{10,11... | collective-permute-start | bytes 1572872 | tf_op jit(solution)/shard_map/ppermute | solution.py:331
  13.5 25.3 %collective-permute-start.3 = (bf16[256,1024]{1,0:T(8,128)(2,1)}, bf16[256,1024]{1,0:T(8,128)(2,1)}, u32[]{:S(2)}, u32[]{:S(2)}) collective-permute-start(bf16[256,1024]{1,0:T(8,128)(2,1)} %get-tuple-element.43), channel_id=1, source_target_pairs={{0,2},{1,3},{2,0},{3,1},{4,6},{5,7},{6,4},{7,5},{8,10},{9,11},{10,... | collective-permute-start | bytes 1572872 | tf_op jit(solution)/shard_map/ppermute | solution.py:331
  16.6 36.3 %collective-permute-start.1 = (bf16[256,2048]{1,0:T(8,128)(2,1)}, bf16[256,2048]{1,0:T(8,128)(2,1)S(1)}, u32[]{:S(2)}, u32[]{:S(2)}) collective-permute-start(bf16[256,2048]{1,0:T(8,128)(2,1)} %get-tuple-element.39), channel_id=1, source_target_pairs={{0,8},{1,9},{2,10},{3,11},{4,12},{5,13},{6,14},{7,15},{8,0},{9,1},... | collective-permute-start | bytes 3145736 | tf_op jit(solution)/shard_map/ppermute | solution.py:331
  18.7 20.0 %collective-permute-start.4 = (bf16[256,1024]{1,0:T(8,128)(2,1)}, bf16[256,1024]{1,0:T(8,128)(2,1)}, u32[]{:S(2)}, u32[]{:S(2)}) collective-permute-start(bf16[256,1024]{1,0:T(8,128)(2,1)} %get-tuple-element.45), channel_id=1, source_target_pairs={{0,3},{1,2},{2,1},{3,0},{4,7},{5,6},{6,5},{7,4},{8,11},{9,10},{10,... | collective-permute-start | bytes 1572872 | tf_op jit(solution)/shard_map/ppermute | solution.py:331
  31.0 32.8 %collective-permute-start.6 = (bf16[256,1024]{1,0:T(8,128)(2,1)}, bf16[256,1024]{1,0:T(8,128)(2,1)}, u32[]{:S(2)}, u32[]{:S(2)}) collective-permute-start(bf16[256,1024]{1,0:T(8,128)(2,1)} %collective-permute-done.5.refs_0_.refs_6_), channel_id=1, source_target_pairs={{0,8},{1,9},{2,10},{3,11},{4,12},{5,13},{6,14},{7,15},{8,0},{9,1},... | collective-permute-start | bytes 1572872 | tf_op jit(solution)/shard_map/ppermute | solution.py:331
  38.8 27.2 %collective-permute-start.9 = (bf16[256,1024]{1,0:T(8,128)(2,1)}, bf16[256,1024]{1,0:T(8,128)(2,1)S(1)}, u32[]{:S(2)}, u32[]{:S(2)}) collective-permute-start(bf16[256,1024]{1,0:T(8,128)(2,1)} %collective-permute-done.5.refs_0_.refs_6_), channel_id=1, source_target_pairs={{0,3},{1,2},{2,1},{3,0},{4,7},{5,6},{6,5},{7,4},{8,11},{9,10},{10,... | collective-permute-start | bytes 1572872 | tf_op jit(solution)/shard_map/ppermute | solution.py:331
  40.2 25.8 %collective-permute-start.7 = (bf16[256,1024]{1,0:T(8,128)(2,1)}, bf16[256,1024]{1,0:T(8,128)(2,1)S(1)}, u32[]{:S(2)}, u32[]{:S(2)}) collective-permute-start(bf16[256,1024]{1,0:T(8,128)(2,1)} %collective-permute-done.5.refs_0_.refs_6_), channel_id=1, source_target_pairs={{0,1},{1,0},{2,3},{3,2},{4,5},{5,4},{6,7},{7,6},{8,9},{9,8},{10,11... | collective-permute-start | bytes 1572872 | tf_op jit(solution)/shard_map/ppermute | solution.py:331
  41.7 24.3 %collective-permute-start.8 = (bf16[256,1024]{1,0:T(8,128)(2,1)}, bf16[256,1024]{1,0:T(8,128)(2,1)S(1)}, u32[]{:S(2)}, u32[]{:S(2)}) collective-permute-start(bf16[256,1024]{1,0:T(8,128)(2,1)} %collective-permute-done.5.refs_0_.refs_6_), channel_id=1, source_target_pairs={{0,2},{1,3},{2,0},{3,1},{4,6},{5,7},{6,4},{7,5},{8,10},{9,11},{10,... | collective-permute-start | bytes 1572872 | tf_op jit(solution)/shard_map/ppermute | solution.py:331
  53.0 1.0 copy-start.2
  57.0 2.4 %copy-start.1 = (bf16[1,128,4096]{2,1,0:T(8,128)(2,1)S(1)}, bf16[1,128,4096]{2,1,0:T(8,128)(2,1)}, u32[]{:S(2)}) copy-start(bf16[1,128,4096]{2,1,0:T(8,128)(2,1)} %param.9) | copy-start | bytes 3145732
  63.7 2.5 %copy-start.4 = (bf16[256,2048]{1,0:T(8,128)(2,1)S(1)}, bf16[256,2048]{1,0:T(8,128)(2,1)}, u32[]{:S(2)}) copy-start(bf16[256,2048]{1,0:T(8,128)(2,1)} %get-tuple-element.54) | copy-start | bytes 3145732
  66.2 6.5 %collective-permute-start.10 = (bf16[256,7168]{1,0:T(8,128)(2,1)S(1)}, bf16[256,7168]{1,0:T(8,128)(2,1)S(1)}, u32[]{:S(2)}, u32[]{:S(2)}) collective-permute-start(bf16[256,7168]{1,0:T(8,128)(2,1)S(1)} %constant_dynamic-update-slice_fusion), channel_id=1, source_target_pairs={{0,4},{1,5},{2,6},{3,7},{4,0},{5,1},{6,2},{7,3},{8,12},{9,13},{10,... | collective-permute-start | bytes 11010056 | tf_op jit(solution)/shard_map/ppermute | solution.py:331
  66.2 26.2 %collective-permute-start.17 = (bf16[256,2048]{1,0:T(8,128)(2,1)S(1)}, bf16[256,2048]{1,0:T(8,128)(2,1)S(1)}, u32[]{:S(2)}, u32[]{:S(2)}) collective-permute-start(bf16[256,2048]{1,0:T(8,128)(2,1)S(1)} %copy-done.4), channel_id=1, source_target_pairs={{0,8},{1,9},{2,10},{3,11},{4,12},{5,13},{6,14},{7,15},{8,0},{9,1},... | collective-permute-start | bytes 3145736 | tf_op jit(solution)/shard_map/ppermute | solution.py:331
  66.3 15.0 %collective-permute-start.11 = (bf16[256,1024]{1,0:T(8,128)(2,1)}, bf16[256,1024]{1,0:T(8,128)(2,1)S(1)}, u32[]{:S(2)}, u32[]{:S(2)}) collective-permute-start(bf16[256,1024]{1,0:T(8,128)(2,1)} %collective-permute-done.6.refs_0_.refs_6_), channel_id=1, source_target_pairs={{0,1},{1,0},{2,3},{3,2},{4,5},{5,4},{6,7},{7,6},{8,9},{9,8},{10,11... | collective-permute-start | bytes 1572872 | tf_op jit(solution)/shard_map/ppermute | solution.py:331
  67.1 25.3 %collective-permute-start.13 = (bf16[256,1024]{1,0:T(8,128)(2,1)}, bf16[256,1024]{1,0:T(8,128)(2,1)S(1)}, u32[]{:S(2)}, u32[]{:S(2)}) collective-permute-start(bf16[256,1024]{1,0:T(8,128)(2,1)} %collective-permute-done.6.refs_0_.refs_6_), channel_id=1, source_target_pairs={{0,2},{1,3},{2,0},{3,1},{4,6},{5,7},{6,4},{7,5},{8,10},{9,11},{10,... | collective-permute-start | bytes 1572872 | tf_op jit(solution)/shard_map/ppermute | solution.py:331
  67.8 24.6 %collective-permute-start.15 = (bf16[256,1024]{1,0:T(8,128)(2,1)}, bf16[256,1024]{1,0:T(8,128)(2,1)S(1)}, u32[]{:S(2)}, u32[]{:S(2)}) collective-permute-start(bf16[256,1024]{1,0:T(8,128)(2,1)} %collective-permute-done.6.refs_0_.refs_6_), channel_id=1, source_target_pairs={{0,3},{1,2},{2,1},{3,0},{4,7},{5,6},{6,5},{7,4},{8,11},{9,10},{10,... | collective-permute-start | bytes 1572872 | tf_op jit(solution)/shard_map/ppermute | solution.py:331
  92.4 2.7 %collective-permute-start.18 = (bf16[256,2048]{1,0:T(8,128)(2,1)S(1)}, bf16[256,2048]{1,0:T(8,128)(2,1)S(1)}, u32[]{:S(2)}, u32[]{:S(2)}) collective-permute-start(bf16[256,2048]{1,0:T(8,128)(2,1)S(1)} %collective-permute-done.17.refs_2_.refs_8_), channel_id=1, source_target_pairs={{0,4},{1,5},{2,6},{3,7},{4,0},{5,1},{6,2},{7,3},{8,12},{9,13},{10,... | collective-permute-start | bytes 3145736 | tf_op jit(solution)/shard_map/ppermute | solution.py:331
  92.4 5.9 %collective-permute-start.12 = (bf16[256,1024]{1,0:T(8,128)(2,1)S(1)}, bf16[256,1024]{1,0:T(8,128)(2,1)S(1)}, u32[]{:S(2)}, u32[]{:S(2)}) collective-permute-start(bf16[256,1024]{1,0:T(8,128)(2,1)S(1)} %collective-permute-done.11.refs_2_.refs_8_), channel_id=1, source_target_pairs={{0,4},{1,5},{2,6},{3,7},{4,0},{5,1},{6,2},{7,3},{8,12},{9,13},{10,... | collective-permute-start | bytes 1572872 | tf_op jit(solution)/shard_map/ppermute | solution.py:331
  92.9 5.4 %collective-permute-start.14 = (bf16[256,1024]{1,0:T(8,128)(2,1)S(1)}, bf16[256,1024]{1,0:T(8,128)(2,1)S(1)}, u32[]{:S(2)}, u32[]{:S(2)}) collective-permute-start(bf16[256,1024]{1,0:T(8,128)(2,1)S(1)} %collective-permute-done.13.refs_4_.refs_10_), channel_id=1, source_target_pairs={{0,4},{1,5},{2,6},{3,7},{4,0},{5,1},{6,2},{7,3},{8,12},{9,13},{10,... | collective-permute-start | bytes 1572872 | tf_op jit(solution)/shard_map/ppermute | solution.py:331
  93.0 5.4 %collective-permute-start.16 = (bf16[256,1024]{1,0:T(8,128)(2,1)S(1)}, bf16[256,1024]{1,0:T(8,128)(2,1)S(1)}, u32[]{:S(2)}, u32[]{:S(2)}) collective-permute-start(bf16[256,1024]{1,0:T(8,128)(2,1)S(1)} %collective-permute-done.15.refs_6_.refs_12_), channel_id=1, source_target_pairs={{0,4},{1,5},{2,6},{3,7},{4,0},{5,1},{6,2},{7,3},{8,12},{9,13},{10,... | collective-permute-start | bytes 1572872 | tf_op jit(solution)/shard_map/ppermute | solution.py:331
  102.2 10.2 %collective-permute-start.21 = (bf16[128,1024]{1,0:T(8,128)(2,1)S(1)}, bf16[128,1024]{1,0:T(8,128)(2,1)S(1)}, u32[]{:S(2)}, u32[]{:S(2)}) collective-permute-start(bf16[128,1024]{1,0:T(8,128)(2,1)S(1)} %pad_maximum_fusion.3), channel_id=1, source_target_pairs={{0,3},{1,2},{2,1},{3,0},{4,7},{5,6},{6,5},{7,4},{8,11},{9,10},{10,... | collective-permute-start | bytes 786440 | tf_op jit(solution)/shard_map/ppermute | solution.py:331
  103.7 13.4 %collective-permute-start.20 = (bf16[128,1024]{1,0:T(8,128)(2,1)S(1)}, bf16[128,1024]{1,0:T(8,128)(2,1)S(1)}, u32[]{:S(2)}, u32[]{:S(2)}) collective-permute-start(bf16[128,1024]{1,0:T(8,128)(2,1)S(1)} %pad_maximum_fusion.2), channel_id=1, source_target_pairs={{0,2},{1,3},{2,0},{3,1},{4,6},{5,7},{6,4},{7,5},{8,10},{9,11},{10,... | collective-permute-start | bytes 786440 | tf_op jit(solution)/shard_map/ppermute | solution.py:331
  105.2 11.9 %collective-permute-start.19 = (bf16[128,1024]{1,0:T(8,128)(2,1)S(1)}, bf16[128,1024]{1,0:T(8,128)(2,1)S(1)}, u32[]{:S(2)}, u32[]{:S(2)}) collective-permute-start(bf16[128,1024]{1,0:T(8,128)(2,1)S(1)} %pad_maximum_fusion.1), channel_id=1, source_target_pairs={{0,1},{1,0},{2,3},{3,2},{4,5},{5,4},{6,7},{7,6},{8,9},{9,8},{10,11... | collective-permute-start | bytes 786440 | tf_op jit(solution)/shard_map/ppermute | solution.py:331

commit v4 on v3

--- a/solution.py
+++ b/solution.py
@@ -59,22 +59,19 @@
     )
 
 
-def column_kernel(wide, meta, block_ref, out_ref, sem):
-    start = pl.multiple_of(meta[0] * wide, wide)
-    copy = pltpu.make_async_copy(block_ref.at[:, pl.ds(start, wide)], out_ref, sem)
-    copy.start()
-    copy.wait()
-
-
-def pack_kernel(groups, units, rows, fold, meta, q_ref, kv_ref, *refs):
+def pack_kernel(groups, units, rows, fold, wide_far, routes, q_ref, kv_ref, *refs):
     outs, sems = refs[:-1], refs[-1]
     per_shard, wide = kv_ref.shape
-    me = meta[0]
+    me = lax.axis_index("ctx")
     copies = []
+    if wide_far:
+        block_ref, outs = outs[0], outs[1:]
+        start = pl.multiple_of(me * wide_far, wide_far)
+        copies.append((block_ref.at[:, pl.ds(start, wide_far)], outs[-1]))
     for t in range(1, groups):
         chosen = 0
         for j in range(units):
-            dest = lax.rem(me + meta[3 + j], groups)
+            dest = lax.rem(me + routes[0, 0, j], groups)
             chosen = chosen + jnp.where(dest == jnp.bitwise_xor(me, t), j, 0)
         start = pl.multiple_of(chosen * rows, rows)
         copies.append((kv_ref, outs[t - 1].at[pl.ds(0, per_shard)]))
@@ -347,31 +344,23 @@
     head_width = QUERY_HEADS * HEAD_WIDTH
     fold = head_width // (2 * KEY_WIDTH)
     sources = lax.rem(me - offsets + groups, groups)
-    source = queries[0]
+    quarter = model // groups
+    half = model // 2
+    wide_far = quarter if swapped else 0
+    shapes = [jax.ShapeDtypeStruct((per_shard + fold * rows, 2 * KEY_WIDTH), BF16)] * (groups - 1)
     if swapped:
-        quarter = model // groups
-        half = model // 2
-        far = pl.pallas_call(
-            functools.partial(column_kernel, quarter),
-            out_shape=jax.ShapeDtypeStruct((out_proj.shape[0], quarter), BF16),
-            in_specs=[in_smem(), anywhere()],
-            out_specs=whole(),
-            scratch_shapes=[pltpu.SemaphoreType.DMA],
-            name="far",
-        )(me[None], out_proj)
-        two = to_chip(far, 2)
-        source = after(source, far)
+        shapes.append(jax.ShapeDtypeStruct((out_proj.shape[0], quarter), BF16))
     sent = pl.pallas_call(
-        functools.partial(pack_kernel, groups, unit_count, rows, fold),
-        out_shape=tuple(
-            jax.ShapeDtypeStruct((per_shard + fold * rows, 2 * KEY_WIDTH), BF16)
-            for _ in range(1, groups)
-        ),
-        in_specs=[in_smem(), anywhere(), anywhere()],
-        out_specs=(whole(),) * (groups - 1),
-        scratch_shapes=[pltpu.SemaphoreType.DMA(((groups - 1) * (1 + fold),))],
+        functools.partial(pack_kernel, groups, unit_count, rows, fold, wide_far),
+        out_shape=tuple(shapes),
+        in_specs=[in_smem(), anywhere(), anywhere()] + [anywhere()] * int(swapped),
+        out_specs=(whole(),) * len(shapes),
+        scratch_shapes=[pltpu.SemaphoreType.DMA(((groups - 1) * (1 + fold) + int(swapped),))],
         name="pack",
-    )(dests_meta, source, keys_values[0])
+    )(unit_dest, queries[0], keys_values[0], *([out_proj] if swapped else []))
+    if swapped:
+        two = to_chip(sent[-1], 2)
+        sent = sent[:-1]
     sent = list(sent)
     if swapped:
         own_other = to_core(out_proj)
@@ -386,8 +375,6 @@
     key_pos = win_start[:, None] + jnp.arange(width, dtype=jnp.int32)[None, :]
     allowed = window_mask(query_pos, key_pos, lengths, tiles).astype(F32)
     meta = jnp.concatenate([dests_meta, win_start]).astype(jnp.int32)
-    if swapped:
-        allowed = after(allowed, one_a)
 
     params = pltpu.CompilerParams(vmem_limit_bytes=(16 if swapped else 40) * MIB)
     sizes = (groups, unit_count, rows, width, per_shard)

time: 119 us -> 118 us (level)
  waiting for transfers between devices: 54.6 us -> 51.7 us
  local copies, waits for them, and re-layouts: 6.31 us -> 8.96 us
    ppermute x22, waiting for transfers between devices: 54.6 us -> 51.7 us  [move(): return lax.ppermute(block, ('dp', 'ctx'), pairs)]
    unnamed x19 -> x20, local copies, waits for them, and re-layouts: 3.46 us -> 6.12 us
    pallas_call x1 -> x0, Pallas kernels: 1.99 us -> none  [on_device(): pl.pallas_call(functools.partial(column_kernel, quarter), out_shape=jax.S...]
  transfers between devices with their start and end apart: 22 -> 22, of which waited for: 9 -> 9; matrix products, arithmetic and copies ran while one was open for 6% -> 7% of each run, Pallas kernels for 24% -> 24%
where the time goes in v4:
time: 118 us; the launch traced here: 117 us
  waiting for transfers between devices  51.7 us (44%)
  Pallas kernels  33 us (28%)
  starting transfers between devices  21.9 us (19%)
  local copies, waits for them, and re-layouts  8.96 us (8%)
    ppermute x22, waiting for transfers between devices, move(): return lax.ppermute(block, ('dp', 'ctx'), pairs)  51.7 us
    ppermute x22, starting transfers between devices, move(): return lax.ppermute(block, ('dp', 'ctx'), pairs)  21.9 us
    pallas_call x4, Pallas kernels, grad_step(): pl.pallas_call(functools.partial(grad_kernel, *sizes, slot, swapped, plan...  15.8 us
    pallas_call x4, Pallas kernels, project_step(): pl.pallas_call(functools.partial(project_kernel, slot, swapped, plan, fir...  8.82 us
    unnamed x20, local copies, waits for them, and re-layouts  6.12 us
    pallas_call x1, Pallas kernels, on_device(): pl.pallas_call(functools.partial(pack_kernel, groups, unit_count, rows, f...  3.95 us
    pallas_call x1, Pallas kernels, on_device(): pl.pallas_call(functools.partial(forward_kernel, *sizes, fold), out_shape...  3 us
  transfers between devices with their start and end apart: 22, of which 9 were waited for; matrix products, arithmetic and copies ran while one was open for 7% of the time, Pallas kernels for 24%

profile of v4, /device:TPU:0, one launch (start us, length us, event | category | flops | bytes accessed | tf_op | source)
XLA Modules:
  0.0 117.2 jit_solution(9564682991243659150)
XLA Ops:
  0.6 0.0 copy-start
  0.7 0.5 collective-permute-start.2
  1.2 1.4 %copy.19.routes = s32[1,4,2]{2,1,0:T(4,128)} copy(s32[1,4,2]{1,2,0:T(2,128)} %param.13) | data formatting | bytes 64 | tf_op args[6]
  2.6 3.9 %pack.1 = (bf16[256,1024]{1,0:T(8,128)(2,1)}, bf16[256,1024]{1,0:T(8,128)(2,1)}, bf16[256,1024]{1,0:T(8,128)(2,1)}, bf16[256,1024]{1,0:T(8,128)(2,1)}) custom-call(s32[1,4,2]{2,1,0:T(4,128)} %copy.19.routes, bf16[128,2048]{1,0:T(8,128)(2,1)} %bitcast.23, bf16[128,1024]{1,0:T(8,128)(2,1)} %bitcast.25, bf16[256,4096]{1,0:T(8,128)(2,1)} %refs_6_.1), custom_call_target="tpu_custom_call" | custom-call | tf_op jit(solution)/shard_map/pack/pallas_call | solution.py:353
  6.6 2.5 %collective-permute-start = (bf16[256,1024]{1,0:T(8,128)(2,1)}, bf16[256,1024]{1,0:T(8,128)(2,1)}, u32[]{:S(2)}, u32[]{:S(2)}) collective-permute-start(bf16[256,1024]{1,0:T(8,128)(2,1)} %get-tuple-element.38), channel_id=1, source_target_pairs={{0,1},{1,0},{2,3},{3,2},{4,5},{5,4},{6,7},{7,6},{8,9},{9,8},{10,11... | collective-permute-start | bytes 1572872 | tf_op jit(solution)/shard_map/ppermute | solution.py:328
  9.1 1.5 %collective-permute-start.1 = (bf16[256,1024]{1,0:T(8,128)(2,1)}, bf16[256,1024]{1,0:T(8,128)(2,1)}, u32[]{:S(2)}, u32[]{:S(2)}) collective-permute-start(bf16[256,1024]{1,0:T(8,128)(2,1)} %get-tuple-element.39), channel_id=1, source_target_pairs={{0,2},{1,3},{2,0},{3,1},{4,6},{5,7},{6,4},{7,5},{8,10},{9,11},{10,... | collective-permute-start | bytes 1572872 | tf_op jit(solution)/shard_map/ppermute | solution.py:328
  10.6 2.6 %collective-permute-start.4 = (bf16[256,1024]{1,0:T(8,128)(2,1)}, bf16[256,1024]{1,0:T(8,128)(2,1)}, u32[]{:S(2)}, u32[]{:S(2)}) collective-permute-start(bf16[256,1024]{1,0:T(8,128)(2,1)} %get-tuple-element.43), channel_id=1, source_target_pairs={{0,16},{1,17},{2,18},{3,19},{4,20},{5,21},{6,22},{7,23},{8,24},{9,... | collective-permute-start | bytes 1572872 | tf_op jit(solution)/shard_map/ppermute | solution.py:328
  13.2 0.8 slice_reduce_fusion.1
  14.0 0.0 copy-start.1
  14.1 1.6 %fusion.17 = (bf16[256,2048]{1,0:T(8,128)(2,1)}, bf16[256,2048]{1,0:T(8,128)(2,1)}) fusion(bf16[256,4096]{1,0:T(8,128)(2,1)S(1)} %copy-done), kind=kLoop, calls=%fused_computation.42 | loop fusion | bytes 4194304 | tf_op jit(solution)/shard_map/slice | solution.py:493
  15.6 1.6 %collective-permute-start.6 = (bf16[256,2048]{1,0:T(8,128)(2,1)}, bf16[256,2048]{1,0:T(8,128)(2,1)}, u32[]{:S(2)}, u32[]{:S(2)}) collective-permute-start(bf16[256,2048]{1,0:T(8,128)(2,1)} %get-tuple-element.44), channel_id=1, source_target_pairs={{0,8},{1,9},{2,10},{3,11},{4,12},{5,13},{6,14},{7,15},{8,0},{9,1},... | collective-permute-start | bytes 3145736 | tf_op jit(solution)/shard_map/ppermute | solution.py:328
  17.2 0.1 and_select_fusion.1
  17.3 0.1 copy.18
  17.4 0.1 add.101
  17.5 0.1 slice_reduce_fusion
  17.6 0.1 convert_reduce_fusion.1
  17.7 0.1 eq.49
  17.8 0.6 collective-permute-start.3
  18.3 0.1 and_select_fusion
  18.4 0.1 convert_reduce_fusion
  18.5 18.4 %collective-permute-done.4.refs_0_.refs_6_ = bf16[256,1024]{1,0:T(8,128)(2,1)} collective-permute-done((bf16[256,1024]{1,0:T(8,128)(2,1)}, bf16[256,1024]{1,0:T(8,128)(2,1)}, u32[]{:S(2)}, u32[]{:S(2)}) %collective-permute-start.4) | collective-permute-done | bytes 524320 | tf_op jit(solution)/shard_map/ppermute | solution.py:328
  36.9 0.5 collective-permute-start.5
  37.4 0.4 fusion.2.refs_1_
  37.8 0.1 concatenate.18.refs_0_.meta
  37.9 0.0 collective-permute-done.refs_4_
  37.9 0.0 collective-permute-done.1.refs_5_
  37.9 0.0 collective-permute-done.3.refs_6_
  37.9 0.6 collective-permute-start.9
  38.5 1.5 %collective-permute-start.7 = (bf16[256,1024]{1,0:T(8,128)(2,1)}, bf16[256,1024]{1,0:T(8,128)(2,1)S(1)}, u32[]{:S(2)}, u32[]{:S(2)}) collective-permute-start(bf16[256,1024]{1,0:T(8,128)(2,1)} %collective-permute-done.4.refs_0_.refs_6_), channel_id=1, source_target_pairs={{0,1},{1,0},{2,3},{3,2},{4,5},{5,4},{6,7},{7,6},{8,9},{9,8},{10,11... | collective-permute-start | bytes 1572872 | tf_op jit(solution)/shard_map/ppermute | solution.py:328
  40.0 1.5 %collective-permute-start.8 = (bf16[256,1024]{1,0:T(8,128)(2,1)}, bf16[256,1024]{1,0:T(8,128)(2,1)S(1)}, u32[]{:S(2)}, u32[]{:S(2)}) collective-permute-start(bf16[256,1024]{1,0:T(8,128)(2,1)} %collective-permute-done.4.refs_0_.refs_6_), channel_id=1, source_target_pairs={{0,2},{1,3},{2,0},{3,1},{4,6},{5,7},{6,4},{7,5},{8,10},{9,11},{10,... | collective-permute-start | bytes 1572872 | tf_op jit(solution)/shard_map/ppermute | solution.py:328
  41.5 1.0 copy-done.2
  42.5 3.0 %forward.1 = (bf16[128,2048]{1,0:T(8,128)(2,1)S(1)}, f32[4,2,256,128]{3,2,1,0:T(8,128)S(1)}, bf16[2,128,1024]{2,1,0:T(8,128)(2,1)S(1)}, bf16[128,2048]{1,0:T(8,128)(2,1)S(1)}) custom-call(s32[7]{0:T(128)S(1)} %concatenate.18.refs_0_.meta, f32[2,64,128]{2,1,0:T(8,128)S(1)} %fusion.2.refs_1_, bf16[128,2048]{1,0:T(8,128)(2,1)S(1)} %bitcast.24, ...), custom_call_target="tpu_custom_call" | custom-call | flops 1073741824 | bytes 8388608 | tf_op jit(solution)/shard_map/forward/pallas_call | solution.py:382
  45.5 4.3 %grad_0.1 = (bf16[128,2048]{1,0:T(8,128)(2,1)}, bf16[128,256]{1,0:T(8,128)(2,1)S(1)}, bf16[128,256]{1,0:T(8,128)(2,1)S(1)}, bf16[128,256]{1,0:T(8,128)(2,1)S(1)}, bf16[128,256]{1,0:T(8,128)(2,1)S(1)}) custom-call(s32[7]{0:T(128)S(1)} %concatenate.18.refs_0_.meta, bf16[128,4096]{1,0:T(8,128)(2,1)S(1)} %bitcast.19, ...), custom_call_target="tpu_custom_call" | custom-call | flops 1073741824 | bytes 12582912 | tf_op jit(solution)/shard_map/grad_0/pallas_call | solution.py:422
  49.8 2.3 %project_0.1.refs_5_ = f32[128,4096]{1,0:T(8,128)S(1)} custom-call(s32[7]{0:T(128)S(1)} %concatenate.18.refs_0_.meta, bf16[128,2048]{1,0:T(8,128)(2,1)S(1)} %get-tuple-element.42.context_ref.refs_3_, bf16[256,4096]{1,0:T(8,128)(2,1)S(1)} %copy-done, bf16[256,4096]{1,0:T(8,128)(2,1)} %collective-permute-done.2.refs_1_.refs_7_), custom_call_target="tpu_custom_call" | custom-call | flops 536870912 | bytes 8388608 | tf_op jit(solution)/shard_map/project_0/pallas_call | solution.py:460
  52.1 0.0 copy-start.4
  52.1 0.1 collective-permute-done.6.refs_0_.refs_6_
  52.2 1.4 %constant_dynamic-update-slice_fusion.5 = bf16[256,7168]{1,0:T(8,128)(2,1)S(1)} fusion(bf16[256,2048]{1,0:T(8,128)(2,1)} %collective-permute-done.6.refs_0_.refs_6_), kind=kLoop, calls=%fused_computation.15 | loop fusion | bytes 2097152
  53.6 8.3 %collective-permute-done.5.refs_0_.refs_6_ = bf16[256,1024]{1,0:T(8,128)(2,1)} collective-permute-done((bf16[256,1024]{1,0:T(8,128)(2,1)}, bf16[256,1024]{1,0:T(8,128)(2,1)}, u32[]{:S(2)}, u32[]{:S(2)}) %collective-permute-start.5) | collective-permute-done | bytes 524320 | tf_op jit(solution)/shard_map/ppermute | solution.py:328
  61.9 1.1 constant_dynamic-update-slice_fusion.4
  63.0 1.1 constant_dynamic-update-slice_fusion.3
  64.3 0.1 collective-permute-start.10
  64.4 0.3 collective-permute-start.17
  64.6 0.6 collective-permute-start.11
  65.2 0.7 collective-permute-start.13
  65.9 2.3 %collective-permute-start.15 = (bf16[256,1024]{1,0:T(8,128)(2,1)}, bf16[256,1024]{1,0:T(8,128)(2,1)S(1)}, u32[]{:S(2)}, u32[]{:S(2)}) collective-permute-start(bf16[256,1024]{1,0:T(8,128)(2,1)} %collective-permute-done.5.refs_0_.refs_6_), channel_id=1, source_target_pairs={{0,3},{1,2},{2,1},{3,0},{4,7},{5,6},{6,5},{7,4},{8,11},{9,10},{10,... | collective-permute-start | bytes 1572872 | tf_op jit(solution)/shard_map/ppermute | solution.py:328
  68.1 2.6 %collective-permute-done.10.refs_4_.refs_10_.refs_1_.refs_7_ = bf16[256,7168]{1,0:T(8,128)(2,1)S(1)} collective-permute-done((bf16[256,7168]{1,0:T(8,128)(2,1)S(1)}, bf16[256,7168]{1,0:T(8,128)(2,1)S(1)}, u32[]{:S(2)}, u32[]{:S(2)}) %collective-permute-start.10) | collective-permute-done | bytes 3670048 | tf_op jit(solution)/shard_map/ppermute | solution.py:328
  70.7 1.8 %project_2.1.refs_4_ = f32[128,4096]{1,0:T(8,128)S(1)} custom-call(s32[7]{0:T(128)S(1)} %concatenate.18.refs_0_.meta, bf16[128,2048]{1,0:T(8,128)(2,1)S(1)} %get-tuple-element.42.context_ref.refs_3_, bf16[256,1024]{1,0:T(8,128)(2,1)} %collective-permute-done.4.refs_0_.refs_6_, bf16[256,1024]{1,0:T(8,128)(2,1)S(1)} %collective-permute-done.7.refs_1_.refs_7_, ...), custom_call_target="tpu_custom_call" | custom-call | flops 536870912 | bytes 8388608 | tf_op jit(solution)/shard_map/project_2/pallas_call | solution.py:460
  72.5 3.8 %grad_2.1 = (bf16[128,2048]{1,0:T(8,128)(2,1)}, bf16[128,256]{1,0:T(8,128)(2,1)S(1)}, bf16[128,256]{1,0:T(8,128)(2,1)S(1)}, bf16[128,256]{1,0:T(8,128)(2,1)S(1)}, bf16[128,256]{1,0:T(8,128)(2,1)S(1)}) custom-call(s32[7]{0:T(128)S(1)} %concatenate.18.refs_0_.meta, bf16[128,4096]{1,0:T(8,128)(2,1)S(1)} %bitcast.20, ...), custom_call_target="tpu_custom_call", output_to_operand_aliasing={{0}: (11, {})} | custom-call | flops 1073741824 | bytes 12582912 | tf_op jit(solution)/shard_map/grad_2/pallas_call | solution.py:422
  76.3 3.3 %collective-permute-done.11.refs_2_.refs_8_ = bf16[256,1024]{1,0:T(8,128)(2,1)S(1)} collective-permute-done((bf16[256,1024]{1,0:T(8,128)(2,1)}, bf16[256,1024]{1,0:T(8,128)(2,1)S(1)}, u32[]{:S(2)}, u32[]{:S(2)}) %collective-permute-start.11) | collective-permute-done | bytes 524320 | tf_op jit(solution)/shard_map/ppermute | solution.py:328
  79.6 10.8 %collective-permute-done.13.refs_4_.refs_10_ = bf16[256,1024]{1,0:T(8,128)(2,1)S(1)} collective-permute-done((bf16[256,1024]{1,0:T(8,128)(2,1)}, bf16[256,1024]{1,0:T(8,128)(2,1)S(1)}, u32[]{:S(2)}, u32[]{:S(2)}) %collective-permute-start.13) | collective-permute-done | bytes 524320 | tf_op jit(solution)/shard_map/ppermute | solution.py:328
  90.4 0.5 collective-permute-start.12
  90.9 0.1 collective-permute-start.14
  91.0 0.4 collective-permute-start.16
  91.4 1.6 %collective-permute-done.18.refs_3_.refs_9_ = bf16[256,2048]{1,0:T(8,128)(2,1)S(1)} collective-permute-done((bf16[256,2048]{1,0:T(8,128)(2,1)S(1)}, bf16[256,2048]{1,0:T(8,128)(2,1)S(1)}, u32[]{:S(2)}, u32[]{:S(2)}) %collective-permute-start.18) | collective-permute-done | bytes 1048608 | tf_op jit(solution)/shard_map/ppermute | solution.py:328
  93.1 3.9 %grad_1.1 = (bf16[128,2048]{1,0:T(8,128)(2,1)}, bf16[128,256]{1,0:T(8,128)(2,1)S(1)}, bf16[128,256]{1,0:T(8,128)(2,1)S(1)}, bf16[128,256]{1,0:T(8,128)(2,1)S(1)}, bf16[128,256]{1,0:T(8,128)(2,1)S(1)}) custom-call(s32[7]{0:T(128)S(1)} %concatenate.18.refs_0_.meta, bf16[128,4096]{1,0:T(8,128)(2,1)S(1)} %bitcast.21, ...), custom_call_target="tpu_custom_call", output_to_operand_aliasing={{0}: (10, {})} | custom-call | flops 1073741824 | bytes 12582912 | tf_op jit(solution)/shard_map/grad_1/pallas_call | solution.py:422
  97.1 3.8 %grad_3.1 = (bf16[128,2048]{1,0:T(8,128)(2,1)}, bf16[128,256]{1,0:T(8,128)(2,1)S(1)}, bf16[128,256]{1,0:T(8,128)(2,1)S(1)}, bf16[128,256]{1,0:T(8,128)(2,1)S(1)}, bf16[128,256]{1,0:T(8,128)(2,1)S(1)}) custom-call(s32[7]{0:T(128)S(1)} %concatenate.18.refs_0_.meta, bf16[128,4096]{1,0:T(8,128)(2,1)S(1)} %bitcast.22, ...), custom_call_target="tpu_custom_call", output_to_operand_aliasing={{0}: (14, {})} | custom-call | flops 1073741824 | bytes 12582912 | tf_op jit(solution)/shard_map/grad_3/pallas_call | solution.py:422
  100.9 1.6 %collective-permute-start.21 = (bf16[128,1024]{1,0:T(8,128)(2,1)S(1)}, bf16[128,1024]{1,0:T(8,128)(2,1)S(1)}, u32[]{:S(2)}, u32[]{:S(2)}) collective-permute-start(bf16[128,1024]{1,0:T(8,128)(2,1)S(1)} %pad_maximum_fusion.3), channel_id=1, source_target_pairs={{0,3},{1,2},{2,1},{3,0},{4,7},{5,6},{6,5},{7,4},{8,11},{9,10},{10,... | collective-permute-start | bytes 786440 | tf_op jit(solution)/shard_map/ppermute | solution.py:328
  102.5 1.5 %collective-permute-start.20 = (bf16[128,1024]{1,0:T(8,128)(2,1)S(1)}, bf16[128,1024]{1,0:T(8,128)(2,1)S(1)}, u32[]{:S(2)}, u32[]{:S(2)}) collective-permute-start(bf16[128,1024]{1,0:T(8,128)(2,1)S(1)} %pad_maximum_fusion.2), channel_id=1, source_target_pairs={{0,2},{1,3},{2,0},{3,1},{4,6},{5,7},{6,4},{7,5},{8,10},{9,11},{10,... | collective-permute-start | bytes 786440 | tf_op jit(solution)/shard_map/ppermute | solution.py:328
  104.0 0.6 collective-permute-start.19
  104.6 2.0 %project_1.1.refs_8_ = f32[128,4096]{1,0:T(8,128)S(1)} custom-call(s32[7]{0:T(128)S(1)} %concatenate.18.refs_0_.meta, bf16[128,2048]{1,0:T(8,128)(2,1)S(1)} %get-tuple-element.42.context_ref.refs_3_, bf16[256,2048]{1,0:T(8,128)(2,1)} %collective-permute-done.6.refs_0_.refs_6_, bf16[256,7168]{1,0:T(8,128)(2,1)S(1)} %collective-permute-done.10.refs_4_.refs_10_.refs_1_.refs_7_, ...), custom_call_target="tpu_custom_call" | custom-call | flops 536870912 | bytes 8388608 | tf_op jit(solution)/shard_map/project_1/pallas_call | solution.py:460
  106.6 2.8 %project_3.1 = bf16[128,4096]{1,0:T(8,128)(2,1)} custom-call(s32[7]{0:T(128)S(1)} %concatenate.18.refs_0_.meta, bf16[128,2048]{1,0:T(8,128)(2,1)S(1)} %get-tuple-element.42.context_ref.refs_3_, bf16[256,1024]{1,0:T(8,128)(2,1)} %collective-permute-done.5.refs_0_.refs_6_, bf16[256,7168]{1,0:T(8,128)(2,1)S(1)} %collective-permute-done.10.refs_4_.refs_10_.refs_1_.refs_7_, ...), custom_call_target="tpu_custom_call" | custom-call | flops 536870912 | bytes 8388608 | tf_op jit(solution)/shard_map/project_3/pallas_call | solution.py:460
  109.4 1.7 %collective-permute-done.21.refs_3_ = bf16[128,1024]{1,0:T(8,128)(2,1)S(1)} collective-permute-done((bf16[128,1024]{1,0:T(8,128)(2,1)S(1)}, bf16[128,1024]{1,0:T(8,128)(2,1)S(1)}, u32[]{:S(2)}, u32[]{:S(2)}) %collective-permute-start.21) | collective-permute-done | bytes 262176 | tf_op jit(solution)/shard_map/ppermute | solution.py:328
  111.0 4.8 %collective-permute-done.20.refs_2_ = bf16[128,1024]{1,0:T(8,128)(2,1)S(1)} collective-permute-done((bf16[128,1024]{1,0:T(8,128)(2,1)S(1)}, bf16[128,1024]{1,0:T(8,128)(2,1)S(1)}, u32[]{:S(2)}, u32[]{:S(2)}) %collective-permute-start.20) | collective-permute-done | bytes 262176 | tf_op jit(solution)/shard_map/ppermute | solution.py:328
  115.8 1.4 %combine_0.1 = bf16[128,1024]{1,0:T(8,128)(2,1)} custom-call(s32[7]{0:T(128)S(1)} %concatenate.18.refs_0_.meta, bf16[128,1024]{1,0:T(8,128)(2,1)S(1)} %pad_maximum_fusion.refs_0_, bf16[128,1024]{1,0:T(8,128)(2,1)S(1)} %collective-permute-done.19.refs_1_, bf16[128,1024]{1,0:T(8,128)(2,1)S(1)} %collective-permute-done.20.refs_2_, ...), custom_call_target="tpu_custom_call" | custom-call | tf_op jit(solution)/shard_map/combine_0/pallas_call | solution.py:537
  (30 shorter events, 0.3 us)
Async XLA Ops:
  0.6 13.4 %copy-start = (bf16[256,4096]{1,0:T(8,128)(2,1)S(1)}, bf16[256,4096]{1,0:T(8,128)(2,1)}, u32[]{:S(2)}) copy-start(bf16[256,4096]{1,0:T(8,128)(2,1)} %refs_6_.1) | copy-start | bytes 6291460
  0.6 16.6 %copy-start.5 = (s32[1,16]{1,0:T(1,128)S(1)}, s32[1,16]{1,0:T(1,128)}, u32[]{:S(2)}) copy-start(s32[1,16]{1,0:T(1,128)} %param.11) | copy-start | bytes 196
  0.7 36.8 %copy-start.6 = (s32[1,4,4]{2,1,0:T(4,128)S(1)}, s32[1,4,4]{2,1,0:T(4,128)}, u32[]{:S(2)}) copy-start(s32[1,4,4]{2,1,0:T(4,128)} %param.12) | copy-start | bytes 196
  0.7 15.0 %collective-permute-start.2 = (bf16[256,4096]{1,0:T(8,128)(2,1)}, bf16[256,4096]{1,0:T(8,128)(2,1)}, u32[]{:S(2)}, u32[]{:S(2)}) collective-permute-start(bf16[256,4096]{1,0:T(8,128)(2,1)} %refs_6_.1), channel_id=1, source_target_pairs={{0,4},{1,5},{2,6},{3,7},{4,0},{5,1},{6,2},{7,3},{8,12},{9,13},{10,... | collective-permute-start | bytes 6291464 | tf_op jit(solution)/shard_map/ppermute | solution.py:328
  2.6 38.8 %copy-start.3 = (bf16[1,128,1024]{2,1,0:T(8,128)(2,1)S(1)}, bf16[1,128,1024]{2,1,0:T(8,128)(2,1)}, u32[]{:S(2)}) copy-start(bf16[1,128,1024]{2,1,0:T(8,128)(2,1)} %param.8) | copy-start | bytes 786436
  6.6 31.3 %collective-permute-start = (bf16[256,1024]{1,0:T(8,128)(2,1)}, bf16[256,1024]{1,0:T(8,128)(2,1)}, u32[]{:S(2)}, u32[]{:S(2)}) collective-permute-start(bf16[256,1024]{1,0:T(8,128)(2,1)} %get-tuple-element.38), channel_id=1, source_target_pairs={{0,1},{1,0},{2,3},{3,2},{4,5},{5,4},{6,7},{7,6},{8,9},{9,8},{10,11... | collective-permute-start | bytes 1572872 | tf_op jit(solution)/shard_map/ppermute | solution.py:328
  9.1 28.8 %collective-permute-start.1 = (bf16[256,1024]{1,0:T(8,128)(2,1)}, bf16[256,1024]{1,0:T(8,128)(2,1)}, u32[]{:S(2)}, u32[]{:S(2)}) collective-permute-start(bf16[256,1024]{1,0:T(8,128)(2,1)} %get-tuple-element.39), channel_id=1, source_target_pairs={{0,2},{1,3},{2,0},{3,1},{4,6},{5,7},{6,4},{7,5},{8,10},{9,11},{10,... | collective-permute-start | bytes 1572872 | tf_op jit(solution)/shard_map/ppermute | solution.py:328
  10.6 26.3 %collective-permute-start.4 = (bf16[256,1024]{1,0:T(8,128)(2,1)}, bf16[256,1024]{1,0:T(8,128)(2,1)}, u32[]{:S(2)}, u32[]{:S(2)}) collective-permute-start(bf16[256,1024]{1,0:T(8,128)(2,1)} %get-tuple-element.43), channel_id=1, source_target_pairs={{0,16},{1,17},{2,18},{3,19},{4,20},{5,21},{6,22},{7,23},{8,24},{9,... | collective-permute-start | bytes 1572872 | tf_op jit(solution)/shard_map/ppermute | solution.py:328
  14.0 31.5 %copy-start.1 = (bf16[1,128,4096]{2,1,0:T(8,128)(2,1)S(1)}, bf16[1,128,4096]{2,1,0:T(8,128)(2,1)}, u32[]{:S(2)}) copy-start(bf16[1,128,4096]{2,1,0:T(8,128)(2,1)} %param.9) | copy-start | bytes 3145732
  15.6 36.6 %collective-permute-start.6 = (bf16[256,2048]{1,0:T(8,128)(2,1)}, bf16[256,2048]{1,0:T(8,128)(2,1)}, u32[]{:S(2)}, u32[]{:S(2)}) collective-permute-start(bf16[256,2048]{1,0:T(8,128)(2,1)} %get-tuple-element.44), channel_id=1, source_target_pairs={{0,8},{1,9},{2,10},{3,11},{4,12},{5,13},{6,14},{7,15},{8,0},{9,1},... | collective-permute-start | bytes 3145736 | tf_op jit(solution)/shard_map/ppermute | solution.py:328
  17.8 20.1 %collective-permute-start.3 = (bf16[256,1024]{1,0:T(8,128)(2,1)}, bf16[256,1024]{1,0:T(8,128)(2,1)}, u32[]{:S(2)}, u32[]{:S(2)}) collective-permute-start(bf16[256,1024]{1,0:T(8,128)(2,1)} %get-tuple-element.41), channel_id=1, source_target_pairs={{0,3},{1,2},{2,1},{3,0},{4,7},{5,6},{6,5},{7,4},{8,11},{9,10},{10,... | collective-permute-start | bytes 1572872 | tf_op jit(solution)/shard_map/ppermute | solution.py:328
  36.9 25.0 %collective-permute-start.5 = (bf16[256,1024]{1,0:T(8,128)(2,1)}, bf16[256,1024]{1,0:T(8,128)(2,1)}, u32[]{:S(2)}, u32[]{:S(2)}) collective-permute-start(bf16[256,1024]{1,0:T(8,128)(2,1)} %collective-permute-done.4.refs_0_.refs_6_), channel_id=1, source_target_pairs={{0,8},{1,9},{2,10},{3,11},{4,12},{5,13},{6,14},{7,15},{8,0},{9,1},... | collective-permute-start | bytes 1572872 | tf_op jit(solution)/shard_map/ppermute | solution.py:328
  37.9 26.2 %collective-permute-start.9 = (bf16[256,1024]{1,0:T(8,128)(2,1)}, bf16[256,1024]{1,0:T(8,128)(2,1)S(1)}, u32[]{:S(2)}, u32[]{:S(2)}) collective-permute-start(bf16[256,1024]{1,0:T(8,128)(2,1)} %collective-permute-done.4.refs_0_.refs_6_), channel_id=1, source_target_pairs={{0,3},{1,2},{2,1},{3,0},{4,7},{5,6},{6,5},{7,4},{8,11},{9,10},{10,... | collective-permute-start | bytes 1572872 | tf_op jit(solution)/shard_map/ppermute | solution.py:328
  38.5 25.6 %collective-permute-start.7 = (bf16[256,1024]{1,0:T(8,128)(2,1)}, bf16[256,1024]{1,0:T(8,128)(2,1)S(1)}, u32[]{:S(2)}, u32[]{:S(2)}) collective-permute-start(bf16[256,1024]{1,0:T(8,128)(2,1)} %collective-permute-done.4.refs_0_.refs_6_), channel_id=1, source_target_pairs={{0,1},{1,0},{2,3},{3,2},{4,5},{5,4},{6,7},{7,6},{8,9},{9,8},{10,11... | collective-permute-start | bytes 1572872 | tf_op jit(solution)/shard_map/ppermute | solution.py:328
  40.0 24.2 %collective-permute-start.8 = (bf16[256,1024]{1,0:T(8,128)(2,1)}, bf16[256,1024]{1,0:T(8,128)(2,1)S(1)}, u32[]{:S(2)}, u32[]{:S(2)}) collective-permute-start(bf16[256,1024]{1,0:T(8,128)(2,1)} %collective-permute-done.4.refs_0_.refs_6_), channel_id=1, source_target_pairs={{0,2},{1,3},{2,0},{3,1},{4,6},{5,7},{6,4},{7,5},{8,10},{9,11},{10,... | collective-permute-start | bytes 1572872 | tf_op jit(solution)/shard_map/ppermute | solution.py:328
  41.5 1.0 copy-start.2
  52.1 12.2 %copy-start.4 = (bf16[256,2048]{1,0:T(8,128)(2,1)S(1)}, bf16[256,2048]{1,0:T(8,128)(2,1)}, u32[]{:S(2)}) copy-start(bf16[256,2048]{1,0:T(8,128)(2,1)} %get-tuple-element.52) | copy-start | bytes 3145732
  64.3 6.5 %collective-permute-start.10 = (bf16[256,7168]{1,0:T(8,128)(2,1)S(1)}, bf16[256,7168]{1,0:T(8,128)(2,1)S(1)}, u32[]{:S(2)}, u32[]{:S(2)}) collective-permute-start(bf16[256,7168]{1,0:T(8,128)(2,1)S(1)} %constant_dynamic-update-slice_fusion), channel_id=1, source_target_pairs={{0,4},{1,5},{2,6},{3,7},{4,0},{5,1},{6,2},{7,3},{8,12},{9,13},{10,... | collective-permute-start | bytes 11010056 | tf_op jit(solution)/shard_map/ppermute | solution.py:328
  64.4 26.1 %collective-permute-start.17 = (bf16[256,2048]{1,0:T(8,128)(2,1)S(1)}, bf16[256,2048]{1,0:T(8,128)(2,1)S(1)}, u32[]{:S(2)}, u32[]{:S(2)}) collective-permute-start(bf16[256,2048]{1,0:T(8,128)(2,1)S(1)} %copy-done.4), channel_id=1, source_target_pairs={{0,8},{1,9},{2,10},{3,11},{4,12},{5,13},{6,14},{7,15},{8,0},{9,1},... | collective-permute-start | bytes 3145736 | tf_op jit(solution)/shard_map/ppermute | solution.py:328
  64.6 15.0 %collective-permute-start.11 = (bf16[256,1024]{1,0:T(8,128)(2,1)}, bf16[256,1024]{1,0:T(8,128)(2,1)S(1)}, u32[]{:S(2)}, u32[]{:S(2)}) collective-permute-start(bf16[256,1024]{1,0:T(8,128)(2,1)} %collective-permute-done.5.refs_0_.refs_6_), channel_id=1, source_target_pairs={{0,1},{1,0},{2,3},{3,2},{4,5},{5,4},{6,7},{7,6},{8,9},{9,8},{10,11... | collective-permute-start | bytes 1572872 | tf_op jit(solution)/shard_map/ppermute | solution.py:328
  65.2 25.2 %collective-permute-start.13 = (bf16[256,1024]{1,0:T(8,128)(2,1)}, bf16[256,1024]{1,0:T(8,128)(2,1)S(1)}, u32[]{:S(2)}, u32[]{:S(2)}) collective-permute-start(bf16[256,1024]{1,0:T(8,128)(2,1)} %collective-permute-done.5.refs_0_.refs_6_), channel_id=1, source_target_pairs={{0,2},{1,3},{2,0},{3,1},{4,6},{5,7},{6,4},{7,5},{8,10},{9,11},{10,... | collective-permute-start | bytes 1572872 | tf_op jit(solution)/shard_map/ppermute | solution.py:328
  65.9 24.5 %collective-permute-start.15 = (bf16[256,1024]{1,0:T(8,128)(2,1)}, bf16[256,1024]{1,0:T(8,128)(2,1)S(1)}, u32[]{:S(2)}, u32[]{:S(2)}) collective-permute-start(bf16[256,1024]{1,0:T(8,128)(2,1)} %collective-permute-done.5.refs_0_.refs_6_), channel_id=1, source_target_pairs={{0,3},{1,2},{2,1},{3,0},{4,7},{5,6},{6,5},{7,4},{8,11},{9,10},{10,... | collective-permute-start | bytes 1572872 | tf_op jit(solution)/shard_map/ppermute | solution.py:328
  90.4 2.7 %collective-permute-start.18 = (bf16[256,2048]{1,0:T(8,128)(2,1)S(1)}, bf16[256,2048]{1,0:T(8,128)(2,1)S(1)}, u32[]{:S(2)}, u32[]{:S(2)}) collective-permute-start(bf16[256,2048]{1,0:T(8,128)(2,1)S(1)} %collective-permute-done.17.refs_2_.refs_8_), channel_id=1, source_target_pairs={{0,4},{1,5},{2,6},{3,7},{4,0},{5,1},{6,2},{7,3},{8,12},{9,13},{10,... | collective-permute-start | bytes 3145736 | tf_op jit(solution)/shard_map/ppermute | solution.py:328
  90.4 6.6 %collective-permute-start.12 = (bf16[256,1024]{1,0:T(8,128)(2,1)S(1)}, bf16[256,1024]{1,0:T(8,128)(2,1)S(1)}, u32[]{:S(2)}, u32[]{:S(2)}) collective-permute-start(bf16[256,1024]{1,0:T(8,128)(2,1)S(1)} %collective-permute-done.11.refs_2_.refs_8_), channel_id=1, source_target_pairs={{0,4},{1,5},{2,6},{3,7},{4,0},{5,1},{6,2},{7,3},{8,12},{9,13},{10,... | collective-permute-start | bytes 1572872 | tf_op jit(solution)/shard_map/ppermute | solution.py:328
  90.9 6.1 %collective-permute-start.14 = (bf16[256,1024]{1,0:T(8,128)(2,1)S(1)}, bf16[256,1024]{1,0:T(8,128)(2,1)S(1)}, u32[]{:S(2)}, u32[]{:S(2)}) collective-permute-start(bf16[256,1024]{1,0:T(8,128)(2,1)S(1)} %collective-permute-done.13.refs_4_.refs_10_), channel_id=1, source_target_pairs={{0,4},{1,5},{2,6},{3,7},{4,0},{5,1},{6,2},{7,3},{8,12},{9,13},{10,... | collective-permute-start | bytes 1572872 | tf_op jit(solution)/shard_map/ppermute | solution.py:328
  91.0 6.1 %collective-permute-start.16 = (bf16[256,1024]{1,0:T(8,128)(2,1)S(1)}, bf16[256,1024]{1,0:T(8,128)(2,1)S(1)}, u32[]{:S(2)}, u32[]{:S(2)}) collective-permute-start(bf16[256,1024]{1,0:T(8,128)(2,1)S(1)} %collective-permute-done.15.refs_6_.refs_12_), channel_id=1, source_target_pairs={{0,4},{1,5},{2,6},{3,7},{4,0},{5,1},{6,2},{7,3},{8,12},{9,13},{10,... | collective-permute-start | bytes 1572872 | tf_op jit(solution)/shard_map/ppermute | solution.py:328
  100.9 10.2 %collective-permute-start.21 = (bf16[128,1024]{1,0:T(8,128)(2,1)S(1)}, bf16[128,1024]{1,0:T(8,128)(2,1)S(1)}, u32[]{:S(2)}, u32[]{:S(2)}) collective-permute-start(bf16[128,1024]{1,0:T(8,128)(2,1)S(1)} %pad_maximum_fusion.3), channel_id=1, source_target_pairs={{0,3},{1,2},{2,1},{3,0},{4,7},{5,6},{6,5},{7,4},{8,11},{9,10},{10,... | collective-permute-start | bytes 786440 | tf_op jit(solution)/shard_map/ppermute | solution.py:328
  102.5 13.3 %collective-permute-start.20 = (bf16[128,1024]{1,0:T(8,128)(2,1)S(1)}, bf16[128,1024]{1,0:T(8,128)(2,1)S(1)}, u32[]{:S(2)}, u32[]{:S(2)}) collective-permute-start(bf16[128,1024]{1,0:T(8,128)(2,1)S(1)} %pad_maximum_fusion.2), channel_id=1, source_target_pairs={{0,2},{1,3},{2,0},{3,1},{4,6},{5,7},{6,4},{7,5},{8,10},{9,11},{10,... | collective-permute-start | bytes 786440 | tf_op jit(solution)/shard_map/ppermute | solution.py:328
  104.0 11.8 %collective-permute-start.19 = (bf16[128,1024]{1,0:T(8,128)(2,1)S(1)}, bf16[128,1024]{1,0:T(8,128)(2,1)S(1)}, u32[]{:S(2)}, u32[]{:S(2)}) collective-permute-start(bf16[128,1024]{1,0:T(8,128)(2,1)S(1)} %pad_maximum_fusion.1), channel_id=1, source_target_pairs={{0,1},{1,0},{2,3},{3,2},{4,5},{5,4},{6,7},{7,6},{8,9},{9,8},{10,11... | collective-permute-start | bytes 786440 | tf_op jit(solution)/shard_map/ppermute | solution.py:328

commit v5 on v4

--- a/solution.py
+++ b/solution.py
@@ -512,15 +512,13 @@
             parts_3 += [own(threes[t], columns[t]), other(to_core(threes[t]), columns[t])]
         q_grad, mine_1 = grad_step(1, parts_1, q_grad)
         q_grad, mine_3 = grad_step(3, parts_3, q_grad)
-        late = send_shares(
-            [
-                jnp.concatenate([mine_0[t], mine_2[t], mine_1[t], mine_3[t]], axis=1)
-                for t in range(groups)
-            ]
+        early = send_shares(
+            [jnp.concatenate([mine_0[t], mine_2[t], mine_1[t]], axis=1) for t in range(groups)]
         )
+        late = send_shares(mine_3)
         total = project_step(1, parts_1, total, False)
         total = project_step(3, parts_3, total, True)
-        batches_of_shares = [((0, 2, 1, 3), late)]
+        batches_of_shares = [((0, 2, 1), early), ((3,), late)]
     else:
         full = lax.all_gather(out_proj, "dp", axis=0, tiled=True)
         batches_of_shares = []

time: 118 us -> 116 us (0.983)
  waiting for transfers between devices: 51.7 us -> 45.1 us
  starting transfers between devices: 21.9 us -> 25.6 us
    ppermute x22 -> x25, waiting for transfers between devices: 51.7 us -> 45.1 us  [move(): return lax.ppermute(block, ('dp', 'ctx'), pairs)]
    ppermute x22 -> x25, starting transfers between devices: 21.9 us -> 25.6 us  [move(): return lax.ppermute(block, ('dp', 'ctx'), pairs)]
    pallas_call x1 -> x2, Pallas kernels: 1.43 us -> 2.58 us  [on_device(): pl.pallas_call(functools.partial(combine_kernel, len(share), order, swapp...]
  transfers between devices with their start and end apart: 22 -> 25, of which waited for: 9 -> 6; matrix products, arithmetic and copies ran while one was open for 7% -> 7% of each run, Pallas kernels for 24% -> 28%
where the time goes in v5:
time: 116 us; the launch traced here: 115 us
  waiting for transfers between devices  45.1 us (39%)
  Pallas kernels  34.1 us (29%)
  starting transfers between devices  25.6 us (22%)
  local copies, waits for them, and re-layouts  8.85 us (8%)
    ppermute x25, waiting for transfers between devices, move(): return lax.ppermute(block, ('dp', 'ctx'), pairs)  45.1 us
    ppermute x25, starting transfers between devices, move(): return lax.ppermute(block, ('dp', 'ctx'), pairs)  25.6 us
    pallas_call x4, Pallas kernels, grad_step(): pl.pallas_call(functools.partial(grad_kernel, *sizes, slot, swapped, plan...  15.8 us
    pallas_call x4, Pallas kernels, project_step(): pl.pallas_call(functools.partial(project_kernel, slot, swapped, plan, fir...  8.79 us
    unnamed x20, local copies, waits for them, and re-layouts  6.14 us
    pallas_call x1, Pallas kernels, on_device(): pl.pallas_call(functools.partial(pack_kernel, groups, unit_count, rows, f...  3.93 us
    pallas_call x1, Pallas kernels, on_device(): pl.pallas_call(functools.partial(forward_kernel, *sizes, fold), out_shape...  3.07 us
    pallas_call x2, Pallas kernels, on_device(): pl.pallas_call(functools.partial(combine_kernel, len(share), order, swapp...  2.58 us
  transfers between devices with their start and end apart: 25, of which 6 were waited for; matrix products, arithmetic and copies ran while one was open for 7% of the time, Pallas kernels for 28%

profile of v5, /device:TPU:0, one launch (start us, length us, event | category | flops | bytes accessed | tf_op | source)
XLA Modules:
  0.0 115.5 jit_solution(2192756952701440597)
XLA Ops:
  0.6 0.0 copy-start
  0.7 0.5 collective-permute-start.2
  1.2 1.4 %copy.20.routes = s32[1,4,2]{2,1,0:T(4,128)} copy(s32[1,4,2]{1,2,0:T(2,128)} %param.13) | data formatting | bytes 64 | tf_op args[6]
  2.6 3.9 %pack.1 = (bf16[256,1024]{1,0:T(8,128)(2,1)}, bf16[256,1024]{1,0:T(8,128)(2,1)}, bf16[256,1024]{1,0:T(8,128)(2,1)}, bf16[256,1024]{1,0:T(8,128)(2,1)}) custom-call(s32[1,4,2]{2,1,0:T(4,128)} %copy.20.routes, bf16[128,2048]{1,0:T(8,128)(2,1)} %bitcast.23, bf16[128,1024]{1,0:T(8,128)(2,1)} %bitcast.25, bf16[256,4096]{1,0:T(8,128)(2,1)} %refs_6_.1), custom_call_target="tpu_custom_call" | custom-call | tf_op jit(solution)/shard_map/pack/pallas_call | solution.py:353
  6.6 2.6 %collective-permute-start = (bf16[256,1024]{1,0:T(8,128)(2,1)}, bf16[256,1024]{1,0:T(8,128)(2,1)}, u32[]{:S(2)}, u32[]{:S(2)}) collective-permute-start(bf16[256,1024]{1,0:T(8,128)(2,1)} %get-tuple-element.38), channel_id=1, source_target_pairs={{0,1},{1,0},{2,3},{3,2},{4,5},{5,4},{6,7},{7,6},{8,9},{9,8},{10,11... | collective-permute-start | bytes 1572872 | tf_op jit(solution)/shard_map/ppermute | solution.py:328
  9.2 1.5 %collective-permute-start.1 = (bf16[256,1024]{1,0:T(8,128)(2,1)}, bf16[256,1024]{1,0:T(8,128)(2,1)}, u32[]{:S(2)}, u32[]{:S(2)}) collective-permute-start(bf16[256,1024]{1,0:T(8,128)(2,1)} %get-tuple-element.39), channel_id=1, source_target_pairs={{0,2},{1,3},{2,0},{3,1},{4,6},{5,7},{6,4},{7,5},{8,10},{9,11},{10,... | collective-permute-start | bytes 1572872 | tf_op jit(solution)/shard_map/ppermute | solution.py:328
  10.7 2.7 %collective-permute-start.4 = (bf16[256,1024]{1,0:T(8,128)(2,1)}, bf16[256,1024]{1,0:T(8,128)(2,1)}, u32[]{:S(2)}, u32[]{:S(2)}) collective-permute-start(bf16[256,1024]{1,0:T(8,128)(2,1)} %get-tuple-element.43), channel_id=1, source_target_pairs={{0,16},{1,17},{2,18},{3,19},{4,20},{5,21},{6,22},{7,23},{8,24},{9,... | collective-permute-start | bytes 1572872 | tf_op jit(solution)/shard_map/ppermute | solution.py:328
  13.3 0.8 slice_reduce_fusion.1
  14.1 0.0 copy-start.1
  14.2 1.4 %fusion.17 = (bf16[256,2048]{1,0:T(8,128)(2,1)}, bf16[256,2048]{1,0:T(8,128)(2,1)}) fusion(bf16[256,4096]{1,0:T(8,128)(2,1)S(1)} %copy-done), kind=kLoop, calls=%fused_computation.42 | loop fusion | bytes 4194304 | tf_op jit(solution)/shard_map/slice | solution.py:493
  15.6 1.5 %collective-permute-start.6 = (bf16[256,2048]{1,0:T(8,128)(2,1)}, bf16[256,2048]{1,0:T(8,128)(2,1)}, u32[]{:S(2)}, u32[]{:S(2)}) collective-permute-start(bf16[256,2048]{1,0:T(8,128)(2,1)} %get-tuple-element.44), channel_id=1, source_target_pairs={{0,8},{1,9},{2,10},{3,11},{4,12},{5,13},{6,14},{7,15},{8,0},{9,1},... | collective-permute-start | bytes 3145736 | tf_op jit(solution)/shard_map/ppermute | solution.py:328
  17.1 0.1 and_select_fusion.1
  17.2 0.1 copy.19
  17.3 0.1 add.101
  17.4 0.1 slice_reduce_fusion
  17.5 0.1 convert_reduce_fusion.1
  17.6 0.1 eq.49
  17.7 0.5 collective-permute-start.3
  18.2 0.1 and_select_fusion
  18.3 0.1 convert_reduce_fusion
  18.3 18.5 %collective-permute-done.4.refs_0_.refs_6_ = bf16[256,1024]{1,0:T(8,128)(2,1)} collective-permute-done((bf16[256,1024]{1,0:T(8,128)(2,1)}, bf16[256,1024]{1,0:T(8,128)(2,1)}, u32[]{:S(2)}, u32[]{:S(2)}) %collective-permute-start.4) | collective-permute-done | bytes 524320 | tf_op jit(solution)/shard_map/ppermute | solution.py:328
  36.9 0.7 collective-permute-start.5
  37.5 0.4 fusion.2.refs_1_
  37.9 0.1 concatenate.18.refs_0_.meta
  38.0 0.0 collective-permute-done.refs_4_
  38.0 0.0 collective-permute-done.1.refs_5_
  38.0 0.6 collective-permute-start.9
  38.6 1.5 %collective-permute-start.7 = (bf16[256,1024]{1,0:T(8,128)(2,1)}, bf16[256,1024]{1,0:T(8,128)(2,1)S(1)}, u32[]{:S(2)}, u32[]{:S(2)}) collective-permute-start(bf16[256,1024]{1,0:T(8,128)(2,1)} %collective-permute-done.4.refs_0_.refs_6_), channel_id=1, source_target_pairs={{0,1},{1,0},{2,3},{3,2},{4,5},{5,4},{6,7},{7,6},{8,9},{9,8},{10,11... | collective-permute-start | bytes 1572872 | tf_op jit(solution)/shard_map/ppermute | solution.py:328
  40.1 1.5 %collective-permute-start.8 = (bf16[256,1024]{1,0:T(8,128)(2,1)}, bf16[256,1024]{1,0:T(8,128)(2,1)S(1)}, u32[]{:S(2)}, u32[]{:S(2)}) collective-permute-start(bf16[256,1024]{1,0:T(8,128)(2,1)} %collective-permute-done.4.refs_0_.refs_6_), channel_id=1, source_target_pairs={{0,2},{1,3},{2,0},{3,1},{4,6},{5,7},{6,4},{7,5},{8,10},{9,11},{10,... | collective-permute-start | bytes 1572872 | tf_op jit(solution)/shard_map/ppermute | solution.py:328
  41.6 1.0 copy-done.2
  42.6 3.1 %forward.1 = (bf16[128,2048]{1,0:T(8,128)(2,1)S(1)}, f32[4,2,256,128]{3,2,1,0:T(8,128)S(1)}, bf16[2,128,1024]{2,1,0:T(8,128)(2,1)S(1)}, bf16[128,2048]{1,0:T(8,128)(2,1)S(1)}) custom-call(s32[7]{0:T(128)S(1)} %concatenate.18.refs_0_.meta, f32[2,64,128]{2,1,0:T(8,128)S(1)} %fusion.2.refs_1_, bf16[128,2048]{1,0:T(8,128)(2,1)S(1)} %bitcast.24, ...), custom_call_target="tpu_custom_call" | custom-call | flops 1073741824 | bytes 8388608 | tf_op jit(solution)/shard_map/forward/pallas_call | solution.py:382
  45.7 4.3 %grad_0.1 = (bf16[128,2048]{1,0:T(8,128)(2,1)}, bf16[128,256]{1,0:T(8,128)(2,1)S(1)}, bf16[128,256]{1,0:T(8,128)(2,1)S(1)}, bf16[128,256]{1,0:T(8,128)(2,1)S(1)}, bf16[128,256]{1,0:T(8,128)(2,1)S(1)}) custom-call(s32[7]{0:T(128)S(1)} %concatenate.18.refs_0_.meta, bf16[128,4096]{1,0:T(8,128)(2,1)S(1)} %bitcast.19, ...), custom_call_target="tpu_custom_call" | custom-call | flops 1073741824 | bytes 12582912 | tf_op jit(solution)/shard_map/grad_0/pallas_call | solution.py:422
  50.0 2.3 %project_0.1.refs_5_ = f32[128,4096]{1,0:T(8,128)S(1)} custom-call(s32[7]{0:T(128)S(1)} %concatenate.18.refs_0_.meta, bf16[128,2048]{1,0:T(8,128)(2,1)S(1)} %get-tuple-element.42.context_ref.refs_3_, bf16[256,4096]{1,0:T(8,128)(2,1)S(1)} %copy-done, bf16[256,4096]{1,0:T(8,128)(2,1)} %collective-permute-done.2.refs_1_.refs_7_), custom_call_target="tpu_custom_call" | custom-call | flops 536870912 | bytes 8388608 | tf_op jit(solution)/shard_map/project_0/pallas_call | solution.py:460
  52.3 0.0 copy-start.4
  52.4 1.4 %constant_dynamic-update-slice_fusion.5 = bf16[256,7168]{1,0:T(8,128)(2,1)S(1)} fusion(bf16[256,2048]{1,0:T(8,128)(2,1)} %collective-permute-done.6.refs_0_.refs_6_), kind=kLoop, calls=%fused_computation.15 | loop fusion | bytes 2097152
  53.8 8.1 %collective-permute-done.5.refs_0_.refs_6_ = bf16[256,1024]{1,0:T(8,128)(2,1)} collective-permute-done((bf16[256,1024]{1,0:T(8,128)(2,1)}, bf16[256,1024]{1,0:T(8,128)(2,1)}, u32[]{:S(2)}, u32[]{:S(2)}) %collective-permute-start.5) | collective-permute-done | bytes 524320 | tf_op jit(solution)/shard_map/ppermute | solution.py:328
  61.9 1.1 constant_dynamic-update-slice_fusion.4
  63.0 1.1 constant_dynamic-update-slice_fusion.3
  64.2 0.1 collective-permute-start.10
  64.3 0.2 collective-permute-start.17
  64.6 0.5 collective-permute-start.11
  65.1 0.8 collective-permute-start.13
  65.8 2.2 %collective-permute-start.15 = (bf16[256,1024]{1,0:T(8,128)(2,1)}, bf16[256,1024]{1,0:T(8,128)(2,1)S(1)}, u32[]{:S(2)}, u32[]{:S(2)}) collective-permute-start(bf16[256,1024]{1,0:T(8,128)(2,1)} %collective-permute-done.5.refs_0_.refs_6_), channel_id=1, source_target_pairs={{0,3},{1,2},{2,1},{3,0},{4,7},{5,6},{6,5},{7,4},{8,11},{9,10},{10,... | collective-permute-start | bytes 1572872 | tf_op jit(solution)/shard_map/ppermute | solution.py:328
  68.0 2.6 %collective-permute-done.10.refs_4_.refs_10_.refs_1_.refs_7_ = bf16[256,7168]{1,0:T(8,128)(2,1)S(1)} collective-permute-done((bf16[256,7168]{1,0:T(8,128)(2,1)S(1)}, bf16[256,7168]{1,0:T(8,128)(2,1)S(1)}, u32[]{:S(2)}, u32[]{:S(2)}) %collective-permute-start.10) | collective-permute-done | bytes 3670048 | tf_op jit(solution)/shard_map/ppermute | solution.py:328
  70.7 1.8 %project_2.1.refs_4_ = f32[128,4096]{1,0:T(8,128)S(1)} custom-call(s32[7]{0:T(128)S(1)} %concatenate.18.refs_0_.meta, bf16[128,2048]{1,0:T(8,128)(2,1)S(1)} %get-tuple-element.42.context_ref.refs_3_, bf16[256,1024]{1,0:T(8,128)(2,1)} %collective-permute-done.4.refs_0_.refs_6_, bf16[256,1024]{1,0:T(8,128)(2,1)S(1)} %collective-permute-done.7.refs_1_.refs_7_, ...), custom_call_target="tpu_custom_call" | custom-call | flops 536870912 | bytes 8388608 | tf_op jit(solution)/shard_map/project_2/pallas_call | solution.py:460
  72.5 3.8 %grad_2.1 = (bf16[128,2048]{1,0:T(8,128)(2,1)}, bf16[128,256]{1,0:T(8,128)(2,1)S(1)}, bf16[128,256]{1,0:T(8,128)(2,1)S(1)}, bf16[128,256]{1,0:T(8,128)(2,1)S(1)}, bf16[128,256]{1,0:T(8,128)(2,1)S(1)}) custom-call(s32[7]{0:T(128)S(1)} %concatenate.18.refs_0_.meta, bf16[128,4096]{1,0:T(8,128)(2,1)S(1)} %bitcast.20, ...), custom_call_target="tpu_custom_call", output_to_operand_aliasing={{0}: (11, {})} | custom-call | flops 1073741824 | bytes 12582912 | tf_op jit(solution)/shard_map/grad_2/pallas_call | solution.py:422
  76.2 3.3 %collective-permute-done.11.refs_2_.refs_8_ = bf16[256,1024]{1,0:T(8,128)(2,1)S(1)} collective-permute-done((bf16[256,1024]{1,0:T(8,128)(2,1)}, bf16[256,1024]{1,0:T(8,128)(2,1)S(1)}, u32[]{:S(2)}, u32[]{:S(2)}) %collective-permute-start.11) | collective-permute-done | bytes 524320 | tf_op jit(solution)/shard_map/ppermute | solution.py:328
  79.5 10.8 %collective-permute-done.13.refs_4_.refs_10_ = bf16[256,1024]{1,0:T(8,128)(2,1)S(1)} collective-permute-done((bf16[256,1024]{1,0:T(8,128)(2,1)}, bf16[256,1024]{1,0:T(8,128)(2,1)S(1)}, u32[]{:S(2)}, u32[]{:S(2)}) %collective-permute-start.13) | collective-permute-done | bytes 524320 | tf_op jit(solution)/shard_map/ppermute | solution.py:328
  90.3 0.5 collective-permute-start.12
  90.9 0.1 collective-permute-start.14
  90.9 0.4 collective-permute-start.16
  91.4 1.6 %collective-permute-done.18.refs_3_.refs_9_ = bf16[256,2048]{1,0:T(8,128)(2,1)S(1)} collective-permute-done((bf16[256,2048]{1,0:T(8,128)(2,1)S(1)}, bf16[256,2048]{1,0:T(8,128)(2,1)S(1)}, u32[]{:S(2)}, u32[]{:S(2)}) %collective-permute-start.18) | collective-permute-done | bytes 1048608 | tf_op jit(solution)/shard_map/ppermute | solution.py:328
  93.0 3.9 %grad_1.1 = (bf16[128,2048]{1,0:T(8,128)(2,1)}, bf16[128,256]{1,0:T(8,128)(2,1)S(1)}, bf16[128,256]{1,0:T(8,128)(2,1)S(1)}, bf16[128,256]{1,0:T(8,128)(2,1)S(1)}, bf16[128,256]{1,0:T(8,128)(2,1)S(1)}) custom-call(s32[7]{0:T(128)S(1)} %concatenate.18.refs_0_.meta, bf16[128,4096]{1,0:T(8,128)(2,1)S(1)} %bitcast.21, ...), custom_call_target="tpu_custom_call", output_to_operand_aliasing={{0}: (10, {})} | custom-call | flops 1073741824 | bytes 12582912 | tf_op jit(solution)/shard_map/grad_1/pallas_call | solution.py:422
  97.0 1.6 %collective-permute-start.24 = (bf16[128,768]{1,0:T(8,128)(2,1)S(1)}, bf16[128,768]{1,0:T(8,128)(2,1)S(1)}, u32[]{:S(2)}, u32[]{:S(2)}) collective-permute-start(bf16[128,768]{1,0:T(8,128)(2,1)S(1)} %pad_maximum_fusion.3), channel_id=1, source_target_pairs={{0,3},{1,2},{2,1},{3,0},{4,7},{5,6},{6,5},{7,4},{8,11},{9,10},{10,... | collective-permute-start | bytes 589832 | tf_op jit(solution)/shard_map/ppermute | solution.py:328
  98.6 1.5 %collective-permute-start.23 = (bf16[128,768]{1,0:T(8,128)(2,1)S(1)}, bf16[128,768]{1,0:T(8,128)(2,1)S(1)}, u32[]{:S(2)}, u32[]{:S(2)}) collective-permute-start(bf16[128,768]{1,0:T(8,128)(2,1)S(1)} %pad_maximum_fusion.2), channel_id=1, source_target_pairs={{0,2},{1,3},{2,0},{3,1},{4,6},{5,7},{6,4},{7,5},{8,10},{9,11},{10,... | collective-permute-start | bytes 589832 | tf_op jit(solution)/shard_map/ppermute | solution.py:328
  100.1 0.6 collective-permute-start.22
  100.7 3.8 %grad_3.1 = (bf16[128,2048]{1,0:T(8,128)(2,1)}, bf16[128,256]{1,0:T(8,128)(2,1)S(1)}, bf16[128,256]{1,0:T(8,128)(2,1)S(1)}, bf16[128,256]{1,0:T(8,128)(2,1)S(1)}, bf16[128,256]{1,0:T(8,128)(2,1)S(1)}) custom-call(s32[7]{0:T(128)S(1)} %concatenate.18.refs_0_.meta, bf16[128,4096]{1,0:T(8,128)(2,1)S(1)} %bitcast.22, ...), custom_call_target="tpu_custom_call", output_to_operand_aliasing={{0}: (14, {})} | custom-call | flops 1073741824 | bytes 12582912 | tf_op jit(solution)/shard_map/grad_3/pallas_call | solution.py:422
  104.5 1.6 %collective-permute-start.19 = (bf16[128,256]{1,0:T(8,128)(2,1)S(1)}, bf16[128,256]{1,0:T(8,128)(2,1)S(1)}, u32[]{:S(2)}, u32[]{:S(2)}) collective-permute-start(bf16[128,256]{1,0:T(8,128)(2,1)S(1)} %get-tuple-element.60), channel_id=1, source_target_pairs={{0,1},{1,0},{2,3},{3,2},{4,5},{5,4},{6,7},{7,6},{8,9},{9,8},{10,11... | collective-permute-start | bytes 196616 | tf_op jit(solution)/shard_map/ppermute | solution.py:328
  106.0 0.6 collective-permute-start.20
  106.6 1.5 %collective-permute-start.21 = (bf16[128,256]{1,0:T(8,128)(2,1)S(1)}, bf16[128,256]{1,0:T(8,128)(2,1)S(1)}, u32[]{:S(2)}, u32[]{:S(2)}) collective-permute-start(bf16[128,256]{1,0:T(8,128)(2,1)S(1)} %get-tuple-element.62), channel_id=1, source_target_pairs={{0,3},{1,2},{2,1},{3,0},{4,7},{5,6},{6,5},{7,4},{8,11},{9,10},{10,... | collective-permute-start | bytes 196616 | tf_op jit(solution)/shard_map/ppermute | solution.py:328
  108.1 2.0 %project_1.1.refs_8_ = f32[128,4096]{1,0:T(8,128)S(1)} custom-call(s32[7]{0:T(128)S(1)} %concatenate.18.refs_0_.meta, bf16[128,2048]{1,0:T(8,128)(2,1)S(1)} %get-tuple-element.42.context_ref.refs_3_, bf16[256,2048]{1,0:T(8,128)(2,1)} %collective-permute-done.6.refs_0_.refs_6_, bf16[256,7168]{1,0:T(8,128)(2,1)S(1)} %collective-permute-done.10.refs_4_.refs_10_.refs_1_.refs_7_, ...), custom_call_target="tpu_custom_call" | custom-call | flops 536870912 | bytes 8388608 | tf_op jit(solution)/shard_map/project_1/pallas_call | solution.py:460
  110.1 2.8 %project_3.1 = bf16[128,4096]{1,0:T(8,128)(2,1)} custom-call(s32[7]{0:T(128)S(1)} %concatenate.18.refs_0_.meta, bf16[128,2048]{1,0:T(8,128)(2,1)S(1)} %get-tuple-element.42.context_ref.refs_3_, bf16[256,1024]{1,0:T(8,128)(2,1)} %collective-permute-done.5.refs_0_.refs_6_, bf16[256,7168]{1,0:T(8,128)(2,1)S(1)} %collective-permute-done.10.refs_4_.refs_10_.refs_1_.refs_7_, ...), custom_call_target="tpu_custom_call" | custom-call | flops 536870912 | bytes 8388608 | tf_op jit(solution)/shard_map/project_3/pallas_call | solution.py:460
  112.8 1.4 %combine_0.1.refs_4_ = bf16[128,1024]{1,0:T(8,128)(2,1)} custom-call(s32[7]{0:T(128)S(1)} %concatenate.18.refs_0_.meta, bf16[128,768]{1,0:T(8,128)(2,1)S(1)} %pad_maximum_fusion.refs_0_, bf16[128,768]{1,0:T(8,128)(2,1)S(1)} %collective-permute-done.22.refs_1_, bf16[128,768]{1,0:T(8,128)(2,1)S(1)} %collective-permute-done.23.refs_2_, ...), custom_call_target="tpu_custom_call" | custom-call | tf_op jit(solution)/shard_map/combine_0/pallas_call | solution.py:535
  114.2 1.2 %combine_3.1 = bf16[128,1024]{1,0:T(8,128)(2,1)} custom-call(s32[7]{0:T(128)S(1)} %concatenate.18.refs_0_.meta, bf16[128,256]{1,0:T(8,128)(2,1)S(1)} %get-tuple-element.59.refs_0_, bf16[128,256]{1,0:T(8,128)(2,1)S(1)} %collective-permute-done.19.refs_1_, bf16[128,256]{1,0:T(8,128)(2,1)S(1)} %collective-permute-done.20.refs_2_, ...), custom_call_target="tpu_custom_call", output_to_operand_aliasing={{}: (5, {})} | custom-call | tf_op jit(solution)/shard_map/combine_3/pallas_call | solution.py:535
  (37 shorter events, 0.3 us)
Async XLA Ops:
  0.6 13.5 %copy-start = (bf16[256,4096]{1,0:T(8,128)(2,1)S(1)}, bf16[256,4096]{1,0:T(8,128)(2,1)}, u32[]{:S(2)}) copy-start(bf16[256,4096]{1,0:T(8,128)(2,1)} %refs_6_.1) | copy-start | bytes 6291460
  0.6 16.5 %copy-start.5 = (s32[1,16]{1,0:T(1,128)S(1)}, s32[1,16]{1,0:T(1,128)}, u32[]{:S(2)}) copy-start(s32[1,16]{1,0:T(1,128)} %param.11) | copy-start | bytes 196
  0.7 36.9 %copy-start.6 = (s32[1,4,4]{2,1,0:T(4,128)S(1)}, s32[1,4,4]{2,1,0:T(4,128)}, u32[]{:S(2)}) copy-start(s32[1,4,4]{2,1,0:T(4,128)} %param.12) | copy-start | bytes 196
  0.7 14.9 %collective-permute-start.2 = (bf16[256,4096]{1,0:T(8,128)(2,1)}, bf16[256,4096]{1,0:T(8,128)(2,1)}, u32[]{:S(2)}, u32[]{:S(2)}) collective-permute-start(bf16[256,4096]{1,0:T(8,128)(2,1)} %refs_6_.1), channel_id=1, source_target_pairs={{0,4},{1,5},{2,6},{3,7},{4,0},{5,1},{6,2},{7,3},{8,12},{9,13},{10,... | collective-permute-start | bytes 6291464 | tf_op jit(solution)/shard_map/ppermute | solution.py:328
  2.6 38.9 %copy-start.3 = (bf16[1,128,1024]{2,1,0:T(8,128)(2,1)S(1)}, bf16[1,128,1024]{2,1,0:T(8,128)(2,1)}, u32[]{:S(2)}) copy-start(bf16[1,128,1024]{2,1,0:T(8,128)(2,1)} %param.8) | copy-start | bytes 786436
  6.6 31.4 %collective-permute-start = (bf16[256,1024]{1,0:T(8,128)(2,1)}, bf16[256,1024]{1,0:T(8,128)(2,1)}, u32[]{:S(2)}, u32[]{:S(2)}) collective-permute-start(bf16[256,1024]{1,0:T(8,128)(2,1)} %get-tuple-element.38), channel_id=1, source_target_pairs={{0,1},{1,0},{2,3},{3,2},{4,5},{5,4},{6,7},{7,6},{8,9},{9,8},{10,11... | collective-permute-start | bytes 1572872 | tf_op jit(solution)/shard_map/ppermute | solution.py:328
  9.2 28.8 %collective-permute-start.1 = (bf16[256,1024]{1,0:T(8,128)(2,1)}, bf16[256,1024]{1,0:T(8,128)(2,1)}, u32[]{:S(2)}, u32[]{:S(2)}) collective-permute-start(bf16[256,1024]{1,0:T(8,128)(2,1)} %get-tuple-element.39), channel_id=1, source_target_pairs={{0,2},{1,3},{2,0},{3,1},{4,6},{5,7},{6,4},{7,5},{8,10},{9,11},{10,... | collective-permute-start | bytes 1572872 | tf_op jit(solution)/shard_map/ppermute | solution.py:328
  10.7 26.2 %collective-permute-start.4 = (bf16[256,1024]{1,0:T(8,128)(2,1)}, bf16[256,1024]{1,0:T(8,128)(2,1)}, u32[]{:S(2)}, u32[]{:S(2)}) collective-permute-start(bf16[256,1024]{1,0:T(8,128)(2,1)} %get-tuple-element.43), channel_id=1, source_target_pairs={{0,16},{1,17},{2,18},{3,19},{4,20},{5,21},{6,22},{7,23},{8,24},{9,... | collective-permute-start | bytes 1572872 | tf_op jit(solution)/shard_map/ppermute | solution.py:328
  14.1 31.6 %copy-start.1 = (bf16[1,128,4096]{2,1,0:T(8,128)(2,1)S(1)}, bf16[1,128,4096]{2,1,0:T(8,128)(2,1)}, u32[]{:S(2)}) copy-start(bf16[1,128,4096]{2,1,0:T(8,128)(2,1)} %param.9) | copy-start | bytes 3145732
  15.6 36.8 %collective-permute-start.6 = (bf16[256,2048]{1,0:T(8,128)(2,1)}, bf16[256,2048]{1,0:T(8,128)(2,1)}, u32[]{:S(2)}, u32[]{:S(2)}) collective-permute-start(bf16[256,2048]{1,0:T(8,128)(2,1)} %get-tuple-element.44), channel_id=1, source_target_pairs={{0,8},{1,9},{2,10},{3,11},{4,12},{5,13},{6,14},{7,15},{8,0},{9,1},... | collective-permute-start | bytes 3145736 | tf_op jit(solution)/shard_map/ppermute | solution.py:328
  17.7 20.4 %collective-permute-start.3 = (bf16[256,1024]{1,0:T(8,128)(2,1)}, bf16[256,1024]{1,0:T(8,128)(2,1)}, u32[]{:S(2)}, u32[]{:S(2)}) collective-permute-start(bf16[256,1024]{1,0:T(8,128)(2,1)} %get-tuple-element.41), channel_id=1, source_target_pairs={{0,3},{1,2},{2,1},{3,0},{4,7},{5,6},{6,5},{7,4},{8,11},{9,10},{10,... | collective-permute-start | bytes 1572872 | tf_op jit(solution)/shard_map/ppermute | solution.py:328
  36.9 25.0 %collective-permute-start.5 = (bf16[256,1024]{1,0:T(8,128)(2,1)}, bf16[256,1024]{1,0:T(8,128)(2,1)}, u32[]{:S(2)}, u32[]{:S(2)}) collective-permute-start(bf16[256,1024]{1,0:T(8,128)(2,1)} %collective-permute-done.4.refs_0_.refs_6_), channel_id=1, source_target_pairs={{0,8},{1,9},{2,10},{3,11},{4,12},{5,13},{6,14},{7,15},{8,0},{9,1},... | collective-permute-start | bytes 1572872 | tf_op jit(solution)/shard_map/ppermute | solution.py:328
  38.0 26.0 %collective-permute-start.9 = (bf16[256,1024]{1,0:T(8,128)(2,1)}, bf16[256,1024]{1,0:T(8,128)(2,1)S(1)}, u32[]{:S(2)}, u32[]{:S(2)}) collective-permute-start(bf16[256,1024]{1,0:T(8,128)(2,1)} %collective-permute-done.4.refs_0_.refs_6_), channel_id=1, source_target_pairs={{0,3},{1,2},{2,1},{3,0},{4,7},{5,6},{6,5},{7,4},{8,11},{9,10},{10,... | collective-permute-start | bytes 1572872 | tf_op jit(solution)/shard_map/ppermute | solution.py:328
  38.6 25.4 %collective-permute-start.7 = (bf16[256,1024]{1,0:T(8,128)(2,1)}, bf16[256,1024]{1,0:T(8,128)(2,1)S(1)}, u32[]{:S(2)}, u32[]{:S(2)}) collective-permute-start(bf16[256,1024]{1,0:T(8,128)(2,1)} %collective-permute-done.4.refs_0_.refs_6_), channel_id=1, source_target_pairs={{0,1},{1,0},{2,3},{3,2},{4,5},{5,4},{6,7},{7,6},{8,9},{9,8},{10,11... | collective-permute-start | bytes 1572872 | tf_op jit(solution)/shard_map/ppermute | solution.py:328
  40.1 24.0 %collective-permute-start.8 = (bf16[256,1024]{1,0:T(8,128)(2,1)}, bf16[256,1024]{1,0:T(8,128)(2,1)S(1)}, u32[]{:S(2)}, u32[]{:S(2)}) collective-permute-start(bf16[256,1024]{1,0:T(8,128)(2,1)} %collective-permute-done.4.refs_0_.refs_6_), channel_id=1, source_target_pairs={{0,2},{1,3},{2,0},{3,1},{4,6},{5,7},{6,4},{7,5},{8,10},{9,11},{10,... | collective-permute-start | bytes 1572872 | tf_op jit(solution)/shard_map/ppermute | solution.py:328
  41.6 1.0 copy-start.2
  52.3 12.0 %copy-start.4 = (bf16[256,2048]{1,0:T(8,128)(2,1)S(1)}, bf16[256,2048]{1,0:T(8,128)(2,1)}, u32[]{:S(2)}) copy-start(bf16[256,2048]{1,0:T(8,128)(2,1)} %get-tuple-element.52) | copy-start | bytes 3145732
  64.2 6.5 %collective-permute-start.10 = (bf16[256,7168]{1,0:T(8,128)(2,1)S(1)}, bf16[256,7168]{1,0:T(8,128)(2,1)S(1)}, u32[]{:S(2)}, u32[]{:S(2)}) collective-permute-start(bf16[256,7168]{1,0:T(8,128)(2,1)S(1)} %constant_dynamic-update-slice_fusion), channel_id=1, source_target_pairs={{0,4},{1,5},{2,6},{3,7},{4,0},{5,1},{6,2},{7,3},{8,12},{9,13},{10,... | collective-permute-start | bytes 11010056 | tf_op jit(solution)/shard_map/ppermute | solution.py:328
  64.3 26.0 %collective-permute-start.17 = (bf16[256,2048]{1,0:T(8,128)(2,1)S(1)}, bf16[256,2048]{1,0:T(8,128)(2,1)S(1)}, u32[]{:S(2)}, u32[]{:S(2)}) collective-permute-start(bf16[256,2048]{1,0:T(8,128)(2,1)S(1)} %copy-done.4), channel_id=1, source_target_pairs={{0,8},{1,9},{2,10},{3,11},{4,12},{5,13},{6,14},{7,15},{8,0},{9,1},... | collective-permute-start | bytes 3145736 | tf_op jit(solution)/shard_map/ppermute | solution.py:328
  64.6 15.0 %collective-permute-start.11 = (bf16[256,1024]{1,0:T(8,128)(2,1)}, bf16[256,1024]{1,0:T(8,128)(2,1)S(1)}, u32[]{:S(2)}, u32[]{:S(2)}) collective-permute-start(bf16[256,1024]{1,0:T(8,128)(2,1)} %collective-permute-done.5.refs_0_.refs_6_), channel_id=1, source_target_pairs={{0,1},{1,0},{2,3},{3,2},{4,5},{5,4},{6,7},{7,6},{8,9},{9,8},{10,11... | collective-permute-start | bytes 1572872 | tf_op jit(solution)/shard_map/ppermute | solution.py:328
  65.1 25.2 %collective-permute-start.13 = (bf16[256,1024]{1,0:T(8,128)(2,1)}, bf16[256,1024]{1,0:T(8,128)(2,1)S(1)}, u32[]{:S(2)}, u32[]{:S(2)}) collective-permute-start(bf16[256,1024]{1,0:T(8,128)(2,1)} %collective-permute-done.5.refs_0_.refs_6_), channel_id=1, source_target_pairs={{0,2},{1,3},{2,0},{3,1},{4,6},{5,7},{6,4},{7,5},{8,10},{9,11},{10,... | collective-permute-start | bytes 1572872 | tf_op jit(solution)/shard_map/ppermute | solution.py:328
  65.8 24.5 %collective-permute-start.15 = (bf16[256,1024]{1,0:T(8,128)(2,1)}, bf16[256,1024]{1,0:T(8,128)(2,1)S(1)}, u32[]{:S(2)}, u32[]{:S(2)}) collective-permute-start(bf16[256,1024]{1,0:T(8,128)(2,1)} %collective-permute-done.5.refs_0_.refs_6_), channel_id=1, source_target_pairs={{0,3},{1,2},{2,1},{3,0},{4,7},{5,6},{6,5},{7,4},{8,11},{9,10},{10,... | collective-permute-start | bytes 1572872 | tf_op jit(solution)/shard_map/ppermute | solution.py:328
  90.3 2.7 %collective-permute-start.18 = (bf16[256,2048]{1,0:T(8,128)(2,1)S(1)}, bf16[256,2048]{1,0:T(8,128)(2,1)S(1)}, u32[]{:S(2)}, u32[]{:S(2)}) collective-permute-start(bf16[256,2048]{1,0:T(8,128)(2,1)S(1)} %collective-permute-done.17.refs_2_.refs_8_), channel_id=1, source_target_pairs={{0,4},{1,5},{2,6},{3,7},{4,0},{5,1},{6,2},{7,3},{8,12},{9,13},{10,... | collective-permute-start | bytes 3145736 | tf_op jit(solution)/shard_map/ppermute | solution.py:328
  90.3 9.7 %collective-permute-start.12 = (bf16[256,1024]{1,0:T(8,128)(2,1)S(1)}, bf16[256,1024]{1,0:T(8,128)(2,1)S(1)}, u32[]{:S(2)}, u32[]{:S(2)}) collective-permute-start(bf16[256,1024]{1,0:T(8,128)(2,1)S(1)} %collective-permute-done.11.refs_2_.refs_8_), channel_id=1, source_target_pairs={{0,4},{1,5},{2,6},{3,7},{4,0},{5,1},{6,2},{7,3},{8,12},{9,13},{10,... | collective-permute-start | bytes 1572872 | tf_op jit(solution)/shard_map/ppermute | solution.py:328
  90.9 9.8 %collective-permute-start.14 = (bf16[256,1024]{1,0:T(8,128)(2,1)S(1)}, bf16[256,1024]{1,0:T(8,128)(2,1)S(1)}, u32[]{:S(2)}, u32[]{:S(2)}) collective-permute-start(bf16[256,1024]{1,0:T(8,128)(2,1)S(1)} %collective-permute-done.13.refs_4_.refs_10_), channel_id=1, source_target_pairs={{0,4},{1,5},{2,6},{3,7},{4,0},{5,1},{6,2},{7,3},{8,12},{9,13},{10,... | collective-permute-start | bytes 1572872 | tf_op jit(solution)/shard_map/ppermute | solution.py:328
  90.9 9.8 %collective-permute-start.16 = (bf16[256,1024]{1,0:T(8,128)(2,1)S(1)}, bf16[256,1024]{1,0:T(8,128)(2,1)S(1)}, u32[]{:S(2)}, u32[]{:S(2)}) collective-permute-start(bf16[256,1024]{1,0:T(8,128)(2,1)S(1)} %collective-permute-done.15.refs_6_.refs_12_), channel_id=1, source_target_pairs={{0,4},{1,5},{2,6},{3,7},{4,0},{5,1},{6,2},{7,3},{8,12},{9,13},{10,... | collective-permute-start | bytes 1572872 | tf_op jit(solution)/shard_map/ppermute | solution.py:328
  97.0 9.7 %collective-permute-start.24 = (bf16[128,768]{1,0:T(8,128)(2,1)S(1)}, bf16[128,768]{1,0:T(8,128)(2,1)S(1)}, u32[]{:S(2)}, u32[]{:S(2)}) collective-permute-start(bf16[128,768]{1,0:T(8,128)(2,1)S(1)} %pad_maximum_fusion.3), channel_id=1, source_target_pairs={{0,3},{1,2},{2,1},{3,0},{4,7},{5,6},{6,5},{7,4},{8,11},{9,10},{10,... | collective-permute-start | bytes 589832 | tf_op jit(solution)/shard_map/ppermute | solution.py:328
  98.6 14.3 %collective-permute-start.23 = (bf16[128,768]{1,0:T(8,128)(2,1)S(1)}, bf16[128,768]{1,0:T(8,128)(2,1)S(1)}, u32[]{:S(2)}, u32[]{:S(2)}) collective-permute-start(bf16[128,768]{1,0:T(8,128)(2,1)S(1)} %pad_maximum_fusion.2), channel_id=1, source_target_pairs={{0,2},{1,3},{2,0},{3,1},{4,6},{5,7},{6,4},{7,5},{8,10},{9,11},{10,... | collective-permute-start | bytes 589832 | tf_op jit(solution)/shard_map/ppermute | solution.py:328
  100.1 12.7 %collective-permute-start.22 = (bf16[128,768]{1,0:T(8,128)(2,1)S(1)}, bf16[128,768]{1,0:T(8,128)(2,1)S(1)}, u32[]{:S(2)}, u32[]{:S(2)}) collective-permute-start(bf16[128,768]{1,0:T(8,128)(2,1)S(1)} %pad_maximum_fusion.1), channel_id=1, source_target_pairs={{0,1},{1,0},{2,3},{3,2},{4,5},{5,4},{6,7},{7,6},{8,9},{9,8},{10,11... | collective-permute-start | bytes 589832 | tf_op jit(solution)/shard_map/ppermute | solution.py:328
  104.5 9.7 %collective-permute-start.19 = (bf16[128,256]{1,0:T(8,128)(2,1)S(1)}, bf16[128,256]{1,0:T(8,128)(2,1)S(1)}, u32[]{:S(2)}, u32[]{:S(2)}) collective-permute-start(bf16[128,256]{1,0:T(8,128)(2,1)S(1)} %get-tuple-element.60), channel_id=1, source_target_pairs={{0,1},{1,0},{2,3},{3,2},{4,5},{5,4},{6,7},{7,6},{8,9},{9,8},{10,11... | collective-permute-start | bytes 196616 | tf_op jit(solution)/shard_map/ppermute | solution.py:328
  106.0 8.2 %collective-permute-start.20 = (bf16[128,256]{1,0:T(8,128)(2,1)S(1)}, bf16[128,256]{1,0:T(8,128)(2,1)S(1)}, u32[]{:S(2)}, u32[]{:S(2)}) collective-permute-start(bf16[128,256]{1,0:T(8,128)(2,1)S(1)} %get-tuple-element.61), channel_id=1, source_target_pairs={{0,2},{1,3},{2,0},{3,1},{4,6},{5,7},{6,4},{7,5},{8,10},{9,11},{10,... | collective-permute-start | bytes 196616 | tf_op jit(solution)/shard_map/ppermute | solution.py:328
  106.6 7.6 %collective-permute-start.21 = (bf16[128,256]{1,0:T(8,128)(2,1)S(1)}, bf16[128,256]{1,0:T(8,128)(2,1)S(1)}, u32[]{:S(2)}, u32[]{:S(2)}) collective-permute-start(bf16[128,256]{1,0:T(8,128)(2,1)S(1)} %get-tuple-element.62), channel_id=1, source_target_pairs={{0,3},{1,2},{2,1},{3,0},{4,7},{5,6},{6,5},{7,4},{8,11},{9,10},{10,... | collective-permute-start | bytes 196616 | tf_op jit(solution)/shard_map/ppermute | solution.py:328

commit v6 on v5

--- a/solution.py
+++ b/solution.py
@@ -494,7 +494,7 @@
         middle = to_core(jnp.concatenate([one_a, three] + twos[:3] + [after(twos[3], total, mine_0[0])], axis=1))
         parts_2 = [own(twos[t], columns[t]) for t in range(groups)]
         parts_2 += [other(middle, columns[t], half + quarter + t * quarter, quarter) for t in range(groups)]
-        threes = [three] + [to_ctx(after(three, *twos[1:]), t) for t in range(1, groups)]
+        threes = [three] + [to_ctx(after(three, *twos[1:3]), t) for t in range(1, groups)]
         q_grad, mine_2 = grad_step(2, parts_2, q_grad)
         total = project_step(2, parts_2, total, False)
         one_b_other = to_core(after(one_b, total, mine_2[0], *threes[1:]))

time: 116 us -> 116 us (level)
  transfers between devices with their start and end apart: 25 -> 25, of which waited for: 6 -> 6; matrix products, arithmetic and copies ran while one was open for 7% -> 7% of each run, Pallas kernels for 28% -> 29%
where the time goes in v6:
time: 116 us; the launch traced here: 115 us
  waiting for transfers between devices  44.9 us (39%)
  Pallas kernels  34.2 us (29%)
  starting transfers between devices  25.6 us (22%)
  local copies, waits for them, and re-layouts  8.85 us (8%)
    ppermute x25, waiting for transfers between devices, move(): return lax.ppermute(block, ('dp', 'ctx'), pairs)  44.9 us
    ppermute x25, starting transfers between devices, move(): return lax.ppermute(block, ('dp', 'ctx'), pairs)  25.6 us
    pallas_call x4, Pallas kernels, grad_step(): pl.pallas_call(functools.partial(grad_kernel, *sizes, slot, swapped, plan...  15.8 us
    pallas_call x4, Pallas kernels, project_step(): pl.pallas_call(functools.partial(project_kernel, slot, swapped, plan, fir...  8.79 us
    unnamed x20, local copies, waits for them, and re-layouts  6.14 us
    pallas_call x1, Pallas kernels, on_device(): pl.pallas_call(functools.partial(pack_kernel, groups, unit_count, rows, f...  3.95 us
    pallas_call x1, Pallas kernels, on_device(): pl.pallas_call(functools.partial(forward_kernel, *sizes, fold), out_shape...  3.06 us
    pallas_call x2, Pallas kernels, on_device(): pl.pallas_call(functools.partial(combine_kernel, len(share), order, swapp...  2.58 us
  transfers between devices with their start and end apart: 25, of which 6 were waited for; matrix products, arithmetic and copies ran while one was open for 7% of the time, Pallas kernels for 29%

profile of v6, /device:TPU:0, one launch (start us, length us, event | category | flops | bytes accessed | tf_op | source)
XLA Modules:
  0.0 115.3 jit_solution(2192756952701440597)
XLA Ops:
  0.6 0.0 copy-start
  0.7 0.5 collective-permute-start.2
  1.2 1.4 %copy.20.routes = s32[1,4,2]{2,1,0:T(4,128)} copy(s32[1,4,2]{1,2,0:T(2,128)} %param.13) | data formatting | bytes 64 | tf_op args[6]
  2.6 4.0 %pack.1 = (bf16[256,1024]{1,0:T(8,128)(2,1)}, bf16[256,1024]{1,0:T(8,128)(2,1)}, bf16[256,1024]{1,0:T(8,128)(2,1)}, bf16[256,1024]{1,0:T(8,128)(2,1)}) custom-call(s32[1,4,2]{2,1,0:T(4,128)} %copy.20.routes, bf16[128,2048]{1,0:T(8,128)(2,1)} %bitcast.23, bf16[128,1024]{1,0:T(8,128)(2,1)} %bitcast.25, bf16[256,4096]{1,0:T(8,128)(2,1)} %refs_6_.1), custom_call_target="tpu_custom_call" | custom-call | tf_op jit(solution)/shard_map/pack/pallas_call | solution.py:353
  6.6 2.5 %collective-permute-start = (bf16[256,1024]{1,0:T(8,128)(2,1)}, bf16[256,1024]{1,0:T(8,128)(2,1)}, u32[]{:S(2)}, u32[]{:S(2)}) collective-permute-start(bf16[256,1024]{1,0:T(8,128)(2,1)} %get-tuple-element.38), channel_id=1, source_target_pairs={{0,1},{1,0},{2,3},{3,2},{4,5},{5,4},{6,7},{7,6},{8,9},{9,8},{10,11... | collective-permute-start | bytes 1572872 | tf_op jit(solution)/shard_map/ppermute | solution.py:328
  9.1 1.5 %collective-permute-start.1 = (bf16[256,1024]{1,0:T(8,128)(2,1)}, bf16[256,1024]{1,0:T(8,128)(2,1)}, u32[]{:S(2)}, u32[]{:S(2)}) collective-permute-start(bf16[256,1024]{1,0:T(8,128)(2,1)} %get-tuple-element.39), channel_id=1, source_target_pairs={{0,2},{1,3},{2,0},{3,1},{4,6},{5,7},{6,4},{7,5},{8,10},{9,11},{10,... | collective-permute-start | bytes 1572872 | tf_op jit(solution)/shard_map/ppermute | solution.py:328
  10.6 2.6 %collective-permute-start.4 = (bf16[256,1024]{1,0:T(8,128)(2,1)}, bf16[256,1024]{1,0:T(8,128)(2,1)}, u32[]{:S(2)}, u32[]{:S(2)}) collective-permute-start(bf16[256,1024]{1,0:T(8,128)(2,1)} %get-tuple-element.43), channel_id=1, source_target_pairs={{0,16},{1,17},{2,18},{3,19},{4,20},{5,21},{6,22},{7,23},{8,24},{9,... | collective-permute-start | bytes 1572872 | tf_op jit(solution)/shard_map/ppermute | solution.py:328
  13.2 0.8 slice_reduce_fusion.1
  14.0 0.0 copy-start.1
  14.1 1.4 %fusion.17 = (bf16[256,2048]{1,0:T(8,128)(2,1)}, bf16[256,2048]{1,0:T(8,128)(2,1)}) fusion(bf16[256,4096]{1,0:T(8,128)(2,1)S(1)} %copy-done), kind=kLoop, calls=%fused_computation.42 | loop fusion | bytes 4194304 | tf_op jit(solution)/shard_map/slice | solution.py:493
  15.5 0.0 collective-permute-done.2.refs_1_.refs_7_
  15.5 1.6 %collective-permute-start.6 = (bf16[256,2048]{1,0:T(8,128)(2,1)}, bf16[256,2048]{1,0:T(8,128)(2,1)}, u32[]{:S(2)}, u32[]{:S(2)}) collective-permute-start(bf16[256,2048]{1,0:T(8,128)(2,1)} %get-tuple-element.44), channel_id=1, source_target_pairs={{0,8},{1,9},{2,10},{3,11},{4,12},{5,13},{6,14},{7,15},{8,0},{9,1},... | collective-permute-start | bytes 3145736 | tf_op jit(solution)/shard_map/ppermute | solution.py:328
  17.1 0.1 and_select_fusion.1
  17.2 0.1 copy.19
  17.2 0.1 add.101
  17.4 0.1 slice_reduce_fusion
  17.5 0.1 convert_reduce_fusion.1
  17.6 0.1 eq.49
  17.6 0.5 collective-permute-start.3
  18.2 0.1 and_select_fusion
  18.3 0.1 convert_reduce_fusion
  18.4 18.4 %collective-permute-done.4.refs_0_.refs_6_ = bf16[256,1024]{1,0:T(8,128)(2,1)} collective-permute-done((bf16[256,1024]{1,0:T(8,128)(2,1)}, bf16[256,1024]{1,0:T(8,128)(2,1)}, u32[]{:S(2)}, u32[]{:S(2)}) %collective-permute-start.4) | collective-permute-done | bytes 524320 | tf_op jit(solution)/shard_map/ppermute | solution.py:328
  36.8 0.6 collective-permute-start.5
  37.4 0.4 fusion.2.refs_1_
  37.8 0.1 concatenate.18.refs_0_.meta
  37.9 0.6 collective-permute-start.9
  38.5 1.5 %collective-permute-start.7 = (bf16[256,1024]{1,0:T(8,128)(2,1)}, bf16[256,1024]{1,0:T(8,128)(2,1)S(1)}, u32[]{:S(2)}, u32[]{:S(2)}) collective-permute-start(bf16[256,1024]{1,0:T(8,128)(2,1)} %collective-permute-done.4.refs_0_.refs_6_), channel_id=1, source_target_pairs={{0,1},{1,0},{2,3},{3,2},{4,5},{5,4},{6,7},{7,6},{8,9},{9,8},{10,11... | collective-permute-start | bytes 1572872 | tf_op jit(solution)/shard_map/ppermute | solution.py:328
  40.0 1.5 %collective-permute-start.8 = (bf16[256,1024]{1,0:T(8,128)(2,1)}, bf16[256,1024]{1,0:T(8,128)(2,1)S(1)}, u32[]{:S(2)}, u32[]{:S(2)}) collective-permute-start(bf16[256,1024]{1,0:T(8,128)(2,1)} %collective-permute-done.4.refs_0_.refs_6_), channel_id=1, source_target_pairs={{0,2},{1,3},{2,0},{3,1},{4,6},{5,7},{6,4},{7,5},{8,10},{9,11},{10,... | collective-permute-start | bytes 1572872 | tf_op jit(solution)/shard_map/ppermute | solution.py:328
  41.5 1.0 copy-done.2
  42.5 3.1 %forward.1 = (bf16[128,2048]{1,0:T(8,128)(2,1)S(1)}, f32[4,2,256,128]{3,2,1,0:T(8,128)S(1)}, bf16[2,128,1024]{2,1,0:T(8,128)(2,1)S(1)}, bf16[128,2048]{1,0:T(8,128)(2,1)S(1)}) custom-call(s32[7]{0:T(128)S(1)} %concatenate.18.refs_0_.meta, f32[2,64,128]{2,1,0:T(8,128)S(1)} %fusion.2.refs_1_, bf16[128,2048]{1,0:T(8,128)(2,1)S(1)} %bitcast.24, ...), custom_call_target="tpu_custom_call" | custom-call | flops 1073741824 | bytes 8388608 | tf_op jit(solution)/shard_map/forward/pallas_call | solution.py:382
  45.6 4.3 %grad_0.1 = (bf16[128,2048]{1,0:T(8,128)(2,1)}, bf16[128,256]{1,0:T(8,128)(2,1)S(1)}, bf16[128,256]{1,0:T(8,128)(2,1)S(1)}, bf16[128,256]{1,0:T(8,128)(2,1)S(1)}, bf16[128,256]{1,0:T(8,128)(2,1)S(1)}) custom-call(s32[7]{0:T(128)S(1)} %concatenate.18.refs_0_.meta, bf16[128,4096]{1,0:T(8,128)(2,1)S(1)} %bitcast.19, ...), custom_call_target="tpu_custom_call" | custom-call | flops 1073741824 | bytes 12582912 | tf_op jit(solution)/shard_map/grad_0/pallas_call | solution.py:422
  49.9 2.3 %project_0.1.refs_5_ = f32[128,4096]{1,0:T(8,128)S(1)} custom-call(s32[7]{0:T(128)S(1)} %concatenate.18.refs_0_.meta, bf16[128,2048]{1,0:T(8,128)(2,1)S(1)} %get-tuple-element.42.context_ref.refs_3_, bf16[256,4096]{1,0:T(8,128)(2,1)S(1)} %copy-done, bf16[256,4096]{1,0:T(8,128)(2,1)} %collective-permute-done.2.refs_1_.refs_7_), custom_call_target="tpu_custom_call" | custom-call | flops 536870912 | bytes 8388608 | tf_op jit(solution)/shard_map/project_0/pallas_call | solution.py:460
  52.3 0.0 copy-start.4
  52.3 0.0 collective-permute-done.6.refs_0_.refs_6_
  52.3 1.4 %constant_dynamic-update-slice_fusion.5 = bf16[256,7168]{1,0:T(8,128)(2,1)S(1)} fusion(bf16[256,2048]{1,0:T(8,128)(2,1)} %collective-permute-done.6.refs_0_.refs_6_), kind=kLoop, calls=%fused_computation.15 | loop fusion | bytes 2097152
  53.7 8.1 %collective-permute-done.5.refs_0_.refs_6_ = bf16[256,1024]{1,0:T(8,128)(2,1)} collective-permute-done((bf16[256,1024]{1,0:T(8,128)(2,1)}, bf16[256,1024]{1,0:T(8,128)(2,1)}, u32[]{:S(2)}, u32[]{:S(2)}) %collective-permute-start.5) | collective-permute-done | bytes 524320 | tf_op jit(solution)/shard_map/ppermute | solution.py:328
  61.8 1.1 constant_dynamic-update-slice_fusion.4
  62.8 1.1 constant_dynamic-update-slice_fusion.3
  64.1 0.1 collective-permute-start.10
  64.2 0.3 collective-permute-start.17
  64.4 0.5 collective-permute-start.11
  65.0 0.7 collective-permute-start.13
  65.7 2.2 %collective-permute-start.15 = (bf16[256,1024]{1,0:T(8,128)(2,1)}, bf16[256,1024]{1,0:T(8,128)(2,1)S(1)}, u32[]{:S(2)}, u32[]{:S(2)}) collective-permute-start(bf16[256,1024]{1,0:T(8,128)(2,1)} %collective-permute-done.5.refs_0_.refs_6_), channel_id=1, source_target_pairs={{0,3},{1,2},{2,1},{3,0},{4,7},{5,6},{6,5},{7,4},{8,11},{9,10},{10,... | collective-permute-start | bytes 1572872 | tf_op jit(solution)/shard_map/ppermute | solution.py:328
  67.9 2.6 %collective-permute-done.10.refs_4_.refs_10_.refs_1_.refs_7_ = bf16[256,7168]{1,0:T(8,128)(2,1)S(1)} collective-permute-done((bf16[256,7168]{1,0:T(8,128)(2,1)S(1)}, bf16[256,7168]{1,0:T(8,128)(2,1)S(1)}, u32[]{:S(2)}, u32[]{:S(2)}) %collective-permute-start.10) | collective-permute-done | bytes 3670048 | tf_op jit(solution)/shard_map/ppermute | solution.py:328
  70.6 1.8 %project_2.1.refs_4_ = f32[128,4096]{1,0:T(8,128)S(1)} custom-call(s32[7]{0:T(128)S(1)} %concatenate.18.refs_0_.meta, bf16[128,2048]{1,0:T(8,128)(2,1)S(1)} %get-tuple-element.42.context_ref.refs_3_, bf16[256,1024]{1,0:T(8,128)(2,1)} %collective-permute-done.4.refs_0_.refs_6_, bf16[256,1024]{1,0:T(8,128)(2,1)S(1)} %collective-permute-done.7.refs_1_.refs_7_, ...), custom_call_target="tpu_custom_call" | custom-call | flops 536870912 | bytes 8388608 | tf_op jit(solution)/shard_map/project_2/pallas_call | solution.py:460
  72.3 3.8 %grad_2.1 = (bf16[128,2048]{1,0:T(8,128)(2,1)}, bf16[128,256]{1,0:T(8,128)(2,1)S(1)}, bf16[128,256]{1,0:T(8,128)(2,1)S(1)}, bf16[128,256]{1,0:T(8,128)(2,1)S(1)}, bf16[128,256]{1,0:T(8,128)(2,1)S(1)}) custom-call(s32[7]{0:T(128)S(1)} %concatenate.18.refs_0_.meta, bf16[128,4096]{1,0:T(8,128)(2,1)S(1)} %bitcast.20, ...), custom_call_target="tpu_custom_call", output_to_operand_aliasing={{0}: (11, {})} | custom-call | flops 1073741824 | bytes 12582912 | tf_op jit(solution)/shard_map/grad_2/pallas_call | solution.py:422
  76.1 3.3 %collective-permute-done.11.refs_2_.refs_8_ = bf16[256,1024]{1,0:T(8,128)(2,1)S(1)} collective-permute-done((bf16[256,1024]{1,0:T(8,128)(2,1)}, bf16[256,1024]{1,0:T(8,128)(2,1)S(1)}, u32[]{:S(2)}, u32[]{:S(2)}) %collective-permute-start.11) | collective-permute-done | bytes 524320 | tf_op jit(solution)/shard_map/ppermute | solution.py:328
  79.4 10.8 %collective-permute-done.13.refs_4_.refs_10_ = bf16[256,1024]{1,0:T(8,128)(2,1)S(1)} collective-permute-done((bf16[256,1024]{1,0:T(8,128)(2,1)}, bf16[256,1024]{1,0:T(8,128)(2,1)S(1)}, u32[]{:S(2)}, u32[]{:S(2)}) %collective-permute-start.13) | collective-permute-done | bytes 524320 | tf_op jit(solution)/shard_map/ppermute | solution.py:328
  90.2 0.5 collective-permute-start.12
  90.7 0.1 collective-permute-start.14
  90.8 0.4 collective-permute-start.16
  91.2 1.6 %collective-permute-done.18.refs_3_.refs_9_ = bf16[256,2048]{1,0:T(8,128)(2,1)S(1)} collective-permute-done((bf16[256,2048]{1,0:T(8,128)(2,1)S(1)}, bf16[256,2048]{1,0:T(8,128)(2,1)S(1)}, u32[]{:S(2)}, u32[]{:S(2)}) %collective-permute-start.18) | collective-permute-done | bytes 1048608 | tf_op jit(solution)/shard_map/ppermute | solution.py:328
  92.8 3.9 %grad_1.1 = (bf16[128,2048]{1,0:T(8,128)(2,1)}, bf16[128,256]{1,0:T(8,128)(2,1)S(1)}, bf16[128,256]{1,0:T(8,128)(2,1)S(1)}, bf16[128,256]{1,0:T(8,128)(2,1)S(1)}, bf16[128,256]{1,0:T(8,128)(2,1)S(1)}) custom-call(s32[7]{0:T(128)S(1)} %concatenate.18.refs_0_.meta, bf16[128,4096]{1,0:T(8,128)(2,1)S(1)} %bitcast.21, ...), custom_call_target="tpu_custom_call", output_to_operand_aliasing={{0}: (10, {})} | custom-call | flops 1073741824 | bytes 12582912 | tf_op jit(solution)/shard_map/grad_1/pallas_call | solution.py:422
  96.8 1.6 %collective-permute-start.24 = (bf16[128,768]{1,0:T(8,128)(2,1)S(1)}, bf16[128,768]{1,0:T(8,128)(2,1)S(1)}, u32[]{:S(2)}, u32[]{:S(2)}) collective-permute-start(bf16[128,768]{1,0:T(8,128)(2,1)S(1)} %pad_maximum_fusion.3), channel_id=1, source_target_pairs={{0,3},{1,2},{2,1},{3,0},{4,7},{5,6},{6,5},{7,4},{8,11},{9,10},{10,... | collective-permute-start | bytes 589832 | tf_op jit(solution)/shard_map/ppermute | solution.py:328
  98.4 1.5 %collective-permute-start.23 = (bf16[128,768]{1,0:T(8,128)(2,1)S(1)}, bf16[128,768]{1,0:T(8,128)(2,1)S(1)}, u32[]{:S(2)}, u32[]{:S(2)}) collective-permute-start(bf16[128,768]{1,0:T(8,128)(2,1)S(1)} %pad_maximum_fusion.2), channel_id=1, source_target_pairs={{0,2},{1,3},{2,0},{3,1},{4,6},{5,7},{6,4},{7,5},{8,10},{9,11},{10,... | collective-permute-start | bytes 589832 | tf_op jit(solution)/shard_map/ppermute | solution.py:328
  100.0 0.6 collective-permute-start.22
  100.6 3.8 %grad_3.1 = (bf16[128,2048]{1,0:T(8,128)(2,1)}, bf16[128,256]{1,0:T(8,128)(2,1)S(1)}, bf16[128,256]{1,0:T(8,128)(2,1)S(1)}, bf16[128,256]{1,0:T(8,128)(2,1)S(1)}, bf16[128,256]{1,0:T(8,128)(2,1)S(1)}) custom-call(s32[7]{0:T(128)S(1)} %concatenate.18.refs_0_.meta, bf16[128,4096]{1,0:T(8,128)(2,1)S(1)} %bitcast.22, ...), custom_call_target="tpu_custom_call", output_to_operand_aliasing={{0}: (14, {})} | custom-call | flops 1073741824 | bytes 12582912 | tf_op jit(solution)/shard_map/grad_3/pallas_call | solution.py:422
  104.3 1.6 %collective-permute-start.19 = (bf16[128,256]{1,0:T(8,128)(2,1)S(1)}, bf16[128,256]{1,0:T(8,128)(2,1)S(1)}, u32[]{:S(2)}, u32[]{:S(2)}) collective-permute-start(bf16[128,256]{1,0:T(8,128)(2,1)S(1)} %get-tuple-element.60), channel_id=1, source_target_pairs={{0,1},{1,0},{2,3},{3,2},{4,5},{5,4},{6,7},{7,6},{8,9},{9,8},{10,11... | collective-permute-start | bytes 196616 | tf_op jit(solution)/shard_map/ppermute | solution.py:328
  105.9 0.6 collective-permute-start.20
  106.5 1.4 %collective-permute-start.21 = (bf16[128,256]{1,0:T(8,128)(2,1)S(1)}, bf16[128,256]{1,0:T(8,128)(2,1)S(1)}, u32[]{:S(2)}, u32[]{:S(2)}) collective-permute-start(bf16[128,256]{1,0:T(8,128)(2,1)S(1)} %get-tuple-element.62), channel_id=1, source_target_pairs={{0,3},{1,2},{2,1},{3,0},{4,7},{5,6},{6,5},{7,4},{8,11},{9,10},{10,... | collective-permute-start | bytes 196616 | tf_op jit(solution)/shard_map/ppermute | solution.py:328
  108.0 2.0 %project_1.1.refs_8_ = f32[128,4096]{1,0:T(8,128)S(1)} custom-call(s32[7]{0:T(128)S(1)} %concatenate.18.refs_0_.meta, bf16[128,2048]{1,0:T(8,128)(2,1)S(1)} %get-tuple-element.42.context_ref.refs_3_, bf16[256,2048]{1,0:T(8,128)(2,1)} %collective-permute-done.6.refs_0_.refs_6_, bf16[256,7168]{1,0:T(8,128)(2,1)S(1)} %collective-permute-done.10.refs_4_.refs_10_.refs_1_.refs_7_, ...), custom_call_target="tpu_custom_call" | custom-call | flops 536870912 | bytes 8388608 | tf_op jit(solution)/shard_map/project_1/pallas_call | solution.py:460
  109.9 2.8 %project_3.1 = bf16[128,4096]{1,0:T(8,128)(2,1)} custom-call(s32[7]{0:T(128)S(1)} %concatenate.18.refs_0_.meta, bf16[128,2048]{1,0:T(8,128)(2,1)S(1)} %get-tuple-element.42.context_ref.refs_3_, bf16[256,1024]{1,0:T(8,128)(2,1)} %collective-permute-done.5.refs_0_.refs_6_, bf16[256,7168]{1,0:T(8,128)(2,1)S(1)} %collective-permute-done.10.refs_4_.refs_10_.refs_1_.refs_7_, ...), custom_call_target="tpu_custom_call" | custom-call | flops 536870912 | bytes 8388608 | tf_op jit(solution)/shard_map/project_3/pallas_call | solution.py:460
  112.7 1.4 %combine_0.1.refs_4_ = bf16[128,1024]{1,0:T(8,128)(2,1)} custom-call(s32[7]{0:T(128)S(1)} %concatenate.18.refs_0_.meta, bf16[128,768]{1,0:T(8,128)(2,1)S(1)} %pad_maximum_fusion.refs_0_, bf16[128,768]{1,0:T(8,128)(2,1)S(1)} %collective-permute-done.22.refs_1_, bf16[128,768]{1,0:T(8,128)(2,1)S(1)} %collective-permute-done.23.refs_2_, ...), custom_call_target="tpu_custom_call" | custom-call | tf_op jit(solution)/shard_map/combine_0/pallas_call | solution.py:535
  114.1 1.2 %combine_3.1 = bf16[128,1024]{1,0:T(8,128)(2,1)} custom-call(s32[7]{0:T(128)S(1)} %concatenate.18.refs_0_.meta, bf16[128,256]{1,0:T(8,128)(2,1)S(1)} %get-tuple-element.59.refs_0_, bf16[128,256]{1,0:T(8,128)(2,1)S(1)} %collective-permute-done.19.refs_1_, bf16[128,256]{1,0:T(8,128)(2,1)S(1)} %collective-permute-done.20.refs_2_, ...), custom_call_target="tpu_custom_call", output_to_operand_aliasing={{}: (5, {})} | custom-call | tf_op jit(solution)/shard_map/combine_3/pallas_call | solution.py:535
  (37 shorter events, 0.3 us)
Async XLA Ops:
  0.6 13.4 %copy-start = (bf16[256,4096]{1,0:T(8,128)(2,1)S(1)}, bf16[256,4096]{1,0:T(8,128)(2,1)}, u32[]{:S(2)}) copy-start(bf16[256,4096]{1,0:T(8,128)(2,1)} %refs_6_.1) | copy-start | bytes 6291460
  0.6 16.5 %copy-start.5 = (s32[1,16]{1,0:T(1,128)S(1)}, s32[1,16]{1,0:T(1,128)}, u32[]{:S(2)}) copy-start(s32[1,16]{1,0:T(1,128)} %param.11) | copy-start | bytes 196
  0.7 36.8 %copy-start.6 = (s32[1,4,4]{2,1,0:T(4,128)S(1)}, s32[1,4,4]{2,1,0:T(4,128)}, u32[]{:S(2)}) copy-start(s32[1,4,4]{2,1,0:T(4,128)} %param.12) | copy-start | bytes 196
  0.7 14.8 %collective-permute-start.2 = (bf16[256,4096]{1,0:T(8,128)(2,1)}, bf16[256,4096]{1,0:T(8,128)(2,1)}, u32[]{:S(2)}, u32[]{:S(2)}) collective-permute-start(bf16[256,4096]{1,0:T(8,128)(2,1)} %refs_6_.1), channel_id=1, source_target_pairs={{0,4},{1,5},{2,6},{3,7},{4,0},{5,1},{6,2},{7,3},{8,12},{9,13},{10,... | collective-permute-start | bytes 6291464 | tf_op jit(solution)/shard_map/ppermute | solution.py:328
  2.6 38.9 %copy-start.3 = (bf16[1,128,1024]{2,1,0:T(8,128)(2,1)S(1)}, bf16[1,128,1024]{2,1,0:T(8,128)(2,1)}, u32[]{:S(2)}) copy-start(bf16[1,128,1024]{2,1,0:T(8,128)(2,1)} %param.8) | copy-start | bytes 786436
  6.6 31.3 %collective-permute-start = (bf16[256,1024]{1,0:T(8,128)(2,1)}, bf16[256,1024]{1,0:T(8,128)(2,1)}, u32[]{:S(2)}, u32[]{:S(2)}) collective-permute-start(bf16[256,1024]{1,0:T(8,128)(2,1)} %get-tuple-element.38), channel_id=1, source_target_pairs={{0,1},{1,0},{2,3},{3,2},{4,5},{5,4},{6,7},{7,6},{8,9},{9,8},{10,11... | collective-permute-start | bytes 1572872 | tf_op jit(solution)/shard_map/ppermute | solution.py:328
  9.1 28.8 %collective-permute-start.1 = (bf16[256,1024]{1,0:T(8,128)(2,1)}, bf16[256,1024]{1,0:T(8,128)(2,1)}, u32[]{:S(2)}, u32[]{:S(2)}) collective-permute-start(bf16[256,1024]{1,0:T(8,128)(2,1)} %get-tuple-element.39), channel_id=1, source_target_pairs={{0,2},{1,3},{2,0},{3,1},{4,6},{5,7},{6,4},{7,5},{8,10},{9,11},{10,... | collective-permute-start | bytes 1572872 | tf_op jit(solution)/shard_map/ppermute | solution.py:328
  10.6 26.2 %collective-permute-start.4 = (bf16[256,1024]{1,0:T(8,128)(2,1)}, bf16[256,1024]{1,0:T(8,128)(2,1)}, u32[]{:S(2)}, u32[]{:S(2)}) collective-permute-start(bf16[256,1024]{1,0:T(8,128)(2,1)} %get-tuple-element.43), channel_id=1, source_target_pairs={{0,16},{1,17},{2,18},{3,19},{4,20},{5,21},{6,22},{7,23},{8,24},{9,... | collective-permute-start | bytes 1572872 | tf_op jit(solution)/shard_map/ppermute | solution.py:328
  14.0 31.6 %copy-start.1 = (bf16[1,128,4096]{2,1,0:T(8,128)(2,1)S(1)}, bf16[1,128,4096]{2,1,0:T(8,128)(2,1)}, u32[]{:S(2)}) copy-start(bf16[1,128,4096]{2,1,0:T(8,128)(2,1)} %param.9) | copy-start | bytes 3145732
  15.5 36.8 %collective-permute-start.6 = (bf16[256,2048]{1,0:T(8,128)(2,1)}, bf16[256,2048]{1,0:T(8,128)(2,1)}, u32[]{:S(2)}, u32[]{:S(2)}) collective-permute-start(bf16[256,2048]{1,0:T(8,128)(2,1)} %get-tuple-element.44), channel_id=1, source_target_pairs={{0,8},{1,9},{2,10},{3,11},{4,12},{5,13},{6,14},{7,15},{8,0},{9,1},... | collective-permute-start | bytes 3145736 | tf_op jit(solution)/shard_map/ppermute | solution.py:328
  17.6 20.3 %collective-permute-start.3 = (bf16[256,1024]{1,0:T(8,128)(2,1)}, bf16[256,1024]{1,0:T(8,128)(2,1)}, u32[]{:S(2)}, u32[]{:S(2)}) collective-permute-start(bf16[256,1024]{1,0:T(8,128)(2,1)} %get-tuple-element.41), channel_id=1, source_target_pairs={{0,3},{1,2},{2,1},{3,0},{4,7},{5,6},{6,5},{7,4},{8,11},{9,10},{10,... | collective-permute-start | bytes 1572872 | tf_op jit(solution)/shard_map/ppermute | solution.py:328
  36.8 25.0 %collective-permute-start.5 = (bf16[256,1024]{1,0:T(8,128)(2,1)}, bf16[256,1024]{1,0:T(8,128)(2,1)}, u32[]{:S(2)}, u32[]{:S(2)}) collective-permute-start(bf16[256,1024]{1,0:T(8,128)(2,1)} %collective-permute-done.4.refs_0_.refs_6_), channel_id=1, source_target_pairs={{0,8},{1,9},{2,10},{3,11},{4,12},{5,13},{6,14},{7,15},{8,0},{9,1},... | collective-permute-start | bytes 1572872 | tf_op jit(solution)/shard_map/ppermute | solution.py:328
  37.9 26.0 %collective-permute-start.9 = (bf16[256,1024]{1,0:T(8,128)(2,1)}, bf16[256,1024]{1,0:T(8,128)(2,1)S(1)}, u32[]{:S(2)}, u32[]{:S(2)}) collective-permute-start(bf16[256,1024]{1,0:T(8,128)(2,1)} %collective-permute-done.4.refs_0_.refs_6_), channel_id=1, source_target_pairs={{0,3},{1,2},{2,1},{3,0},{4,7},{5,6},{6,5},{7,4},{8,11},{9,10},{10,... | collective-permute-start | bytes 1572872 | tf_op jit(solution)/shard_map/ppermute | solution.py:328
  38.5 25.4 %collective-permute-start.7 = (bf16[256,1024]{1,0:T(8,128)(2,1)}, bf16[256,1024]{1,0:T(8,128)(2,1)S(1)}, u32[]{:S(2)}, u32[]{:S(2)}) collective-permute-start(bf16[256,1024]{1,0:T(8,128)(2,1)} %collective-permute-done.4.refs_0_.refs_6_), channel_id=1, source_target_pairs={{0,1},{1,0},{2,3},{3,2},{4,5},{5,4},{6,7},{7,6},{8,9},{9,8},{10,11... | collective-permute-start | bytes 1572872 | tf_op jit(solution)/shard_map/ppermute | solution.py:328
  40.0 24.0 %collective-permute-start.8 = (bf16[256,1024]{1,0:T(8,128)(2,1)}, bf16[256,1024]{1,0:T(8,128)(2,1)S(1)}, u32[]{:S(2)}, u32[]{:S(2)}) collective-permute-start(bf16[256,1024]{1,0:T(8,128)(2,1)} %collective-permute-done.4.refs_0_.refs_6_), channel_id=1, source_target_pairs={{0,2},{1,3},{2,0},{3,1},{4,6},{5,7},{6,4},{7,5},{8,10},{9,11},{10,... | collective-permute-start | bytes 1572872 | tf_op jit(solution)/shard_map/ppermute | solution.py:328
  41.5 1.0 copy-start.2
  52.3 11.9 %copy-start.4 = (bf16[256,2048]{1,0:T(8,128)(2,1)S(1)}, bf16[256,2048]{1,0:T(8,128)(2,1)}, u32[]{:S(2)}) copy-start(bf16[256,2048]{1,0:T(8,128)(2,1)} %get-tuple-element.52) | copy-start | bytes 3145732
  64.1 6.5 %collective-permute-start.10 = (bf16[256,7168]{1,0:T(8,128)(2,1)S(1)}, bf16[256,7168]{1,0:T(8,128)(2,1)S(1)}, u32[]{:S(2)}, u32[]{:S(2)}) collective-permute-start(bf16[256,7168]{1,0:T(8,128)(2,1)S(1)} %constant_dynamic-update-slice_fusion), channel_id=1, source_target_pairs={{0,4},{1,5},{2,6},{3,7},{4,0},{5,1},{6,2},{7,3},{8,12},{9,13},{10,... | collective-permute-start | bytes 11010056 | tf_op jit(solution)/shard_map/ppermute | solution.py:328
  64.2 26.0 %collective-permute-start.17 = (bf16[256,2048]{1,0:T(8,128)(2,1)S(1)}, bf16[256,2048]{1,0:T(8,128)(2,1)S(1)}, u32[]{:S(2)}, u32[]{:S(2)}) collective-permute-start(bf16[256,2048]{1,0:T(8,128)(2,1)S(1)} %copy-done.4), channel_id=1, source_target_pairs={{0,8},{1,9},{2,10},{3,11},{4,12},{5,13},{6,14},{7,15},{8,0},{9,1},... | collective-permute-start | bytes 3145736 | tf_op jit(solution)/shard_map/ppermute | solution.py:328
  64.4 15.0 %collective-permute-start.11 = (bf16[256,1024]{1,0:T(8,128)(2,1)}, bf16[256,1024]{1,0:T(8,128)(2,1)S(1)}, u32[]{:S(2)}, u32[]{:S(2)}) collective-permute-start(bf16[256,1024]{1,0:T(8,128)(2,1)} %collective-permute-done.5.refs_0_.refs_6_), channel_id=1, source_target_pairs={{0,1},{1,0},{2,3},{3,2},{4,5},{5,4},{6,7},{7,6},{8,9},{9,8},{10,11... | collective-permute-start | bytes 1572872 | tf_op jit(solution)/shard_map/ppermute | solution.py:328
  65.0 25.2 %collective-permute-start.13 = (bf16[256,1024]{1,0:T(8,128)(2,1)}, bf16[256,1024]{1,0:T(8,128)(2,1)S(1)}, u32[]{:S(2)}, u32[]{:S(2)}) collective-permute-start(bf16[256,1024]{1,0:T(8,128)(2,1)} %collective-permute-done.5.refs_0_.refs_6_), channel_id=1, source_target_pairs={{0,2},{1,3},{2,0},{3,1},{4,6},{5,7},{6,4},{7,5},{8,10},{9,11},{10,... | collective-permute-start | bytes 1572872 | tf_op jit(solution)/shard_map/ppermute | solution.py:328
  65.7 24.5 %collective-permute-start.15 = (bf16[256,1024]{1,0:T(8,128)(2,1)}, bf16[256,1024]{1,0:T(8,128)(2,1)S(1)}, u32[]{:S(2)}, u32[]{:S(2)}) collective-permute-start(bf16[256,1024]{1,0:T(8,128)(2,1)} %collective-permute-done.5.refs_0_.refs_6_), channel_id=1, source_target_pairs={{0,3},{1,2},{2,1},{3,0},{4,7},{5,6},{6,5},{7,4},{8,11},{9,10},{10,... | collective-permute-start | bytes 1572872 | tf_op jit(solution)/shard_map/ppermute | solution.py:328
  90.2 2.7 %collective-permute-start.18 = (bf16[256,2048]{1,0:T(8,128)(2,1)S(1)}, bf16[256,2048]{1,0:T(8,128)(2,1)S(1)}, u32[]{:S(2)}, u32[]{:S(2)}) collective-permute-start(bf16[256,2048]{1,0:T(8,128)(2,1)S(1)} %collective-permute-done.17.refs_2_.refs_8_), channel_id=1, source_target_pairs={{0,4},{1,5},{2,6},{3,7},{4,0},{5,1},{6,2},{7,3},{8,12},{9,13},{10,... | collective-permute-start | bytes 3145736 | tf_op jit(solution)/shard_map/ppermute | solution.py:328
  90.2 9.8 %collective-permute-start.12 = (bf16[256,1024]{1,0:T(8,128)(2,1)S(1)}, bf16[256,1024]{1,0:T(8,128)(2,1)S(1)}, u32[]{:S(2)}, u32[]{:S(2)}) collective-permute-start(bf16[256,1024]{1,0:T(8,128)(2,1)S(1)} %collective-permute-done.11.refs_2_.refs_8_), channel_id=1, source_target_pairs={{0,4},{1,5},{2,6},{3,7},{4,0},{5,1},{6,2},{7,3},{8,12},{9,13},{10,... | collective-permute-start | bytes 1572872 | tf_op jit(solution)/shard_map/ppermute | solution.py:328
  90.7 9.9 %collective-permute-start.14 = (bf16[256,1024]{1,0:T(8,128)(2,1)S(1)}, bf16[256,1024]{1,0:T(8,128)(2,1)S(1)}, u32[]{:S(2)}, u32[]{:S(2)}) collective-permute-start(bf16[256,1024]{1,0:T(8,128)(2,1)S(1)} %collective-permute-done.13.refs_4_.refs_10_), channel_id=1, source_target_pairs={{0,4},{1,5},{2,6},{3,7},{4,0},{5,1},{6,2},{7,3},{8,12},{9,13},{10,... | collective-permute-start | bytes 1572872 | tf_op jit(solution)/shard_map/ppermute | solution.py:328
  90.8 9.8 %collective-permute-start.16 = (bf16[256,1024]{1,0:T(8,128)(2,1)S(1)}, bf16[256,1024]{1,0:T(8,128)(2,1)S(1)}, u32[]{:S(2)}, u32[]{:S(2)}) collective-permute-start(bf16[256,1024]{1,0:T(8,128)(2,1)S(1)} %collective-permute-done.15.refs_6_.refs_12_), channel_id=1, source_target_pairs={{0,4},{1,5},{2,6},{3,7},{4,0},{5,1},{6,2},{7,3},{8,12},{9,13},{10,... | collective-permute-start | bytes 1572872 | tf_op jit(solution)/shard_map/ppermute | solution.py:328
  96.8 9.7 %collective-permute-start.24 = (bf16[128,768]{1,0:T(8,128)(2,1)S(1)}, bf16[128,768]{1,0:T(8,128)(2,1)S(1)}, u32[]{:S(2)}, u32[]{:S(2)}) collective-permute-start(bf16[128,768]{1,0:T(8,128)(2,1)S(1)} %pad_maximum_fusion.3), channel_id=1, source_target_pairs={{0,3},{1,2},{2,1},{3,0},{4,7},{5,6},{6,5},{7,4},{8,11},{9,10},{10,... | collective-permute-start | bytes 589832 | tf_op jit(solution)/shard_map/ppermute | solution.py:328
  98.4 14.2 %collective-permute-start.23 = (bf16[128,768]{1,0:T(8,128)(2,1)S(1)}, bf16[128,768]{1,0:T(8,128)(2,1)S(1)}, u32[]{:S(2)}, u32[]{:S(2)}) collective-permute-start(bf16[128,768]{1,0:T(8,128)(2,1)S(1)} %pad_maximum_fusion.2), channel_id=1, source_target_pairs={{0,2},{1,3},{2,0},{3,1},{4,6},{5,7},{6,4},{7,5},{8,10},{9,11},{10,... | collective-permute-start | bytes 589832 | tf_op jit(solution)/shard_map/ppermute | solution.py:328
  100.0 12.7 %collective-permute-start.22 = (bf16[128,768]{1,0:T(8,128)(2,1)S(1)}, bf16[128,768]{1,0:T(8,128)(2,1)S(1)}, u32[]{:S(2)}, u32[]{:S(2)}) collective-permute-start(bf16[128,768]{1,0:T(8,128)(2,1)S(1)} %pad_maximum_fusion.1), channel_id=1, source_target_pairs={{0,1},{1,0},{2,3},{3,2},{4,5},{5,4},{6,7},{7,6},{8,9},{9,8},{10,11... | collective-permute-start | bytes 589832 | tf_op jit(solution)/shard_map/ppermute | solution.py:328
  104.3 9.7 %collective-permute-start.19 = (bf16[128,256]{1,0:T(8,128)(2,1)S(1)}, bf16[128,256]{1,0:T(8,128)(2,1)S(1)}, u32[]{:S(2)}, u32[]{:S(2)}) collective-permute-start(bf16[128,256]{1,0:T(8,128)(2,1)S(1)} %get-tuple-element.60), channel_id=1, source_target_pairs={{0,1},{1,0},{2,3},{3,2},{4,5},{5,4},{6,7},{7,6},{8,9},{9,8},{10,11... | collective-permute-start | bytes 196616 | tf_op jit(solution)/shard_map/ppermute | solution.py:328
  105.9 8.2 %collective-permute-start.20 = (bf16[128,256]{1,0:T(8,128)(2,1)S(1)}, bf16[128,256]{1,0:T(8,128)(2,1)S(1)}, u32[]{:S(2)}, u32[]{:S(2)}) collective-permute-start(bf16[128,256]{1,0:T(8,128)(2,1)S(1)} %get-tuple-element.61), channel_id=1, source_target_pairs={{0,2},{1,3},{2,0},{3,1},{4,6},{5,7},{6,4},{7,5},{8,10},{9,11},{10,... | collective-permute-start | bytes 196616 | tf_op jit(solution)/shard_map/ppermute | solution.py:328
  106.5 7.6 %collective-permute-start.21 = (bf16[128,256]{1,0:T(8,128)(2,1)S(1)}, bf16[128,256]{1,0:T(8,128)(2,1)S(1)}, u32[]{:S(2)}, u32[]{:S(2)}) collective-permute-start(bf16[128,256]{1,0:T(8,128)(2,1)S(1)} %get-tuple-element.62), channel_id=1, source_target_pairs={{0,3},{1,2},{2,1},{3,0},{4,7},{5,6},{6,5},{7,4},{8,11},{9,10},{10,... | collective-permute-start | bytes 196616 | tf_op jit(solution)/shard_map/ppermute | solution.py:328
